TPU v7x, 32 devices: a whole 2x2x4 slice. The times are simulated.
32 devices in a mesh: row: 4 (over z), col: 8 (over y, x, core).
Axes of the slice: x: 2, y: 2, z: 4, core: 2. Of those that a mesh axis runs over, the one named last changes fastest.
Arguments:
- hidden_acts: bfloat16 [1024, 26624], P('col', 'row'), may hold values from -0.1875 to 0.1875
- out_grad: bfloat16 [1024, 16384], P('row', 'col'), may hold values from -6 to 6
- down_weight: bfloat16 [26624, 16384], P('row', 'col'), may hold values from -0.046875 to 0.046875
Outputs:
- weight_grad: bfloat16 [26624, 16384], P('row', 'col')
- hidden_grad: bfloat16 [1024, 26624], P('col', 'row')
All inputs are finite; a program needn't handle non-finite values.
Results may differ from a plain program's by a relative error of at most 0.02.
Values may be sent and summed in bfloat16 or wider, within the bound.
No kernel may reach another device: no remote copies, remote signals or barrier semaphores. Data moves between devices by JAX's collectives and lax.ppermute only.
A program may use at most 128 MiB of HBM per device.

v0:
```python
import jax
import jax.numpy as jnp
from jax import lax
from jax.sharding import PartitionSpec as P


def per_device(hidden_acts, out_grad, down_weight):
    grad_full = lax.all_gather(out_grad, "row", axis=0, tiled=True)
    acts_full = lax.all_gather(hidden_acts, "col", axis=0, tiled=True)
    weight_grad = lax.dot_general(
        acts_full, grad_full, (((0,), (0,)), ((), ())), preferred_element_type=jnp.float32
    )
    partial_grad = lax.dot_general(
        grad_full, down_weight, (((1,), (1,)), ((), ())), preferred_element_type=jnp.float32
    )
    hidden_grad = lax.psum_scatter(
        partial_grad.astype(jnp.bfloat16), "col", scatter_dimension=0, tiled=True
    )
    return (weight_grad.astype(jnp.bfloat16), hidden_grad)


def solution(mesh):
    in_specs = (P("col", "row"), P("row", "col"), P("row", "col"))
    out_specs = (P("row", "col"), P("col", "row"))
    return jax.shard_map(
        per_device, mesh=mesh, in_specs=in_specs, out_specs=out_specs, check_vma=False
    )
```

profile of v0, /device:TPU:0, one launch (start us, length us, event | category | flops | bytes accessed | tf_op | source)
XLA Modules:
  0.0 278.7 jit_solution(17420272761931426327)
XLA Ops:
  7.2 0.0 all-gather.5.cloned.1.call-start
  7.2 0.7 all-gather.5.cloned.1.call-update
  7.9 0.0 all-gather.3.cloned.1.call-start
  7.9 0.7 all-gather.3.cloned.1.call-update
  8.6 0.0 reduce-scatter.2.cloned.1.call-start
  8.7 84.4 %all-gather.5.cloned.1.call-done = bf16[1024,2048]{1,0:T(8,128)(2,1)} async-done(((bf16[256,2048]{1,0:T(8,128)(2,1)}), bf16[1024,2048]{1,0:T(8,128)(2,1)}) %all-gather.5.cloned.1.call-update) | async-done | bytes 4194320 | tf_op jit(solution)/shard_map/all_gather | solution.py:8
  93.1 37.5 %convolution_convert_fusion.1 = bf16[1024,6656]{1,0:T(8,128)(2,1)} fusion(bf16[1024,2048]{1,0:T(8,128)(2,1)} %all-gather.5.cloned.1.call-done, bf16[6656,2048]{1,0:T(8,128)(2,1)} %param.5), kind=kOutput, calls=%fused_computation.1 | convolution fusion | flops 27924103168 | bytes 45088768 | tf_op jit(solution)/shard_map/dot_general | solution.py:13
  130.6 0.0 reduce-scatter.2.cloned.1.call-update
  130.6 39.5 %all-gather.3.cloned.1.call-done = bf16[1024,6656]{1,0:T(8,128)(2,1)} async-done(((bf16[128,6656]{1,0:T(8,128)(2,1)}), bf16[1024,6656]{1,0:T(8,128)(2,1)}) %all-gather.3.cloned.1.call-update) | async-done | bytes 13631504 | tf_op jit(solution)/shard_map/all_gather | solution.py:9
  170.1 35.9 %convolution_convert_fusion = bf16[6656,2048]{1,0:T(8,128)(2,1)} fusion(bf16[1024,6656]{1,0:T(8,128)(2,1)} %all-gather.3.cloned.1.call-done, bf16[1024,2048]{1,0:T(8,128)(2,1)} %all-gather.5.cloned.1.call-done), kind=kOutput, calls=%fused_computation | convolution fusion | flops 27930918912 | bytes 45088768 | tf_op jit(solution)/shard_map/dot_general | solution.py:10
  205.9 66.2 %reduce-scatter.2.cloned.1.call-done = bf16[128,6656]{1,0:T(8,128)(2,1)} async-done(((bf16[1024,6656]{1,0:T(8,128)(2,1)}), bf16[128,6656]{1,0:T(8,128)(2,1)}) %reduce-scatter.2.cloned.1.call-update) | async-done | bytes 1703952 | tf_op jit(solution)/shard_map/reduce_scatter | solution.py:16
Async XLA Ops:
  7.2 85.9 %all-gather.5.cloned.1.call-start = ((), (), s32[]{:S(2)}) async-start(), calls=%async_computation.2 | async-start | bytes 5242880 | tf_op jit(solution)/shard_map/all_gather | solution.py:8
  7.9 162.2 %all-gather.3.cloned.1.call-start = ((), (), s32[]{:S(2)}) async-start(), calls=%async_computation.1 | async-start | bytes 15335424 | tf_op jit(solution)/shard_map/all_gather | solution.py:9
  8.6 263.5 %reduce-scatter.2.cloned.1.call-start = ((), (), s32[]{:S(2)}) async-start(), calls=%async_computation.3 | async-start | bytes 15335424 | tf_op jit(solution)/shard_map/reduce_scatter | solution.py:16
Sparse Core Ops, SparseCore 0:
  9.6 83.4 all-gather.4
  95.0 75.0 all-gather.2
  174.2 97.9 reduce-scatter.1
where the time goes:
time: 279 us
  waiting for transfers between devices  191 us (68%)
  matrix products  73.4 us (26%)
  between operations  13.7 us (5%)
    all_gather x1, waiting for transfers between devices, per_device(): grad_full = lax.all_gather(out_grad, 'row', axis=0, tiled=True)  84.4 us
    reduce_scatter x1, waiting for transfers between devices, per_device(): lax.psum_scatter(partial_grad.astype(jnp.bfloat16), 'col', scatter_dimens...  66.2 us
    all_gather x1, waiting for transfers between devices, per_device(): acts_full = lax.all_gather(hidden_acts, 'col', axis=0, tiled=True)  39.5 us
    dot_general x1, matrix products, per_device(): lax.dot_general(grad_full, down_weight, (((1,), (1,)), ((), ())), preferr...  37.5 us
    dot_general x1, matrix products, per_device(): lax.dot_general(acts_full, grad_full, (((0,), (0,)), ((), ())), preferred...  35.9 us
  transfers between devices with their start and end apart: 3, of which 3 were waited for; matrix products, arithmetic and copies ran while one was open for 26% of the time, Pallas kernels for 0%

commit v1 on v0

v1 whole, which is shorter than its diff:
```python
import functools

import jax
import jax.numpy as jnp
from jax import lax
from jax.experimental import pallas as pl
from jax.experimental.pallas import tpu as pltpu
from jax.sharding import PartitionSpec as P

F32, BF16 = jnp.float32, jnp.bfloat16
ANYWHERE = pl.BlockSpec(memory_space=pl.ANY)
PARAMS = pltpu.CompilerParams(vmem_limit_bytes=58 * 1024 * 1024)


def halving_order(bits):
    if not bits:
        return [0]
    keep = halving_order(bits[1:])
    return [o ^ bits[0] for o in keep] + keep


def flip(x, bit, n):
    return lax.ppermute(x, "col", [(i, i ^ bit) for i in range(n)])


def partial_kernel(order, c, me_ref, g_ref, w_ref, *refs):
    send_ref, keep_ref, rel = refs[-3:]
    half = len(order) // 2

    @pl.when(pl.program_id(0) == 0)
    def _():
        for p, j in enumerate(order):
            start = pl.multiple_of((me_ref[0] ^ j) * c, c)
            rel[pl.ds(p * c, c), :] = g_ref[pl.ds(start, c), :]

    res = lax.dot_general(
        rel[...], w_ref[...], (((1,), (1,)), ((), ())), preferred_element_type=F32
    ).astype(BF16)
    res = res.reshape(2 * half, c, res.shape[-1])
    send_ref[...] = res[:half]
    keep_ref[...] = res[half:]


def partial_sums(me, grads, weight, order, c, tile, first, count, after):
    n, depth = len(order), grads.shape[1]
    out = jax.ShapeDtypeStruct((n // 2, c, count * tile), BF16)
    out_spec = pl.BlockSpec((n // 2, c, tile), lambda i, s: (0, 0, i))
    return pl.pallas_call(
        functools.partial(partial_kernel, order, c),
        out_shape=(out, out),
        grid_spec=pltpu.PrefetchScalarGridSpec(
            num_scalar_prefetch=1,
            grid=(count,),
            in_specs=[
                pl.BlockSpec((n * c, depth), lambda i, s: (0, 0)),
                pl.BlockSpec((tile, depth), lambda i, s: (first + i, 0)),
            ]
            + [ANYWHERE] * len(after),
            out_specs=(out_spec, out_spec),
            scratch_shapes=[pltpu.VMEM((n * c, depth), BF16)],
        ),
        compiler_params=PARAMS,
        cost_estimate=pl.CostEstimate(
            flops=2 * n * c * depth * count * tile,
            bytes_accessed=2 * (n * c * depth + count * tile * depth + n * c * count * tile),
            transcendentals=0,
        ),
        name="partial_sums",
    )(me, grads, weight, *after)


def weight_kernel(places, chunks, n, me_ref, *refs):
    acts_refs, refs = refs[: len(places)], refs[len(places):]
    grads_refs, out_ref, acts = refs[: len(chunks)], refs[-2], refs[-1]
    for (j, begin), ref in zip(places, acts_refs):
        for at, c in chunks:
            if begin <= at and at + c <= begin + ref.shape[0]:
                start = pl.multiple_of(at * n + (me_ref[0] ^ j) * c, c)
                acts[pl.ds(start, c), :] = ref[pl.ds(at - begin, c), :]
    total = None
    for (at, c), ref in zip(chunks, grads_refs):
        term = lax.dot_general(
            acts[pl.ds(at * n, c * n), :], ref[...],
            (((0,), (0,)), ((), ())), preferred_element_type=F32,
        )
        total = term if total is None else total + term
    out_ref[...] = total.astype(BF16)


def weight_rows(me, pieces, grads, chunks, n, before, shape, tile, first, count, after):
    places = [place for place, _ in pieces]
    rows, width = sum(g.shape[0] for g in grads), shape[1]
    in_specs = [pl.BlockSpec((a.shape[0], tile), lambda i, s: (0, first + i)) for _, a in pieces]
    in_specs += [
        pl.BlockSpec(g.shape, lambda i, s: (0, 0), pipeline_mode=pl.Buffered(1)) for g in grads
    ]
    args = [a for _, a in pieces] + list(grads) + list(after)
    in_specs += [ANYWHERE] * len(after)
    aliases = {}
    if before is not None:
        in_specs.append(ANYWHERE)
        args.append(before)
        aliases = {len(args): 0}
    return pl.pallas_call(
        functools.partial(weight_kernel, places, chunks, n),
        out_shape=jax.ShapeDtypeStruct(shape, BF16),
        grid_spec=pltpu.PrefetchScalarGridSpec(
            num_scalar_prefetch=1,
            grid=(count,),
            in_specs=in_specs,
            out_specs=pl.BlockSpec((tile, width), lambda i, s: (first + i, 0)),
            scratch_shapes=[pltpu.VMEM((rows, tile), BF16)],
        ),
        input_output_aliases=aliases,
        compiler_params=PARAMS,
        cost_estimate=pl.CostEstimate(
            flops=2 * rows * width * count * tile,
            bytes_accessed=2 * (rows * width + (rows + width) * count * tile),
            transcendentals=0,
        ),
        name="weight_rows",
    )(me, *args)


def sums_kernel(sizes, n_final, *refs):
    outs = refs[-len(sizes) + n_final - 1:] if n_final else refs[-len(sizes):]
    at, column = 0, 0
    for job, size in enumerate(sizes):
        total = refs[at][...].astype(F32)
        for ref in refs[at + 1 : at + size]:
            total = total + ref[...].astype(F32)
        at += size
        if job < len(sizes) - n_final:
            outs[job][...] = total.astype(BF16)
        else:
            width = total.shape[-1]
            outs[-1][:, pl.ds(column, width)] = total[0].astype(BF16)
            column += width


def sums(jobs, after, final=None, shape=None, before=None):
    final, at = final or ([], 0)
    everything = jobs + final
    heights = [job[0][0][0].shape[1] for job in everything]
    steps = min(4, min(heights) // 16)
    in_specs, args, out_specs, out_shape = [], [], [], []
    for job, (terms, size) in enumerate(everything):
        _, c, f = terms[0][0].shape
        for array, first in terms:
            in_specs.append(
                pl.BlockSpec((size, c // steps, f), lambda i, b=first // size: (b, i, 0))
            )
            args.append(array)
        if job < len(jobs):
            out_specs.append(pl.BlockSpec((size, c // steps, f), lambda i: (0, i, 0)))
            out_shape.append(jax.ShapeDtypeStruct((size, c, f), BF16))
    args += after
    in_specs += [ANYWHERE] * len(after)
    aliases = {}
    if final:
        height = heights[-1] // steps
        out_specs.append(pl.BlockSpec((height, shape[1]), lambda i: (at // height + i, 0)))
        out_shape.append(jax.ShapeDtypeStruct(shape, BF16))
        if before is not None:
            aliases = {len(args): len(jobs)}
            args.append(before)
            in_specs.append(ANYWHERE)
    bytes_accessed = sum(
        2 * (len(terms) + 1) * size * terms[0][0].shape[1] * terms[0][0].shape[2]
        for terms, size in everything
    )
    return pl.pallas_call(
        functools.partial(sums_kernel, [len(terms) for terms, _ in everything], len(final)),
        out_shape=out_shape,
        grid=(steps,),
        in_specs=in_specs,
        out_specs=out_specs,
        input_output_aliases=aliases,
        compiler_params=PARAMS,
        cost_estimate=pl.CostEstimate(
            flops=bytes_accessed, bytes_accessed=bytes_accessed, transcendentals=0
        ),
        name="sums",
    )(*args)


class Halving:
    def __init__(self, send, keep, bits, n):
        self.bits, self.n = list(bits), n
        self.kept, self.offset = keep.shape[0], 0
        self.terms = [[keep, 0]]
        self.take(send)

    def take(self, out):
        self.terms = self.terms + [[flip(out, self.bits.pop(0), self.n), 0]]

    def job(self):
        size = self.kept // 2 if self.bits else 1
        self.kept = size
        job = ([(array, first) for array, first in self.terms], size)
        self.terms = [[array, first + size] for array, first in self.terms]
        return job


def per_device(n_row, n_col, hidden_acts, out_grad, down_weight):
    tokens, units = hidden_acts.shape
    features = out_grad.shape[1]
    owners = n_col // n_row
    bits = [1 << b for b in range(n_col.bit_length() - 1)]
    sizes = [tokens // 2] + ([tokens // 4] * 2 if tokens >= 64 else [tokens // 2])
    chunks = [(sum(sizes[:k]), c) for k, c in enumerate(sizes)]
    tile = 128 * max(d for d in (1, 2, 4) if units % (128 * d) == 0)
    tiles = units // tile
    me = lax.axis_index("col").astype(jnp.int32).reshape(1)

    by_owner = out_grad.reshape(owners, tokens, features)
    grads = [
        lax.all_gather(by_owner[:, at : at + c], "row").reshape(n_col * c, features)
        for at, c in chunks
    ]

    half = tokens // 2
    whole = {0: hidden_acts}
    for bit in bits[1:]:
        whole[bit] = flip(hidden_acts, bit, n_col)
    first_hop = [whole[bit] for bit in bits[1:]]
    for j in list(whole):
        whole[j ^ 1] = flip(whole[j], 1, n_col)
    pieces = [((j, 0), a) for j, a in whole.items()]
    for h, far in enumerate((bits[1:], bits[:0:-1])):
        held = {}
        for bit in far:
            for j in list(held):
                held[j ^ bit] = flip(held[j], bit, n_col)
            held[bit] = whole[bit][h * half : (h + 1) * half]
        for j, a in held.items():
            if j not in whole:
                pieces += [((j, h * half), a), ((j ^ 1, h * half), flip(a, 1, n_col))]

    split = (tiles + 1) // 2
    ranges = [(0, split, bits), (split, tiles - split, bits[:1] + bits[:0:-1])]

    def start(k, after):
        at, c = chunks[k]
        parts = []
        for first, count, order in ranges:
            send, keep = partial_sums(
                me, grads[k], down_weight, halving_order(order), c, tile, first, count, after
            )
            parts.append(Halving(send, keep, order, n_col))
            after = [send]
        return parts, after

    cuts = [round(tiles * f / 13) for f in (0, 4, 6, 10, 13)]
    weight_grad, hidden_grad = None, None

    def work(w, after):
        nonlocal weight_grad
        weight_grad = weight_rows(
            me, pieces, grads, chunks, n_col, weight_grad, (units, features), tile,
            cuts[w], cuts[w + 1] - cuts[w], after,
        )
        return [weight_grad]

    def advance(parts, after):
        nonlocal hidden_grad
        going = [p for chunk in parts for p in chunk[1] if p.bits]
        ended = [chunk for chunk in parts if not chunk[1][0].bits]
        assert len(ended) < 2
        final = ([p.job() for p in ended[0][1]], chunks[ended[0][0]][0]) if ended else None
        outs = sums([p.job() for p in going], after, final, (tokens, units), hidden_grad)
        for p, out in zip(going, outs):
            p.take(out)
        if ended:
            hidden_grad = outs[-1]
        return [outs[0]]

    after, parts, w = first_hop, [], 0
    for k in range(len(chunks)):
        if k == len(chunks) - 1:
            after, w = work(0, after), 1
        new, after = start(k, after)
        parts.append((k, new))
        if k == len(chunks) - 1:
            after, w = work(1, after), 2
        after = advance(parts, after)
        parts = [p for p in parts if p[1][0].terms[0][1] < n_col // 2]
    while parts:
        if w < len(cuts) - 1:
            after, w = work(w, after), w + 1
        after = advance(parts, after)
        parts = [p for p in parts if p[1][0].terms[0][1] < n_col // 2]
    return weight_grad, hidden_grad


def solution(mesh):
    in_specs = (P("col", "row"), P("row", "col"), P("row", "col"))
    out_specs = (P("row", "col"), P("col", "row"))
    return jax.shard_map(
        functools.partial(per_device, mesh.shape["row"], mesh.shape["col"]),
        mesh=mesh, in_specs=in_specs, out_specs=out_specs, check_vma=False,
    )
```

time: 279 us -> 272 us (0.975)
  Pallas kernels: 0 us -> 131 us
  waiting for transfers between devices: 191 us -> 92.9 us
  matrix products: 73.4 us -> 0 us
  starting transfers between devices: 0.11 us -> 24 us
  local copies, waits for them, and re-layouts: 0 us -> 8.85 us
    pallas_call x0 -> x15, Pallas kernels: none -> 131 us  [the longest x6 65.6 us: partial_sums(): pl.pallas_call(functools.partial(partial_kernel, order, c), out_shape=(ou...]
    all_gather x2 -> x3, waiting for transfers between devices: 124 us -> 27.1 us  [per_device(): lax.all_gather(by_owner[:, at:at + c], 'row').reshape(n_col * c, features)]
    dot_general x2 -> x0, matrix products: 73.4 us -> none  [the longest x1 37.5 us: per_device(): lax.dot_general(grad_full, down_weight, (((1,), (1,)), ((), ())), preferr...]
    reduce_scatter x1 -> x0, waiting for transfers between devices: 66.2 us -> none  [per_device(): lax.psum_scatter(partial_grad.astype(jnp.bfloat16), 'col', scatter_dimens...]
    ppermute x0 -> x27, waiting for transfers between devices: none -> 65.8 us  [flip(): return lax.ppermute(x, 'col', [(i, i ^ bit) for i in range(n)])]
    ppermute x0 -> x27, starting transfers between devices: none -> 23.9 us  [flip(): return lax.ppermute(x, 'col', [(i, i ^ bit) for i in range(n)])]
    slice x0 -> x4, local copies, waits for them, and re-layouts: none -> 4.71 us  [the longest x2 2.75 us: per_device(): by_owner[:, at:at + c]]
    unnamed x0 -> x40, local copies, waits for them, and re-layouts: none -> 4.14 us
  transfers between devices with their start and end apart: 3 -> 30, of which waited for: 3 -> 8; matrix products, arithmetic and copies ran while one was open for 26% -> 1% of each run, Pallas kernels for 0% -> 40%
where the time goes in v1:
time: 272 us; the launch traced here: 271 us
  Pallas kernels  131 us (48%)
  waiting for transfers between devices  92.9 us (34%)
  starting transfers between devices  24 us (9%)
  between operations  14 us (5%)
  local copies, waits for them, and re-layouts  8.85 us (3%)
    ppermute x27, waiting for transfers between devices, flip(): return lax.ppermute(x, 'col', [(i, i ^ bit) for i in range(n)])  65.8 us
    pallas_call x6, Pallas kernels, partial_sums(): pl.pallas_call(functools.partial(partial_kernel, order, c), out_shape=(ou...  65.6 us
    pallas_call x4, Pallas kernels, weight_rows(): pl.pallas_call(functools.partial(weight_kernel, places, chunks, n), out_s...  48.8 us
    all_gather x3, waiting for transfers between devices, per_device(): lax.all_gather(by_owner[:, at:at + c], 'row').reshape(n_col * c, features)  27.1 us
    ppermute x27, starting transfers between devices, flip(): return lax.ppermute(x, 'col', [(i, i ^ bit) for i in range(n)])  23.9 us
    pallas_call x5, Pallas kernels, sums(): pl.pallas_call(functools.partial(sums_kernel, [len(terms) for terms, _ in...  17.1 us
  transfers between devices with their start and end apart: 30, of which 8 were waited for; matrix products, arithmetic and copies ran while one was open for 1% of the time, Pallas kernels for 40%

profile of v1, /device:TPU:0, one launch (start us, length us, event | category | flops | bytes accessed | tf_op | source)
XLA Modules:
  0.0 271.2 jit_solution(3381317369651381275)
XLA Ops:
  7.2 1.9 slice.22
  9.2 3.0 %collective-permute-start.1 = (bf16[128,6656]{1,0:T(8,128)(2,1)}, bf16[128,6656]{1,0:T(8,128)(2,1)S(1)}, u32[]{:S(2)}, u32[]{:S(2)}) collective-permute-start(bf16[128,6656]{1,0:T(8,128)(2,1)} %refs_0_.7), channel_id=1, source_target_pairs={{0,4},{1,5},{2,6},{3,7},{4,0},{5,1},{6,2},{7,3},{8,12},{9,13},{10,... | collective-permute-start | bytes 5111816 | tf_op jit(solution)/shard_map/ppermute | solution.py:23
  12.2 1.5 collective-permute-start
  13.7 35.9 %collective-permute-done.1.refs_1_.refs_2_ = bf16[128,6656]{1,0:T(8,128)(2,1)S(1)} collective-permute-done((bf16[128,6656]{1,0:T(8,128)(2,1)}, bf16[128,6656]{1,0:T(8,128)(2,1)S(1)}, u32[]{:S(2)}, u32[]{:S(2)}) %collective-permute-start.1) | collective-permute-done | bytes 1703968 | tf_op jit(solution)/shard_map/ppermute | solution.py:23
  49.6 1.5 collective-permute-done.refs_0_.refs_1_
  51.1 7.7 %all-gather.7.cloned.1.call-done = bf16[8,64,2048]{2,1,0:T(8,128)(2,1)} async-done(((bf16[2,64,2048]{2,1,0:T(8,128)(2,1)}), bf16[8,64,2048]{2,1,0:T(8,128)(2,1)}) %all-gather.7.cloned.1.call-update) | async-done | bytes 2097168 | tf_op jit(solution)/shard_map/all_gather | solution.py:218
  58.8 13.5 %partial_sums.6 = (bf16[4,64,3584]{2,1,0:T(8,128)(2,1)}, bf16[4,64,3584]{2,1,0:T(8,128)(2,1)}) custom-call(s32[1]{0:T(128)} %bitcast.me_ref, bf16[512,2048]{1,0:T(8,128)(2,1)} %bitcast.5, bf16[6656,2048]{1,0:T(8,128)(2,1)} %w_ref.11, bf16[128,6656]{1,0:T(8,128)(2,1)} %copy-done.2, bf16[128,6656]{1,0:T(8,128)(2,1)} %copy-done), custom_call_target="tpu_custom_call" | custom-call | flops 7516192768 | bytes 20447232 | tf_op jit(solution)/shard_map/partial_sums/pallas_call | solution.py:48
  72.3 12.1 %partial_sums.7 = (bf16[4,64,3072]{2,1,0:T(8,128)(2,1)}, bf16[4,64,3072]{2,1,0:T(8,128)(2,1)}) custom-call(s32[1]{0:T(128)} %bitcast.me_ref, bf16[512,2048]{1,0:T(8,128)(2,1)} %bitcast.6, bf16[6656,2048]{1,0:T(8,128)(2,1)} %w_ref.11, bf16[4,64,3584]{2,1,0:T(8,128)(2,1)} %get-tuple-element.29.refs_0_), custom_call_target="tpu_custom_call" | custom-call | flops 6442450944 | bytes 17825792 | tf_op jit(solution)/shard_map/partial_sums/pallas_call | solution.py:48
  84.4 0.4 collective-permute-start.10
  84.8 0.9 fusion
  85.8 1.0 slice.21
  86.8 1.5 collective-permute-start.7
  88.2 1.0 slice.20
  89.2 1.5 collective-permute-start.5
  90.7 4.4 %sums.5 = (bf16[2,64,3584]{2,1,0:T(8,128)(2,1)}, bf16[2,64,3072]{2,1,0:T(8,128)(2,1)}) custom-call(bf16[4,64,3584]{2,1,0:T(8,128)(2,1)} %get-tuple-element.28.refs_0_.refs_10_, bf16[4,64,3584]{2,1,0:T(8,128)(2,1)} %collective-permute-done.9.refs_1_.refs_11_, bf16[4,64,3072]{2,1,0:T(8,128)(2,1)} %get-tuple-element.30.refs_2_.refs_3_.refs_14_, ...), custom_call_target="tpu_custom_call" | custom-call | flops 5111808 | bytes 5111808 | tf_op jit(solution)/shard_map/sums/pallas_call | solution.py:172
  95.1 0.5 collective-permute-start.12
  95.6 16.9 %all-gather.9.cloned.1.call-done = bf16[8,32,2048]{2,1,0:T(8,128)(2,1)} async-done(((bf16[2,32,2048]{2,1,0:T(8,128)(2,1)}), bf16[8,32,2048]{2,1,0:T(8,128)(2,1)}) %all-gather.9.cloned.1.call-update) | async-done | bytes 1048592 | tf_op jit(solution)/shard_map/all_gather | solution.py:218
  112.5 10.7 %partial_sums.8 = (bf16[4,32,3584]{2,1,0:T(8,128)(2,1)}, bf16[4,32,3584]{2,1,0:T(8,128)(2,1)}) custom-call(s32[1]{0:T(128)} %bitcast.me_ref, bf16[256,2048]{1,0:T(8,128)(2,1)} %bitcast.11, bf16[6656,2048]{1,0:T(8,128)(2,1)} %w_ref.11, bf16[2,64,3584]{2,1,0:T(8,128)(2,1)} %get-tuple-element.32.refs_0_), custom_call_target="tpu_custom_call" | custom-call | flops 3758096384 | bytes 17563648 | tf_op jit(solution)/shard_map/partial_sums/pallas_call | solution.py:48
  123.2 9.2 %partial_sums.9 = (bf16[4,32,3072]{2,1,0:T(8,128)(2,1)}, bf16[4,32,3072]{2,1,0:T(8,128)(2,1)}) custom-call(s32[1]{0:T(128)} %bitcast.me_ref, bf16[256,2048]{1,0:T(8,128)(2,1)} %bitcast.12, bf16[6656,2048]{1,0:T(8,128)(2,1)} %w_ref.11, bf16[4,32,3584]{2,1,0:T(8,128)(2,1)} %get-tuple-element.35.refs_0_), custom_call_target="tpu_custom_call" | custom-call | flops 3221225472 | bytes 15204352 | tf_op jit(solution)/shard_map/partial_sums/pallas_call | solution.py:48
  132.5 1.5 collective-permute-start.11
  135.1 0.7 copy-done.5
  135.9 19.7 %collective-permute-done.11.refs_2_.refs_12_ = bf16[2,64,3584]{2,1,0:T(8,128)(2,1)} collective-permute-done((bf16[2,64,3584]{2,1,0:T(8,128)(2,1)}, bf16[2,64,3584]{2,1,0:T(8,128)(2,1)}, u32[]{:S(2)}, u32[]{:S(2)}) %collective-permute-start.11) | collective-permute-done | bytes 917536 | tf_op jit(solution)/shard_map/ppermute | solution.py:23
  155.6 0.5 collective-permute-start.6
  156.1 3.4 %sums.6 = (bf16[1,64,3584]{2,1,0:T(8,128)(2,1)}, bf16[1,64,3072]{2,1,0:T(8,128)(2,1)}, bf16[2,32,3584]{2,1,0:T(8,128)(2,1)}, bf16[2,32,3072]{2,1,0:T(8,128)(2,1)}) custom-call(bf16[4,64,3584]{2,1,0:T(8,128)(2,1)} %get-tuple-element.28.refs_0_.refs_10_, bf16[4,64,3584]{2,1,0:T(8,128)(2,1)} %collective-permute-done.9.refs_1_.refs_11_, ...), custom_call_target="tpu_custom_call" | custom-call | flops 5963776 | bytes 5963776 | tf_op jit(solution)/shard_map/sums/pallas_call | solution.py:172
  159.5 1.5 collective-permute-start.17
  161.1 2.4 all-gather.11.cloned.1.call-done
  163.5 14.1 %weight_rows.4.refs_0_.refs_14_ = bf16[6656,2048]{1,0:T(8,128)(2,1)} custom-call(s32[1]{0:T(128)} %bitcast.me_ref, bf16[128,6656]{1,0:T(8,128)(2,1)} %refs_0_.7, bf16[128,6656]{1,0:T(8,128)(2,1)} %copy-done.2, bf16[128,6656]{1,0:T(8,128)(2,1)} %copy-done, bf16[128,6656]{1,0:T(8,128)(2,1)} %collective-permute-done.2.refs_3_, ...), custom_call_target="tpu_custom_call" | custom-call | flops 8589934592 | bytes 16777216 | tf_op jit(solution)/shard_map/weight_rows/pallas_call | solution.py:104
  177.6 10.7 %partial_sums.10 = (bf16[4,32,3584]{2,1,0:T(8,128)(2,1)}, bf16[4,32,3584]{2,1,0:T(8,128)(2,1)}) custom-call(s32[1]{0:T(128)} %bitcast.me_ref, bf16[256,2048]{1,0:T(8,128)(2,1)} %bitcast.18, bf16[6656,2048]{1,0:T(8,128)(2,1)} %w_ref.11, bf16[6656,2048]{1,0:T(8,128)(2,1)} %weight_rows.4.refs_0_.refs_14_), custom_call_target="tpu_custom_call" | custom-call | flops 3758096384 | bytes 17563648 | tf_op jit(solution)/shard_map/partial_sums/pallas_call | solution.py:48
  188.3 9.4 %partial_sums.11 = (bf16[4,32,3072]{2,1,0:T(8,128)(2,1)}, bf16[4,32,3072]{2,1,0:T(8,128)(2,1)}) custom-call(s32[1]{0:T(128)} %bitcast.me_ref, bf16[256,2048]{1,0:T(8,128)(2,1)} %bitcast.19, bf16[6656,2048]{1,0:T(8,128)(2,1)} %w_ref.11, bf16[4,32,3584]{2,1,0:T(8,128)(2,1)} %get-tuple-element.40.refs_0_), custom_call_target="tpu_custom_call" | custom-call | flops 3221225472 | bytes 15204352 | tf_op jit(solution)/shard_map/partial_sums/pallas_call | solution.py:48
  198.1 1.5 collective-permute-start.16
  199.6 1.5 collective-permute-start.19
  201.1 0.6 collective-permute-start.20
  201.6 9.1 %weight_rows.5.refs_18_.refs_14_ = bf16[6656,2048]{1,0:T(8,128)(2,1)} custom-call(s32[1]{0:T(128)} %bitcast.me_ref, bf16[128,6656]{1,0:T(8,128)(2,1)} %refs_0_.7, bf16[128,6656]{1,0:T(8,128)(2,1)} %copy-done.2, bf16[128,6656]{1,0:T(8,128)(2,1)} %copy-done, bf16[128,6656]{1,0:T(8,128)(2,1)} %collective-permute-done.2.refs_3_, ...), custom_call_target="tpu_custom_call", output_to_operand_aliasing={{}: (15, {})} | custom-call | flops 4294967296 | bytes 10485760 | tf_op jit(solution)/shard_map/weight_rows/pallas_call | solution.py:104
  210.7 8.4 %collective-permute-done.20.refs_17_ = bf16[1,64,3072]{2,1,0:T(8,128)(2,1)S(1)} collective-permute-done((bf16[1,64,3072]{2,1,0:T(8,128)(2,1)S(1)}, bf16[1,64,3072]{2,1,0:T(8,128)(2,1)S(1)}, u32[]{:S(2)}, u32[]{:S(2)}) %collective-permute-start.20) | collective-permute-done | bytes 393248 | tf_op jit(solution)/shard_map/ppermute | solution.py:23
  219.2 0.7 copy-done.13
  220.7 4.2 %sums.7 = (bf16[1,32,3584]{2,1,0:T(8,128)(2,1)}, bf16[1,32,3072]{2,1,0:T(8,128)(2,1)}, bf16[2,32,3584]{2,1,0:T(8,128)(2,1)}, bf16[2,32,3072]{2,1,0:T(8,128)(2,1)}, bf16[128,6656]{1,0:T(8,128)(2,1)}) custom-call(bf16[4,32,3584]{2,1,0:T(8,128)(2,1)} %get-tuple-element.34.refs_6_.refs_0_, bf16[4,32,3584]{2,1,0:T(8,128)(2,1)} %collective-permute-done.13.refs_7_.refs_1_, ...), custom_call_target="tpu_custom_call" | custom-call | flops 8519680 | bytes 8519680 | tf_op jit(solution)/shard_map/sums/pallas_call | solution.py:172
  224.9 1.5 collective-permute-start.24
  226.5 1.5 collective-permute-start.23
  228.0 0.5 collective-permute-start.22
  228.5 0.6 collective-permute-start.21
  229.1 14.1 %weight_rows.6.refs_14_ = bf16[6656,2048]{1,0:T(8,128)(2,1)} custom-call(s32[1]{0:T(128)} %bitcast.me_ref, bf16[128,6656]{1,0:T(8,128)(2,1)} %refs_0_.7, bf16[128,6656]{1,0:T(8,128)(2,1)} %copy-done.2, bf16[128,6656]{1,0:T(8,128)(2,1)} %copy-done, bf16[128,6656]{1,0:T(8,128)(2,1)} %collective-permute-done.2.refs_3_, ...), custom_call_target="tpu_custom_call", output_to_operand_aliasing={{}: (15, {})} | custom-call | flops 8589934592 | bytes 16777216 | tf_op jit(solution)/shard_map/weight_rows/pallas_call | solution.py:104
  243.2 0.6 copy-done.16
  244.3 2.8 %sums.8 = (bf16[1,32,3584]{2,1,0:T(8,128)(2,1)}, bf16[1,32,3072]{2,1,0:T(8,128)(2,1)}, bf16[128,6656]{1,0:T(8,128)(2,1)}) custom-call(bf16[4,32,3584]{2,1,0:T(8,128)(2,1)} %get-tuple-element.39.refs_6_.refs_0_, bf16[4,32,3584]{2,1,0:T(8,128)(2,1)} %copy-done.4, bf16[2,32,3584]{2,1,0:T(8,128)(2,1)} %copy-done.8, ...), custom_call_target="tpu_custom_call", output_to_operand_aliasing={{2}: (15, {})} | custom-call | flops 3833856 | bytes 3833856 | tf_op jit(solution)/shard_map/sums/pallas_call | solution.py:172
  247.0 1.5 collective-permute-start.26
  248.6 1.5 collective-permute-start.25
  250.0 11.6 %weight_rows.7.refs_8_ = bf16[6656,2048]{1,0:T(8,128)(2,1)} custom-call(s32[1]{0:T(128)} %bitcast.me_ref, bf16[128,6656]{1,0:T(8,128)(2,1)} %refs_0_.7, bf16[128,6656]{1,0:T(8,128)(2,1)} %copy-done.2, bf16[128,6656]{1,0:T(8,128)(2,1)} %copy-done, bf16[128,6656]{1,0:T(8,128)(2,1)} %collective-permute-done.2.refs_3_, ...), custom_call_target="tpu_custom_call", output_to_operand_aliasing={{}: (15, {})} | custom-call | flops 6442450944 | bytes 13631488 | tf_op jit(solution)/shard_map/weight_rows/pallas_call | solution.py:104
  261.7 0.6 copy-done.17
  262.4 2.3 sums.9
  (74 shorter events, 3.3 us)
Async XLA Ops:
  7.2 51.6 %all-gather.7.cloned.1.call-start = ((), (), s32[]{:S(2)}) async-start(), calls=%async_computation | async-start | bytes 2621440 | tf_op jit(solution)/shard_map/all_gather | solution.py:218
  9.1 103.4 %all-gather.9.cloned.1.call-start = ((), (), s32[]{:S(2)}) async-start(), calls=%async_computation.1 | async-start | bytes 1310720 | tf_op jit(solution)/shard_map/all_gather | solution.py:218
  9.2 40.4 %collective-permute-start.1 = (bf16[128,6656]{1,0:T(8,128)(2,1)}, bf16[128,6656]{1,0:T(8,128)(2,1)S(1)}, u32[]{:S(2)}, u32[]{:S(2)}) collective-permute-start(bf16[128,6656]{1,0:T(8,128)(2,1)} %refs_0_.7), channel_id=1, source_target_pairs={{0,4},{1,5},{2,6},{3,7},{4,0},{5,1},{6,2},{7,3},{8,12},{9,13},{10,... | collective-permute-start | bytes 5111816 | tf_op jit(solution)/shard_map/ppermute | solution.py:23
  12.2 38.9 %collective-permute-start = (bf16[128,6656]{1,0:T(8,128)(2,1)}, bf16[128,6656]{1,0:T(8,128)(2,1)S(1)}, u32[]{:S(2)}, u32[]{:S(2)}) collective-permute-start(bf16[128,6656]{1,0:T(8,128)(2,1)} %refs_0_.7), channel_id=1, source_target_pairs={{0,2},{1,3},{2,0},{3,1},{4,6},{5,7},{6,4},{7,5},{8,10},{9,11},{10,... | collective-permute-start | bytes 5111816 | tf_op jit(solution)/shard_map/ppermute | solution.py:23
  49.6 9.2 %copy-start = (bf16[128,6656]{1,0:T(8,128)(2,1)}, bf16[128,6656]{1,0:T(8,128)(2,1)S(1)}, u32[]{:S(2)}) copy-start(bf16[128,6656]{1,0:T(8,128)(2,1)S(1)} %collective-permute-done.1.refs_1_.refs_2_) | copy-start | bytes 5111812
  51.1 7.7 %copy-start.2 = (bf16[128,6656]{1,0:T(8,128)(2,1)}, bf16[128,6656]{1,0:T(8,128)(2,1)S(1)}, u32[]{:S(2)}) copy-start(bf16[128,6656]{1,0:T(8,128)(2,1)S(1)} %collective-permute-done.refs_0_.refs_1_) | copy-start | bytes 5111812
  72.3 12.5 %copy-start.10 = (bf16[256,2048]{1,0:T(8,128)(2,1)S(1)}, bf16[256,2048]{1,0:T(8,128)(2,1)}, u32[]{:S(2)}) copy-start(bf16[256,2048]{1,0:T(8,128)(2,1)} %param.4) | copy-start | bytes 3145732
  72.3 18.4 %collective-permute-start.9 = (bf16[4,64,3584]{2,1,0:T(8,128)(2,1)}, bf16[4,64,3584]{2,1,0:T(8,128)(2,1)}, u32[]{:S(2)}, u32[]{:S(2)}) collective-permute-start(bf16[4,64,3584]{2,1,0:T(8,128)(2,1)} %get-tuple-element.29.refs_0_), channel_id=1, source_target_pairs={{0,1},{1,0},{2,3},{3,2},{4,5},{5,4},{6,7},{7,6},{8,9},{9,8},{10,11... | collective-permute-start | bytes 5505032 | tf_op jit(solution)/shard_map/ppermute | solution.py:23
  72.3 13.5 %copy-start.1 = (bf16[128,6656]{1,0:T(8,128)(2,1)S(1)}, bf16[128,6656]{1,0:T(8,128)(2,1)}, u32[]{:S(2)}) copy-start(bf16[128,6656]{1,0:T(8,128)(2,1)} %copy-done) | copy-start | bytes 5111812
  84.4 3.9 %copy-start.3 = (bf16[128,6656]{1,0:T(8,128)(2,1)S(1)}, bf16[128,6656]{1,0:T(8,128)(2,1)}, u32[]{:S(2)}) copy-start(bf16[128,6656]{1,0:T(8,128)(2,1)} %copy-done.2) | copy-start | bytes 5111812
  84.4 6.3 %collective-permute-start.10 = (bf16[4,64,3072]{2,1,0:T(8,128)(2,1)}, bf16[4,64,3072]{2,1,0:T(8,128)(2,1)}, u32[]{:S(2)}, u32[]{:S(2)}) collective-permute-start(bf16[4,64,3072]{2,1,0:T(8,128)(2,1)} %get-tuple-element.31.refs_4_), channel_id=1, source_target_pairs={{0,1},{1,0},{2,3},{3,2},{4,5},{5,4},{6,7},{7,6},{8,9},{9,8},{10,11... | collective-permute-start | bytes 4718600 | tf_op jit(solution)/shard_map/ppermute | solution.py:23
  85.7 77.7 %all-gather.11.cloned.1.call-start = ((), (), s32[]{:S(2)}) async-start(), calls=%async_computation.2 | async-start | bytes 1310720 | tf_op jit(solution)/shard_map/all_gather | solution.py:218
  86.8 47.2 %collective-permute-start.7 = (bf16[64,6656]{1,0:T(8,128)(2,1)}, bf16[64,6656]{1,0:T(8,128)(2,1)}, u32[]{:S(2)}, u32[]{:S(2)}) collective-permute-start(bf16[64,6656]{1,0:T(8,128)(2,1)} %slice.21), channel_id=1, source_target_pairs={{0,2},{1,3},{2,0},{3,1},{4,6},{5,7},{6,4},{7,5},{8,10},{9,11},{10,... | collective-permute-start | bytes 2555912 | tf_op jit(solution)/shard_map/ppermute | solution.py:23
  89.2 45.0 %collective-permute-start.5 = (bf16[64,6656]{1,0:T(8,128)(2,1)}, bf16[64,6656]{1,0:T(8,128)(2,1)}, u32[]{:S(2)}, u32[]{:S(2)}) collective-permute-start(bf16[64,6656]{1,0:T(8,128)(2,1)} %slice.20), channel_id=1, source_target_pairs={{0,4},{1,5},{2,6},{3,7},{4,0},{5,1},{6,2},{7,3},{8,12},{9,13},{10,... | collective-permute-start | bytes 2555912 | tf_op jit(solution)/shard_map/ppermute | solution.py:23
  95.1 39.4 %collective-permute-start.12 = (bf16[2,64,3072]{2,1,0:T(8,128)(2,1)}, bf16[2,64,3072]{2,1,0:T(8,128)(2,1)}, u32[]{:S(2)}, u32[]{:S(2)}) collective-permute-start(bf16[2,64,3072]{2,1,0:T(8,128)(2,1)} %get-tuple-element.33), channel_id=1, source_target_pairs={{0,4},{1,5},{2,6},{3,7},{4,0},{5,1},{6,2},{7,3},{8,12},{9,13},{10,... | collective-permute-start | bytes 2359304 | tf_op jit(solution)/shard_map/ppermute | solution.py:23
  132.5 2.5 collective-permute-start.14
  132.5 23.1 %collective-permute-start.11 = (bf16[2,64,3584]{2,1,0:T(8,128)(2,1)}, bf16[2,64,3584]{2,1,0:T(8,128)(2,1)}, u32[]{:S(2)}, u32[]{:S(2)}) collective-permute-start(bf16[2,64,3584]{2,1,0:T(8,128)(2,1)} %get-tuple-element.32.refs_0_), channel_id=1, source_target_pairs={{0,2},{1,3},{2,0},{3,1},{4,6},{5,7},{6,4},{7,5},{8,10},{9,11},{10,... | collective-permute-start | bytes 2752520 | tf_op jit(solution)/shard_map/ppermute | solution.py:23
  134.0 21.6 %collective-permute-start.13 = (bf16[4,32,3584]{2,1,0:T(8,128)(2,1)}, bf16[4,32,3584]{2,1,0:T(8,128)(2,1)}, u32[]{:S(2)}, u32[]{:S(2)}) collective-permute-start(bf16[4,32,3584]{2,1,0:T(8,128)(2,1)} %get-tuple-element.35.refs_0_), channel_id=1, source_target_pairs={{0,1},{1,0},{2,3},{3,2},{4,5},{5,4},{6,7},{7,6},{8,9},{9,8},{10,11... | collective-permute-start | bytes 2752520 | tf_op jit(solution)/shard_map/ppermute | solution.py:23
  134.2 25.3 %collective-permute-start.2 = (bf16[128,6656]{1,0:T(8,128)(2,1)}, bf16[128,6656]{1,0:T(8,128)(2,1)}, u32[]{:S(2)}, u32[]{:S(2)}) collective-permute-start(bf16[128,6656]{1,0:T(8,128)(2,1)} %refs_0_.7), channel_id=1, source_target_pairs={{0,1},{1,0},{2,3},{3,2},{4,5},{5,4},{6,7},{7,6},{8,9},{9,8},{10,11... | collective-permute-start | bytes 5111816 | tf_op jit(solution)/shard_map/ppermute | solution.py:23
  134.5 29.0 %collective-permute-start.4 = (bf16[128,6656]{1,0:T(8,128)(2,1)S(1)}, bf16[128,6656]{1,0:T(8,128)(2,1)}, u32[]{:S(2)}, u32[]{:S(2)}) collective-permute-start(bf16[128,6656]{1,0:T(8,128)(2,1)S(1)} %copy-done.1), channel_id=1, source_target_pairs={{0,1},{1,0},{2,3},{3,2},{4,5},{5,4},{6,7},{7,6},{8,9},{9,8},{10,11... | collective-permute-start | bytes 5111816 | tf_op jit(solution)/shard_map/ppermute | solution.py:23
  135.0 0.9 copy-start.5
  135.0 28.5 %collective-permute-start.3 = (bf16[128,6656]{1,0:T(8,128)(2,1)S(1)}, bf16[128,6656]{1,0:T(8,128)(2,1)}, u32[]{:S(2)}, u32[]{:S(2)}) collective-permute-start(bf16[128,6656]{1,0:T(8,128)(2,1)S(1)} %copy-done.3), channel_id=1, source_target_pairs={{0,1},{1,0},{2,3},{3,2},{4,5},{5,4},{6,7},{7,6},{8,9},{9,8},{10,11... | collective-permute-start | bytes 5111816 | tf_op jit(solution)/shard_map/ppermute | solution.py:23
  155.6 7.9 %collective-permute-start.8 = (bf16[64,6656]{1,0:T(8,128)(2,1)}, bf16[64,6656]{1,0:T(8,128)(2,1)}, u32[]{:S(2)}, u32[]{:S(2)}) collective-permute-start(bf16[64,6656]{1,0:T(8,128)(2,1)} %collective-permute-done.7.refs_8_), channel_id=1, source_target_pairs={{0,1},{1,0},{2,3},{3,2},{4,5},{5,4},{6,7},{7,6},{8,9},{9,8},{10,11... | collective-permute-start | bytes 2555912 | tf_op jit(solution)/shard_map/ppermute | solution.py:23
  155.6 7.9 %collective-permute-start.6 = (bf16[64,6656]{1,0:T(8,128)(2,1)}, bf16[64,6656]{1,0:T(8,128)(2,1)}, u32[]{:S(2)}, u32[]{:S(2)}) collective-permute-start(bf16[64,6656]{1,0:T(8,128)(2,1)} %collective-permute-done.5.refs_6_), channel_id=1, source_target_pairs={{0,1},{1,0},{2,3},{3,2},{4,5},{5,4},{6,7},{7,6},{8,9},{9,8},{10,11... | collective-permute-start | bytes 2555912 | tf_op jit(solution)/shard_map/ppermute | solution.py:23
  159.5 41.5 %collective-permute-start.17 = (bf16[2,32,3072]{2,1,0:T(8,128)(2,1)}, bf16[2,32,3072]{2,1,0:T(8,128)(2,1)}, u32[]{:S(2)}, u32[]{:S(2)}) collective-permute-start(bf16[2,32,3072]{2,1,0:T(8,128)(2,1)} %get-tuple-element.42), channel_id=1, source_target_pairs={{0,4},{1,5},{2,6},{3,7},{4,0},{5,1},{6,2},{7,3},{8,12},{9,13},{10,... | collective-permute-start | bytes 1179656 | tf_op jit(solution)/shard_map/ppermute | solution.py:23
  188.3 9.9 %copy-start.18 = (bf16[2,32,3584]{2,1,0:T(8,128)(2,1)S(1)}, bf16[2,32,3584]{2,1,0:T(8,128)(2,1)}, u32[]{:S(2)}) copy-start(bf16[2,32,3584]{2,1,0:T(8,128)(2,1)} %get-tuple-element.41) | copy-start | bytes 1376260
  188.3 11.3 %copy-start.11 = (bf16[1,64,3584]{2,1,0:T(8,128)(2,1)S(1)}, bf16[1,64,3584]{2,1,0:T(8,128)(2,1)}, u32[]{:S(2)}) copy-start(bf16[1,64,3584]{2,1,0:T(8,128)(2,1)} %get-tuple-element.38.refs_13_) | copy-start | bytes 1376260
  188.3 12.8 %copy-start.19 = (bf16[1,64,3072]{2,1,0:T(8,128)(2,1)S(1)}, bf16[1,64,3072]{2,1,0:T(8,128)(2,1)}, u32[]{:S(2)}) copy-start(bf16[1,64,3072]{2,1,0:T(8,128)(2,1)} %get-tuple-element.45) | copy-start | bytes 1179652
  188.3 30.9 %collective-permute-start.15 = (bf16[4,32,3584]{2,1,0:T(8,128)(2,1)}, bf16[4,32,3584]{2,1,0:T(8,128)(2,1)S(1)}, u32[]{:S(2)}, u32[]{:S(2)}) collective-permute-start(bf16[4,32,3584]{2,1,0:T(8,128)(2,1)} %get-tuple-element.40.refs_0_), channel_id=1, source_target_pairs={{0,1},{1,0},{2,3},{3,2},{4,5},{5,4},{6,7},{7,6},{8,9},{9,8},{10,11... | collective-permute-start | bytes 2752520 | tf_op jit(solution)/shard_map/ppermute | solution.py:23
  197.7 21.4 %collective-permute-start.18 = (bf16[4,32,3072]{2,1,0:T(8,128)(2,1)}, bf16[4,32,3072]{2,1,0:T(8,128)(2,1)S(1)}, u32[]{:S(2)}, u32[]{:S(2)}) collective-permute-start(bf16[4,32,3072]{2,1,0:T(8,128)(2,1)} %get-tuple-element.44.refs_13_), channel_id=1, source_target_pairs={{0,1},{1,0},{2,3},{3,2},{4,5},{5,4},{6,7},{7,6},{8,9},{9,8},{10,11... | collective-permute-start | bytes 2359304 | tf_op jit(solution)/shard_map/ppermute | solution.py:23
  198.1 21.0 %collective-permute-start.16 = (bf16[2,32,3584]{2,1,0:T(8,128)(2,1)S(1)}, bf16[2,32,3584]{2,1,0:T(8,128)(2,1)S(1)}, u32[]{:S(2)}, u32[]{:S(2)}) collective-permute-start(bf16[2,32,3584]{2,1,0:T(8,128)(2,1)S(1)} %copy-done.18), channel_id=1, source_target_pairs={{0,2},{1,3},{2,0},{3,1},{4,6},{5,7},{6,4},{7,5},{8,10},{9,11},{10,... | collective-permute-start | bytes 1376264 | tf_op jit(solution)/shard_map/ppermute | solution.py:23
  199.6 19.5 %collective-permute-start.19 = (bf16[1,64,3584]{2,1,0:T(8,128)(2,1)S(1)}, bf16[1,64,3584]{2,1,0:T(8,128)(2,1)S(1)}, u32[]{:S(2)}, u32[]{:S(2)}) collective-permute-start(bf16[1,64,3584]{2,1,0:T(8,128)(2,1)S(1)} %copy-done.11), channel_id=1, source_target_pairs={{0,4},{1,5},{2,6},{3,7},{4,0},{5,1},{6,2},{7,3},{8,12},{9,13},{10,... | collective-permute-start | bytes 1376264 | tf_op jit(solution)/shard_map/ppermute | solution.py:23
  201.1 18.0 %collective-permute-start.20 = (bf16[1,64,3072]{2,1,0:T(8,128)(2,1)S(1)}, bf16[1,64,3072]{2,1,0:T(8,128)(2,1)S(1)}, u32[]{:S(2)}, u32[]{:S(2)}) collective-permute-start(bf16[1,64,3072]{2,1,0:T(8,128)(2,1)S(1)} %copy-done.19), channel_id=1, source_target_pairs={{0,2},{1,3},{2,0},{3,1},{4,6},{5,7},{6,4},{7,5},{8,10},{9,11},{10,... | collective-permute-start | bytes 1179656 | tf_op jit(solution)/shard_map/ppermute | solution.py:23
  219.1 0.8 copy-start.13
  219.1 0.9 copy-start.7
  219.1 1.1 copy-start.12
  219.1 1.3 copy-start.6
  219.1 1.6 copy-start.4
  224.9 18.2 %collective-permute-start.24 = (bf16[1,32,3072]{2,1,0:T(8,128)(2,1)}, bf16[1,32,3072]{2,1,0:T(8,128)(2,1)S(1)}, u32[]{:S(2)}, u32[]{:S(2)}) collective-permute-start(bf16[1,32,3072]{2,1,0:T(8,128)(2,1)} %get-tuple-element.49), channel_id=1, source_target_pairs={{0,2},{1,3},{2,0},{3,1},{4,6},{5,7},{6,4},{7,5},{8,10},{9,11},{10,... | collective-permute-start | bytes 589832 | tf_op jit(solution)/shard_map/ppermute | solution.py:23
  226.5 16.7 %collective-permute-start.23 = (bf16[1,32,3584]{2,1,0:T(8,128)(2,1)}, bf16[1,32,3584]{2,1,0:T(8,128)(2,1)S(1)}, u32[]{:S(2)}, u32[]{:S(2)}) collective-permute-start(bf16[1,32,3584]{2,1,0:T(8,128)(2,1)} %get-tuple-element.48.refs_13_), channel_id=1, source_target_pairs={{0,4},{1,5},{2,6},{3,7},{4,0},{5,1},{6,2},{7,3},{8,12},{9,13},{10,... | collective-permute-start | bytes 688136 | tf_op jit(solution)/shard_map/ppermute | solution.py:23
  228.0 15.2 %collective-permute-start.22 = (bf16[2,32,3072]{2,1,0:T(8,128)(2,1)}, bf16[2,32,3072]{2,1,0:T(8,128)(2,1)S(1)}, u32[]{:S(2)}, u32[]{:S(2)}) collective-permute-start(bf16[2,32,3072]{2,1,0:T(8,128)(2,1)} %get-tuple-element.47), channel_id=1, source_target_pairs={{0,4},{1,5},{2,6},{3,7},{4,0},{5,1},{6,2},{7,3},{8,12},{9,13},{10,... | collective-permute-start | bytes 1179656 | tf_op jit(solution)/shard_map/ppermute | solution.py:23
  228.5 14.7 %collective-permute-start.21 = (bf16[2,32,3584]{2,1,0:T(8,128)(2,1)}, bf16[2,32,3584]{2,1,0:T(8,128)(2,1)S(1)}, u32[]{:S(2)}, u32[]{:S(2)}) collective-permute-start(bf16[2,32,3584]{2,1,0:T(8,128)(2,1)} %get-tuple-element.46), channel_id=1, source_target_pairs={{0,2},{1,3},{2,0},{3,1},{4,6},{5,7},{6,4},{7,5},{8,10},{9,11},{10,... | collective-permute-start | bytes 1376264 | tf_op jit(solution)/shard_map/ppermute | solution.py:23
  243.2 0.8 copy-start.15
  243.2 0.9 copy-start.9
  243.2 1.0 copy-start.8
  247.0 14.6 %collective-permute-start.26 = (bf16[1,32,3072]{2,1,0:T(8,128)(2,1)}, bf16[1,32,3072]{2,1,0:T(8,128)(2,1)S(1)}, u32[]{:S(2)}, u32[]{:S(2)}) collective-permute-start(bf16[1,32,3072]{2,1,0:T(8,128)(2,1)} %get-tuple-element.52), channel_id=1, source_target_pairs={{0,2},{1,3},{2,0},{3,1},{4,6},{5,7},{6,4},{7,5},{8,10},{9,11},{10,... | collective-permute-start | bytes 589832 | tf_op jit(solution)/shard_map/ppermute | solution.py:23
  248.6 13.1 %collective-permute-start.25 = (bf16[1,32,3584]{2,1,0:T(8,128)(2,1)}, bf16[1,32,3584]{2,1,0:T(8,128)(2,1)S(1)}, u32[]{:S(2)}, u32[]{:S(2)}) collective-permute-start(bf16[1,32,3584]{2,1,0:T(8,128)(2,1)} %get-tuple-element.51.refs_13_), channel_id=1, source_target_pairs={{0,4},{1,5},{2,6},{3,7},{4,0},{5,1},{6,2},{7,3},{8,12},{9,13},{10,... | collective-permute-start | bytes 688136 | tf_op jit(solution)/shard_map/ppermute | solution.py:23
  261.6 0.8 copy-start.14
  (2 other events, 1.3 us)
Sparse Core Ops, SparseCore 0:
  10.1 48.6 all-gather.6
  85.8 26.6 all-gather.8
  136.0 27.4 all-gather.10

commit v2 on v0

v2 whole, which is shorter than its diff:
```python
import functools

import jax
import jax.numpy as jnp
from jax import lax
from jax.experimental import pallas as pl
from jax.experimental.pallas import tpu as pltpu
from jax.sharding import PartitionSpec as P

F32, BF16 = jnp.float32, jnp.bfloat16
ANYWHERE = pl.BlockSpec(memory_space=pl.ANY)
PARAMS = pltpu.CompilerParams(vmem_limit_bytes=58 * 1024 * 1024)


def cost(flops, values):
    return pl.CostEstimate(flops=flops, bytes_accessed=2 * values, transcendentals=0)


def halving_order(bits):
    if not bits:
        return [0]
    keep = halving_order(bits[1:])
    return [o ^ bits[0] for o in keep] + keep


def flip(x, bits, n):
    return lax.ppermute(x, "col", [(i, i ^ bits[i & 1]) for i in range(n)])


def near_shift(x, s, n):
    pairs = [(i, (i + s) % n) for i in range(n)]
    return lax.ppermute(x, "row", [(i, j) for i, j in pairs if abs(i - j) <= n // 2])


def far_shift(x, e, n):
    half = n // 2
    up = [(i, i + e) for i in range(half, n - e)]
    down = [(i, i - e) for i in range(e, half)]
    return lax.ppermute(x, "row", up + down)


def assemble_kernel(n_row, orders, c, where_ref, own_ref, *refs):
    half = n_row // 2
    near, far = refs[: n_row - 1], refs[n_row - 1 : n_row + half - 2]
    grads_ref, turned_ref, rel = refs[-3:]
    me, row = where_ref[0], where_ref[1]
    rows = own_ref.shape[0]

    def put(s, ref):
        start = pl.multiple_of(lax.rem(row - s + n_row, n_row) * rows, rows)
        grads_ref[pl.ds(start, rows), :] = ref[...]

    put(0, own_ref)
    for s in range(1, n_row):
        if s == half:
            put(s, near[s - 1])
            continue
        came_far = (row < s) if s < half else (row >= s)
        pl.when(came_far)(functools.partial(put, s, far[abs(s - half) - 1]))
        pl.when(jnp.logical_not(came_far))(functools.partial(put, s, near[s - 1]))
    for p, (j0, j1) in enumerate(zip(*orders)):
        start = pl.multiple_of((me ^ jnp.where(me & 1, j1, j0)) * c, c)
        rel[pl.ds(p * c, c), :] = grads_ref[pl.ds(start, c), :]
    turned_ref[...] = rel[...].T


def assemble(where, own, near, far, orders, c, after):
    n_row, depth, rows = len(near) + 1, own.shape[1], len(orders[0]) * c
    steps = 2
    part = pl.BlockSpec((own.shape[0], depth // steps), lambda i, s: (0, i))
    arrays = [own, *near, *far]
    return pl.pallas_call(
        functools.partial(assemble_kernel, n_row, orders, c),
        out_shape=(
            jax.ShapeDtypeStruct((rows, depth), BF16),
            jax.ShapeDtypeStruct((depth, rows), BF16),
        ),
        grid_spec=pltpu.PrefetchScalarGridSpec(
            num_scalar_prefetch=1,
            grid=(steps,),
            in_specs=[part] * len(arrays) + [ANYWHERE] * len(after),
            out_specs=(
                pl.BlockSpec((rows, depth // steps), lambda i, s: (0, i)),
                pl.BlockSpec((depth // steps, rows), lambda i, s: (i, 0)),
            ),
            scratch_shapes=[pltpu.VMEM((rows, depth // steps), BF16)],
        ),
        compiler_params=PARAMS,
        cost_estimate=cost(0, 3 * rows * depth),
        name="assemble",
    )(where, *arrays, *after)


def partial_kernel(w_ref, g_ref, *refs):
    send_ref, keep_ref = refs[-2:]
    res = jnp.dot(w_ref[...], g_ref[...], preferred_element_type=F32).astype(BF16).T
    rows = res.shape[0] // 2
    send_ref[...] = res[:rows].reshape(send_ref.shape)
    keep_ref[...] = res[rows:].reshape(keep_ref.shape)


def partial_sums(turned, weight, n, c, tile, first, count, after):
    depth = weight.shape[1]
    out = jax.ShapeDtypeStruct((n // 2, c, count * tile), BF16)
    out_spec = pl.BlockSpec((n // 2, c, tile), lambda i: (0, 0, i))
    return pl.pallas_call(
        partial_kernel,
        out_shape=(out, out),
        grid=(count,),
        in_specs=[
            pl.BlockSpec((tile, depth), lambda i: (first + i, 0)),
            pl.BlockSpec((depth, n * c), lambda i: (0, 0), pipeline_mode=pl.Buffered(1)),
        ]
        + [ANYWHERE] * len(after),
        out_specs=(out_spec, out_spec),
        compiler_params=PARAMS,
        cost_estimate=cost(
            2 * n * c * depth * count * tile,
            n * c * depth + count * tile * depth + n * c * count * tile,
        ),
        name="partial_sums",
    )(weight, turned, *after)


def weight_kernel(places, chunks, n, where_ref, *refs):
    acts_refs, refs = refs[: len(places)], refs[len(places):]
    grads_refs, out_ref, acts = refs[: len(chunks)], refs[-2], refs[-1]
    me = where_ref[0]
    for (j0, j1), ref in zip(places, acts_refs):
        owner = me ^ jnp.where(me & 1, j1, j0)
        for at, c in chunks:
            start = pl.multiple_of(at * n + owner * c, c)
            acts[pl.ds(start, c), :] = ref[pl.ds(at, c), :]
    total = None
    for (at, c), ref in zip(chunks, grads_refs):
        term = lax.dot_general(
            acts[pl.ds(at * n, c * n), :], ref[...],
            (((0,), (0,)), ((), ())), preferred_element_type=F32,
        )
        total = term if total is None else total + term
    out_ref[...] = total.astype(BF16)


def weight_rows(where, pieces, grads, chunks, n, before, shape, tile, first, count, after):
    places = [place for place, _ in pieces]
    rows, width = sum(g.shape[0] for g in grads), shape[1]
    in_specs = [pl.BlockSpec((a.shape[0], tile), lambda i, s: (0, first + i)) for _, a in pieces]
    in_specs += [
        pl.BlockSpec(g.shape, lambda i, s: (0, 0), pipeline_mode=pl.Buffered(1)) for g in grads
    ]
    args = [a for _, a in pieces] + list(grads) + list(after)
    in_specs += [ANYWHERE] * len(after)
    aliases = {}
    if before is not None:
        in_specs.append(ANYWHERE)
        args.append(before)
        aliases = {len(args): 0}
    return pl.pallas_call(
        functools.partial(weight_kernel, places, chunks, n),
        out_shape=jax.ShapeDtypeStruct(shape, BF16),
        grid_spec=pltpu.PrefetchScalarGridSpec(
            num_scalar_prefetch=1,
            grid=(count,),
            in_specs=in_specs,
            out_specs=pl.BlockSpec((tile, width), lambda i, s: (first + i, 0)),
            scratch_shapes=[pltpu.VMEM((rows, tile), BF16)],
        ),
        input_output_aliases=aliases,
        compiler_params=PARAMS,
        cost_estimate=cost(
            2 * rows * width * count * tile, rows * width + (rows + width) * count * tile
        ),
        name="weight_rows",
    )(where, *args)


def sums_kernel(jobs, n_final, *refs):
    n_out = len(jobs) - n_final + (n_final > 0)
    outs, base = refs[-n_out:], 0
    at = 0
    for job, (width, cuts, spans) in enumerate(jobs):
        for lo, hi in zip(cuts, cuts[1:]):
            total = None
            for (begin, end), ref in zip(spans, refs[at : at + len(spans)]):
                if begin <= lo and hi <= end:
                    term = ref[:, :, lo - begin : hi - begin].astype(F32)
                    total = term if total is None else total + term
            if job < n_out - (n_final > 0):
                outs[job][:, :, lo:hi] = total.astype(BF16)
            else:
                outs[-1][:, base + lo : base + hi] = total[0].astype(BF16)
        if job >= len(jobs) - n_final:
            base += width
        at += len(spans)


def sums(going, ended, at, shape, before, after):
    parts = going + ended
    jobs = [part.job() for part in parts]
    steps = min(2, min(part.c for part in parts) // 16)
    in_specs, args, out_specs, out_shape, values = [], [], [], [], 0
    for part, (terms, size) in zip(parts, jobs):
        for array, first, _ in terms:
            in_specs.append(
                pl.BlockSpec(
                    (size, part.c // steps, array.shape[2]),
                    lambda i, b=first // size: (b, i, 0),
                )
            )
            args.append(array)
        values += (len(terms) + 1) * size * part.c * part.width
        if part in going:
            out_specs.append(pl.BlockSpec((size, part.c // steps, part.width), lambda i: (0, i, 0)))
            out_shape.append(jax.ShapeDtypeStruct((size, part.c, part.width), BF16))
    args += after
    in_specs += [ANYWHERE] * len(after)
    aliases = {}
    if ended:
        height = ended[0].c // steps
        out_specs.append(pl.BlockSpec((height, shape[1]), lambda i: (at // height + i, 0)))
        out_shape.append(jax.ShapeDtypeStruct(shape, BF16))
        if before is not None:
            aliases = {len(args): len(going)}
            args.append(before)
            in_specs.append(ANYWHERE)
    layout = [
        (part.width, part.cuts, [span for _, _, span in terms])
        for part, (terms, _) in zip(parts, jobs)
    ]
    outs = pl.pallas_call(
        functools.partial(sums_kernel, layout, len(ended)),
        out_shape=out_shape,
        grid=(steps,),
        in_specs=in_specs,
        out_specs=out_specs,
        input_output_aliases=aliases,
        compiler_params=PARAMS,
        cost_estimate=cost(values, values),
        name="sums",
    )(*args)
    for part, out in zip(going, outs):
        part.take(out)
    return outs[-1] if ended else before, [outs[0]]


class Halving:
    def __init__(self, sends, keeps, levels, n):
        self.levels, self.n = list(levels), n
        self.half, self.c = keeps[0].shape[:2]
        self.cuts = [0]
        for keep in keeps:
            self.cuts.append(self.cuts[-1] + keep.shape[2])
        self.width = self.cuts[-1]
        spans = list(zip(self.cuts, self.cuts[1:]))
        bits = self.levels.pop(0)
        self.terms = [[keep, 0, span] for keep, span in zip(keeps, spans)]
        self.terms += [[flip(send, bits, n), 0, span] for send, span in zip(sends, spans)]

    def take(self, out):
        self.terms.append([flip(out, self.levels.pop(0), self.n), 0, (0, self.width)])

    def job(self):
        size = self.half = self.half // 2 if self.levels else 1
        job = ([tuple(term) for term in self.terms], size)
        self.terms = [[array, first + size, span] for array, first, span in self.terms]
        return job


def hold_kernel(*refs):
    refs[-1][...] = jnp.zeros_like(refs[-1])


def hold(after):
    return pl.pallas_call(
        hold_kernel,
        out_shape=jax.ShapeDtypeStruct((8, 128), F32),
        grid=(1,),
        in_specs=[ANYWHERE] * len(after),
        out_specs=pl.BlockSpec((8, 128), lambda i: (0, 0)),
        compiler_params=PARAMS,
        cost_estimate=cost(50 * 10**9, 8 * 128),
        name="hold",
    )(*after)


def per_device(n_row, n_col, hidden_acts, out_grad, down_weight):
    tokens, units = hidden_acts.shape
    features = out_grad.shape[1]
    owners = n_col // n_row
    further = [1 << b for b in range(1, n_col.bit_length() - 1)]
    levels = [(1, 1), *zip(further, further[::-1])]
    kept = [halving_order([bits[h] for bits in levels[1:]]) for h in (0, 1)]
    orders = [[o ^ 1 for o in kept[1 - h]] + kept[h] for h in (0, 1)]
    c = tokens // 2
    chunks = [(0, c), (c, c)]
    tile = 128 * max(d for d in (1, 2, 4) if units % (128 * d) == 0)
    tiles = units // tile
    cut = (tiles + 1) // 2
    col, row = lax.axis_index("col"), lax.axis_index("row")
    where = jnp.stack([col, row]).astype(jnp.int32)

    whole = {bit: flip(hidden_acts, (bit, bit), n_col) for bit in further}

    by_owner = out_grad.reshape(owners, tokens, features)
    own = [by_owner[:, at : at + c].reshape(owners * c, features) for at, c in chunks]

    def near_blocks(x):
        return [near_shift(x, s, n_row) for s in range(1, n_row)]

    def far_blocks(near):
        return [far_shift(near[n_row // 2 - 1], e, n_row) for e in range(1, n_row // 2)]

    near0 = near_blocks(own[0])
    *near0, own[1] = lax.optimization_barrier((*near0, own[1]))
    far0 = far_blocks(near0)
    near1 = near_blocks(own[1])
    grads0, turned0 = assemble(where, own[0], near0, far0, orders, c, list(whole.values()))

    corners = []
    for t, bits in enumerate(levels[1:]):
        passed = [((j0 ^ bits[0], j1 ^ bits[1]), flip(a, bits, n_col)) for (j0, j1), a in corners]
        if t < len(further) - 1:
            mine = jnp.where(col & 1, whole[bits[1]], whole[bits[0]])
            corners = corners + passed + [(bits, mine)]
        else:
            corners = corners + passed
    corners = [((j0, j1), a) for (j0, j1), a in corners if j0 not in whole]

    def partials(turned, first, count, after):
        send, keep = partial_sums(turned, down_weight, n_col, c, tile, first, count, after)
        return send, keep, [send]

    send, keep, after = partials(turned0, 0, tiles, [])
    zero = Halving([send], [keep], levels, n_col)

    *near1, tied = lax.optimization_barrier((*near1, after[0]))
    far1 = far_blocks(near1)
    pieces = [((0, 0), hidden_acts)] + [((j, j), a) for j, a in whole.items()] + corners
    pieces += [((j1 ^ 1, j0 ^ 1), flip(a, (1, 1), n_col)) for (j0, j1), a in pieces]

    hidden_grad, weight_grad, done = None, None, 0

    def advance(going, ended, at, after):
        nonlocal hidden_grad
        hidden_grad, after = sums(going, ended, at, (tokens, units), hidden_grad, after)
        return after

    def work(count, after):
        nonlocal weight_grad, done
        count = min(tiles - done, count)
        if count:
            weight_grad = weight_rows(
                where, pieces, grads, chunks, n_col, weight_grad, (units, features), tile,
                done, count, after,
            )
            done += count
        return [weight_grad]

    after = [hold([tied] + near1 + [a for _, a in corners])]
    after = advance([zero], [], 0, after)
    exchanged = [a for _, a in pieces[n_col // 2 :]]
    grads1, turned1 = assemble(where, own[1], near1, far1, orders, c, after + exchanged[:1])
    grads = [grads0, grads1]
    send_a, keep_a, after = partials(turned1, 0, cut, after)
    a1 = Halving([send_a], [keep_a], levels, n_col)
    send_b, keep_b, after = partials(turned1, cut, tiles - cut, after)
    b1 = Halving([send_b], [keep_b], levels, n_col)
    after = advance([zero, a1], [], 0, after)
    after = work(2, after)
    after = advance([b1], [], 0, after)
    parts, steps = [zero, a1, b1], len(levels) - 1
    for step in range(steps):
        after = work(-(-(tiles - done) // (steps - step)), after)
        going, ended = [p for p in parts if p.levels], [p for p in parts if not p.levels]
        after = advance(going, ended, 0 if zero in ended else c, after)
        parts = going
    return weight_grad, hidden_grad


def solution(mesh):
    in_specs = (P("col", "row"), P("row", "col"), P("row", "col"))
    out_specs = (P("row", "col"), P("col", "row"))
    return jax.shard_map(
        functools.partial(per_device, mesh.shape["row"], mesh.shape["col"]),
        mesh=mesh, in_specs=in_specs, out_specs=out_specs, check_vma=False,
    )
```

time: 279 us -> 210 us (0.75)
  waiting for transfers between devices: 191 us -> 43.1 us
  Pallas kernels: 0 us -> 120 us
  matrix products: 73.4 us -> 0 us
  starting transfers between devices: 0.11 us -> 33.2 us
  between operations: 13.7 us -> 0.86 us
  local copies, waits for them, and re-layouts: 0 us -> 9.05 us
    all_gather x2 -> x0, waiting for transfers between devices: 124 us -> none  [the longest x1 84.4 us: per_device(): grad_full = lax.all_gather(out_grad, 'row', axis=0, tiled=True)]
    pallas_call x0 -> x14, Pallas kernels: none -> 120 us  [the longest x3 49.2 us: partial_sums(): pl.pallas_call(partial_kernel, out_shape=(out, out), grid=(count,), in_sp...]
    dot_general x2 -> x0, matrix products: 73.4 us -> none  [the longest x1 37.5 us: per_device(): lax.dot_general(grad_full, down_weight, (((1,), (1,)), ((), ())), preferr...]
    reduce_scatter x1 -> x0, waiting for transfers between devices: 66.2 us -> none  [per_device(): lax.psum_scatter(partial_grad.astype(jnp.bfloat16), 'col', scatter_dimens...]
    ppermute x0 -> x24, waiting for transfers between devices: none -> 43.1 us  [the longest x6 28.8 us: near_shift(): lax.ppermute(x, 'row', [(i, j) for i, j in pairs if abs(i - j) <= n // 2])]
    ppermute x0 -> x24, starting transfers between devices: none -> 33.2 us  [the longest x6 19.2 us: near_shift(): lax.ppermute(x, 'row', [(i, j) for i, j in pairs if abs(i - j) <= n // 2])]
    unnamed x0 -> x28, local copies, waits for them, and re-layouts: none -> 6.77 us
  transfers between devices with their start and end apart: 3 -> 24, of which waited for: 3 -> 5; matrix products, arithmetic and copies ran while one was open for 26% -> 2% of each run, Pallas kernels for 0% -> 54%
where the time goes in v2:
time: 210 us; the launch traced here: 209 us
  Pallas kernels  120 us (57%)
  waiting for transfers between devices  43.1 us (21%)
  starting transfers between devices  33.2 us (16%)
  local copies, waits for them, and re-layouts  9.05 us (4%)
  other arithmetic  2.16 us (1%)
    pallas_call x3, Pallas kernels, partial_sums(): pl.pallas_call(partial_kernel, out_shape=(out, out), grid=(count,), in_sp...  49.2 us
    pallas_call x3, Pallas kernels, weight_rows(): pl.pallas_call(functools.partial(weight_kernel, places, chunks, n), out_s...  46.7 us
    ppermute x6, waiting for transfers between devices, near_shift(): lax.ppermute(x, 'row', [(i, j) for i, j in pairs if abs(i - j) <= n // 2])  28.8 us
    ppermute x6, starting transfers between devices, near_shift(): lax.ppermute(x, 'row', [(i, j) for i, j in pairs if abs(i - j) <= n // 2])  19.2 us
    pallas_call x5, Pallas kernels, sums(): pl.pallas_call(functools.partial(sums_kernel, layout, len(ended)), out_sh...  15.6 us
    ppermute x16, starting transfers between devices, flip(): return lax.ppermute(x, 'col', [(i, i ^ bits[i & 1]) for i in range(n)])  11.3 us
    ppermute x2, waiting for transfers between devices, far_shift(): return lax.ppermute(x, 'row', up + down)  10.2 us
    pallas_call x2, Pallas kernels, assemble(): pl.pallas_call(functools.partial(assemble_kernel, n_row, orders, c), out_...  8.4 us
  transfers between devices with their start and end apart: 24, of which 5 were waited for; matrix products, arithmetic and copies ran while one was open for 2% of the time, Pallas kernels for 54%

profile of v2, /device:TPU:0, one launch (start us, length us, event | category | flops | bytes accessed | tf_op | source)
XLA Modules:
  0.0 208.9 jit_solution(3778551620834579264)
XLA Ops:
  0.6 3.0 %collective-permute-start.1 = (bf16[128,6656]{1,0:T(8,128)(2,1)}, bf16[128,6656]{1,0:T(8,128)(2,1)S(1)}, u32[]{:S(2)}, u32[]{:S(2)}) collective-permute-start(bf16[128,6656]{1,0:T(8,128)(2,1)} %refs_0_.5), channel_id=1, source_target_pairs={{0,4},{1,5},{2,6},{3,7},{4,0},{5,1},{6,2},{7,3},{8,12},{9,13},{10,... | collective-permute-start | bytes 5111816 | tf_op jit(solution)/shard_map/ppermute | solution.py:27
  3.7 1.5 collective-permute-start
  5.2 2.3 %fusion = (bf16[2,64,2048]{2,1,0:T(8,128)(2,1)}, bf16[2,64,2048]{2,1,0:T(8,128)(2,1)}) fusion(bf16[2,128,2048]{2,1,0:T(8,128)(2,1)} %bitcast.9), kind=kLoop, calls=%fused_computation.2 | loop fusion | bytes 2097152 | tf_op jit(solution)/shard_map/slice | solution.py:305
  7.4 1.3 collective-permute-start.9
  8.7 3.7 %collective-permute-start.8 = (bf16[128,2048]{1,0:T(8,128)(2,1)}, bf16[128,2048]{1,0:T(8,128)(2,1)}, u32[]{:S(2)}, u32[]{:S(2)}) collective-permute-start(bf16[128,2048]{1,0:T(8,128)(2,1)} %bitcast.3.own_ref), channel_id=1, source_target_pairs={{0,16},{8,24},{16,0},{24,8},{1,17},{9,25},{17,1},{25,9},{2,18},{10... | collective-permute-start | bytes 1572872 | tf_op jit(solution)/shard_map/ppermute | solution.py:32
  12.4 5.0 %collective-permute-start.7 = (bf16[128,2048]{1,0:T(8,128)(2,1)}, bf16[128,2048]{1,0:T(8,128)(2,1)}, u32[]{:S(2)}, u32[]{:S(2)}) collective-permute-start(bf16[128,2048]{1,0:T(8,128)(2,1)} %bitcast.3.own_ref), channel_id=1, source_target_pairs={{0,8},{8,16},{16,24},{1,9},{9,17},{17,25},{2,10},{10,18},{18,26},{... | collective-permute-start | bytes 1572872 | tf_op jit(solution)/shard_map/ppermute | solution.py:32
  17.5 5.9 %collective-permute-done.9.refs_2_ = bf16[128,2048]{1,0:T(8,128)(2,1)} collective-permute-done((bf16[128,2048]{1,0:T(8,128)(2,1)}, bf16[128,2048]{1,0:T(8,128)(2,1)}, u32[]{:S(2)}, u32[]{:S(2)}) %collective-permute-start.9) | collective-permute-done | bytes 524320 | tf_op jit(solution)/shard_map/ppermute | solution.py:32
  23.3 22.9 %collective-permute-done.8.refs_1_ = bf16[128,2048]{1,0:T(8,128)(2,1)} collective-permute-done((bf16[128,2048]{1,0:T(8,128)(2,1)}, bf16[128,2048]{1,0:T(8,128)(2,1)}, u32[]{:S(2)}, u32[]{:S(2)}) %collective-permute-start.8) | collective-permute-done | bytes 524320 | tf_op jit(solution)/shard_map/ppermute | solution.py:32
  46.2 1.3 collective-permute-start.10
  47.5 1.5 broadcast_select_fusion
  49.3 0.5 copy-done.2
  49.8 0.5 collective-permute-start.2
  50.3 0.7 pad_add_fusion.where_ref
  51.0 1.3 collective-permute-start.13
  52.3 5.6 %collective-permute-start.12 = (bf16[128,2048]{1,0:T(8,128)(2,1)}, bf16[128,2048]{1,0:T(8,128)(2,1)S(1)}, u32[]{:S(2)}, u32[]{:S(2)}) collective-permute-start(bf16[128,2048]{1,0:T(8,128)(2,1)} %bitcast.6), channel_id=1, source_target_pairs={{0,16},{8,24},{16,0},{24,8},{1,17},{9,25},{17,1},{25,9},{2,18},{10... | collective-permute-start | bytes 1572872 | tf_op jit(solution)/shard_map/ppermute | solution.py:32
  57.9 5.4 %collective-permute-done.10.refs_3_ = bf16[128,2048]{1,0:T(8,128)(2,1)} collective-permute-done((bf16[128,2048]{1,0:T(8,128)(2,1)}, bf16[128,2048]{1,0:T(8,128)(2,1)}, u32[]{:S(2)}, u32[]{:S(2)}) %collective-permute-start.10) | collective-permute-done | bytes 524320 | tf_op jit(solution)/shard_map/ppermute | solution.py:39
  63.3 2.3 %collective-permute-start.11 = (bf16[128,2048]{1,0:T(8,128)(2,1)}, bf16[128,2048]{1,0:T(8,128)(2,1)}, u32[]{:S(2)}, u32[]{:S(2)}) collective-permute-start(bf16[128,2048]{1,0:T(8,128)(2,1)} %bitcast.7), channel_id=1, source_target_pairs={{0,8},{8,16},{16,24},{1,9},{9,17},{17,25},{2,10},{10,18},{18,26},{... | collective-permute-start | bytes 1572872 | tf_op jit(solution)/shard_map/ppermute | solution.py:32
  65.6 4.2 %assemble.2 = (bf16[512,2048]{1,0:T(8,128)(2,1)}, bf16[2048,512]{1,0:T(8,128)(2,1)}) custom-call(s32[2]{0:T(128)} %pad_add_fusion.where_ref, bf16[128,2048]{1,0:T(8,128)(2,1)} %bitcast.3.own_ref, bf16[128,2048]{1,0:T(8,128)(2,1)} %collective-permute-done.7.refs_0_, bf16[128,2048]{1,0:T(8,128)(2,1)} %collective-permute-done.8.refs_1_, ...), custom_call_target="tpu_custom_call" | custom-call | bytes 6291456 | tf_op jit(solution)/shard_map/assemble/pallas_call | solution.py:72
  69.8 23.2 %partial_sums.3 = (bf16[4,64,6656]{2,1,0:T(8,128)(2,1)}, bf16[4,64,6656]{2,1,0:T(8,128)(2,1)}) custom-call(bf16[6656,2048]{1,0:T(8,128)(2,1)} %w_ref.5, bf16[2048,512]{1,0:T(8,128)(2,1)} %get-tuple-element.30.g_ref), custom_call_target="tpu_custom_call" | custom-call | flops 13958643712 | bytes 36175872 | tf_op jit(solution)/shard_map/partial_sums/pallas_call | solution.py:106
  93.1 1.5 collective-permute-start.14
  94.6 0.6 hold.1.refs_2_
  95.2 4.1 %collective-permute-done.15.refs_1_.refs_7_ = bf16[4,64,6656]{2,1,0:T(8,128)(2,1)S(1)} collective-permute-done((bf16[4,64,6656]{2,1,0:T(8,128)(2,1)}, bf16[4,64,6656]{2,1,0:T(8,128)(2,1)S(1)}, u32[]{:S(2)}, u32[]{:S(2)}) %collective-permute-start.15) | collective-permute-done | bytes 3407904 | tf_op jit(solution)/shard_map/ppermute | solution.py:27
  99.3 1.7 copy-done.4
  101.0 3.0 %sums.5.refs_4_.refs_0_ = bf16[2,64,6656]{2,1,0:T(8,128)(2,1)} custom-call(bf16[4,64,6656]{2,1,0:T(8,128)(2,1)} %get-tuple-element.35.refs_0_.refs_6_, bf16[4,64,6656]{2,1,0:T(8,128)(2,1)} %copy-done.4, f32[8,128]{1,0:T(8,128)} %hold.1.refs_2_), custom_call_target="tpu_custom_call" | custom-call | flops 2555904 | bytes 5111808 | tf_op jit(solution)/shard_map/sums/pallas_call | solution.py:230
  104.0 0.5 collective-permute-start.17
  104.6 4.8 %collective-permute-done.14.refs_3_ = bf16[128,2048]{1,0:T(8,128)(2,1)} collective-permute-done((bf16[128,2048]{1,0:T(8,128)(2,1)S(1)}, bf16[128,2048]{1,0:T(8,128)(2,1)}, u32[]{:S(2)}, u32[]{:S(2)}) %collective-permute-start.14) | collective-permute-done | bytes 524320 | tf_op jit(solution)/shard_map/ppermute | solution.py:39
  109.4 4.2 %assemble.3 = (bf16[512,2048]{1,0:T(8,128)(2,1)}, bf16[2048,512]{1,0:T(8,128)(2,1)}) custom-call(s32[2]{0:T(128)} %pad_add_fusion.where_ref, bf16[128,2048]{1,0:T(8,128)(2,1)} %bitcast.8, bf16[128,2048]{1,0:T(8,128)(2,1)} %collective-permute-done.11.refs_1_.refs_0_, bf16[128,2048]{1,0:T(8,128)(2,1)} %copy-done.11, bf16[128,2048]{1,0:T(8,128)(2,1)} %copy-done.10, ...), custom_call_target="tpu_custom_call" | custom-call | bytes 6291456 | tf_op jit(solution)/shard_map/assemble/pallas_call | solution.py:72
  113.6 13.9 %partial_sums.4 = (bf16[4,64,3584]{2,1,0:T(8,128)(2,1)}, bf16[4,64,3584]{2,1,0:T(8,128)(2,1)}) custom-call(bf16[6656,2048]{1,0:T(8,128)(2,1)} %w_ref.5, bf16[2048,512]{1,0:T(8,128)(2,1)} %get-tuple-element.38.g_ref, bf16[2,64,6656]{2,1,0:T(8,128)(2,1)} %sums.5.refs_4_.refs_0_), custom_call_target="tpu_custom_call" | custom-call | flops 7516192768 | bytes 20447232 | tf_op jit(solution)/shard_map/partial_sums/pallas_call | solution.py:106
  127.5 0.5 collective-permute-start.5
  128.1 0.4 collective-permute-start.6
  128.5 12.1 %partial_sums.5 = (bf16[4,64,3072]{2,1,0:T(8,128)(2,1)}, bf16[4,64,3072]{2,1,0:T(8,128)(2,1)}) custom-call(bf16[6656,2048]{1,0:T(8,128)(2,1)} %w_ref.5, bf16[2048,512]{1,0:T(8,128)(2,1)} %get-tuple-element.38.g_ref, bf16[4,64,3584]{2,1,0:T(8,128)(2,1)} %get-tuple-element.40.refs_0_), custom_call_target="tpu_custom_call" | custom-call | flops 6442450944 | bytes 17825792 | tf_op jit(solution)/shard_map/partial_sums/pallas_call | solution.py:106
  140.7 1.3 copy-done.6
  142.0 3.3 %sums.6 = (bf16[1,64,6656]{2,1,0:T(8,128)(2,1)}, bf16[2,64,3584]{2,1,0:T(8,128)(2,1)}) custom-call(bf16[4,64,6656]{2,1,0:T(8,128)(2,1)} %get-tuple-element.35.refs_0_.refs_6_, bf16[4,64,6656]{2,1,0:T(8,128)(2,1)} %copy-done.4, bf16[2,64,6656]{2,1,0:T(8,128)(2,1)} %collective-permute-done.17.refs_2_.refs_8_, ...), custom_call_target="tpu_custom_call" | custom-call | flops 3080192 | bytes 6160384 | tf_op jit(solution)/shard_map/sums/pallas_call | solution.py:230
  145.3 0.4 collective-permute-start.21
  145.7 0.5 collective-permute-start.18
  146.3 9.7 %weight_rows.3.refs_2_.refs_11_ = bf16[6656,2048]{1,0:T(8,128)(2,1)} custom-call(s32[2]{0:T(128)} %pad_add_fusion.where_ref, bf16[128,6656]{1,0:T(8,128)(2,1)} %refs_0_.5, bf16[128,6656]{1,0:T(8,128)(2,1)} %copy-done.2, bf16[128,6656]{1,0:T(8,128)(2,1)} %copy-done, bf16[128,6656]{1,0:T(8,128)(2,1)} %collective-permute-done.2.refs_4_.refs_3_, ...), custom_call_target="tpu_custom_call" | custom-call | flops 4294967296 | bytes 10485760 | tf_op jit(solution)/shard_map/weight_rows/pallas_call | solution.py:158
  156.0 2.2 %sums.7.refs_10_ = bf16[2,64,3072]{2,1,0:T(8,128)(2,1)} custom-call(bf16[4,64,3072]{2,1,0:T(8,128)(2,1)} %get-tuple-element.43.refs_0_.refs_3_.refs_4_, bf16[4,64,3072]{2,1,0:T(8,128)(2,1)} %collective-permute-done.19.refs_1_.refs_4_.refs_5_, bf16[6656,2048]{1,0:T(8,128)(2,1)} %weight_rows.3.refs_2_.refs_11_), custom_call_target="tpu_custom_call" | custom-call | flops 1179648 | bytes 2359296 | tf_op jit(solution)/shard_map/sums/pallas_call | solution.py:230
  158.3 1.5 collective-permute-start.20
  159.8 19.7 %weight_rows.4.refs_10_.refs_11_ = bf16[6656,2048]{1,0:T(8,128)(2,1)} custom-call(s32[2]{0:T(128)} %pad_add_fusion.where_ref, bf16[128,6656]{1,0:T(8,128)(2,1)} %refs_0_.5, bf16[128,6656]{1,0:T(8,128)(2,1)} %copy-done.2, bf16[128,6656]{1,0:T(8,128)(2,1)} %copy-done, ...), custom_call_target="tpu_custom_call", output_to_operand_aliasing={{}: (12, {})} | custom-call | flops 12884901888 | bytes 23068672 | tf_op jit(solution)/shard_map/weight_rows/pallas_call | solution.py:158
  179.5 0.9 copy-done.8
  180.4 0.3 copy-done.9
  180.7 0.9 copy-done.7
  181.7 4.0 %sums.8 = (bf16[1,64,3584]{2,1,0:T(8,128)(2,1)}, bf16[1,64,3072]{2,1,0:T(8,128)(2,1)}, bf16[128,6656]{1,0:T(8,128)(2,1)}) custom-call(bf16[4,64,3584]{2,1,0:T(8,128)(2,1)} %get-tuple-element.39.refs_3_.refs_0_, bf16[4,64,3584]{2,1,0:T(8,128)(2,1)} %copy-done.6, bf16[2,64,3584]{2,1,0:T(8,128)(2,1)} %copy-done.7, ...), custom_call_target="tpu_custom_call" | custom-call | flops 3833856 | bytes 7667712 | tf_op jit(solution)/shard_map/sums/pallas_call | solution.py:230
  185.7 1.7 collective-permute-start.23
  187.3 0.4 collective-permute-start.22
  187.8 17.2 %weight_rows.5.refs_8_ = bf16[6656,2048]{1,0:T(8,128)(2,1)} custom-call(s32[2]{0:T(128)} %pad_add_fusion.where_ref, bf16[128,6656]{1,0:T(8,128)(2,1)} %refs_0_.5, bf16[128,6656]{1,0:T(8,128)(2,1)} %copy-done.2, bf16[128,6656]{1,0:T(8,128)(2,1)} %copy-done, bf16[128,6656]{1,0:T(8,128)(2,1)} %collective-permute-done.2.refs_4_.refs_3_, ...), custom_call_target="tpu_custom_call", output_to_operand_aliasing={{}: (12, {})} | custom-call | flops 10737418240 | bytes 19922944 | tf_op jit(solution)/shard_map/weight_rows/pallas_call | solution.py:158
  205.0 0.7 copy-done.13
  205.9 3.0 %sums.9 = bf16[128,6656]{1,0:T(8,128)(2,1)} custom-call(bf16[4,64,3584]{2,1,0:T(8,128)(2,1)} %get-tuple-element.39.refs_3_.refs_0_, bf16[4,64,3584]{2,1,0:T(8,128)(2,1)} %copy-done.6, bf16[2,64,3584]{2,1,0:T(8,128)(2,1)} %copy-done.7, bf16[1,64,3584]{2,1,0:T(8,128)(2,1)} %copy-done.12, ...), custom_call_target="tpu_custom_call", output_to_operand_aliasing={{}: (9, {})} | custom-call | flops 2129920 | bytes 4259840 | tf_op jit(solution)/shard_map/sums/pallas_call | solution.py:230
  (45 shorter events, 0.7 us)
Async XLA Ops:
  0.6 46.9 %collective-permute-start.1 = (bf16[128,6656]{1,0:T(8,128)(2,1)}, bf16[128,6656]{1,0:T(8,128)(2,1)S(1)}, u32[]{:S(2)}, u32[]{:S(2)}) collective-permute-start(bf16[128,6656]{1,0:T(8,128)(2,1)} %refs_0_.5), channel_id=1, source_target_pairs={{0,4},{1,5},{2,6},{3,7},{4,0},{5,1},{6,2},{7,3},{8,12},{9,13},{10,... | collective-permute-start | bytes 5111816 | tf_op jit(solution)/shard_map/ppermute | solution.py:27
  3.7 43.9 %collective-permute-start = (bf16[128,6656]{1,0:T(8,128)(2,1)}, bf16[128,6656]{1,0:T(8,128)(2,1)S(1)}, u32[]{:S(2)}, u32[]{:S(2)}) collective-permute-start(bf16[128,6656]{1,0:T(8,128)(2,1)} %refs_0_.5), channel_id=1, source_target_pairs={{0,2},{1,3},{2,0},{3,1},{4,6},{5,7},{6,4},{7,5},{8,10},{9,11},{10,... | collective-permute-start | bytes 5111816 | tf_op jit(solution)/shard_map/ppermute | solution.py:27
  7.4 15.9 %collective-permute-start.9 = (bf16[128,2048]{1,0:T(8,128)(2,1)}, bf16[128,2048]{1,0:T(8,128)(2,1)}, u32[]{:S(2)}, u32[]{:S(2)}) collective-permute-start(bf16[128,2048]{1,0:T(8,128)(2,1)} %bitcast.3.own_ref), channel_id=1, source_target_pairs={{8,0},{16,8},{24,16},{9,1},{17,9},{25,17},{10,2},{18,10},{26,18},{... | collective-permute-start | bytes 1572872 | tf_op jit(solution)/shard_map/ppermute | solution.py:32
  8.7 37.5 %collective-permute-start.8 = (bf16[128,2048]{1,0:T(8,128)(2,1)}, bf16[128,2048]{1,0:T(8,128)(2,1)}, u32[]{:S(2)}, u32[]{:S(2)}) collective-permute-start(bf16[128,2048]{1,0:T(8,128)(2,1)} %bitcast.3.own_ref), channel_id=1, source_target_pairs={{0,16},{8,24},{16,0},{24,8},{1,17},{9,25},{17,1},{25,9},{2,18},{10... | collective-permute-start | bytes 1572872 | tf_op jit(solution)/shard_map/ppermute | solution.py:32
  12.4 33.8 %collective-permute-start.7 = (bf16[128,2048]{1,0:T(8,128)(2,1)}, bf16[128,2048]{1,0:T(8,128)(2,1)}, u32[]{:S(2)}, u32[]{:S(2)}) collective-permute-start(bf16[128,2048]{1,0:T(8,128)(2,1)} %bitcast.3.own_ref), channel_id=1, source_target_pairs={{0,8},{8,16},{16,24},{1,9},{9,17},{17,25},{2,10},{10,18},{18,26},{... | collective-permute-start | bytes 1572872 | tf_op jit(solution)/shard_map/ppermute | solution.py:32
  46.2 17.1 %collective-permute-start.10 = (bf16[128,2048]{1,0:T(8,128)(2,1)}, bf16[128,2048]{1,0:T(8,128)(2,1)}, u32[]{:S(2)}, u32[]{:S(2)}) collective-permute-start(bf16[128,2048]{1,0:T(8,128)(2,1)} %collective-permute-done.8.refs_1_), channel_id=1, source_target_pairs={{16,24},{8,0},{17,25},{9,1},{18,26},{10,2},{19,27},{11,3},{20,28},... | collective-permute-start | bytes 1572872 | tf_op jit(solution)/shard_map/ppermute | solution.py:39
  47.5 1.7 copy-start
  47.5 2.3 %copy-start.2 = (bf16[128,6656]{1,0:T(8,128)(2,1)}, bf16[128,6656]{1,0:T(8,128)(2,1)S(1)}, u32[]{:S(2)}) copy-start(bf16[128,6656]{1,0:T(8,128)(2,1)S(1)} %collective-permute-done.refs_4_.refs_1_) | copy-start | bytes 5111812
  49.8 44.8 %collective-permute-start.2 = (bf16[128,6656]{1,0:T(8,128)(2,1)}, bf16[128,6656]{1,0:T(8,128)(2,1)}, u32[]{:S(2)}, u32[]{:S(2)}) collective-permute-start(bf16[128,6656]{1,0:T(8,128)(2,1)} %broadcast_select_fusion), channel_id=1, source_target_pairs={{0,4},{1,3},{2,6},{3,1},{4,0},{5,7},{6,2},{7,5},{8,12},{9,11},{10,... | collective-permute-start | bytes 5111816 | tf_op jit(solution)/shard_map/ppermute | solution.py:27
  50.3 54.3 %collective-permute-start.3 = (bf16[128,6656]{1,0:T(8,128)(2,1)}, bf16[128,6656]{1,0:T(8,128)(2,1)S(1)}, u32[]{:S(2)}, u32[]{:S(2)}) collective-permute-start(bf16[128,6656]{1,0:T(8,128)(2,1)} %refs_0_.5), channel_id=1, source_target_pairs={{0,1},{1,0},{2,3},{3,2},{4,5},{5,4},{6,7},{7,6},{8,9},{9,8},{10,11... | collective-permute-start | bytes 5111816 | tf_op jit(solution)/shard_map/ppermute | solution.py:27
  51.0 42.0 %collective-permute-start.13 = (bf16[128,2048]{1,0:T(8,128)(2,1)}, bf16[128,2048]{1,0:T(8,128)(2,1)S(1)}, u32[]{:S(2)}, u32[]{:S(2)}) collective-permute-start(bf16[128,2048]{1,0:T(8,128)(2,1)} %bitcast.5), channel_id=1, source_target_pairs={{8,0},{16,8},{24,16},{9,1},{17,9},{25,17},{10,2},{18,10},{26,18},{... | collective-permute-start | bytes 1572872 | tf_op jit(solution)/shard_map/ppermute | solution.py:32
  52.3 40.8 %collective-permute-start.12 = (bf16[128,2048]{1,0:T(8,128)(2,1)}, bf16[128,2048]{1,0:T(8,128)(2,1)S(1)}, u32[]{:S(2)}, u32[]{:S(2)}) collective-permute-start(bf16[128,2048]{1,0:T(8,128)(2,1)} %bitcast.6), channel_id=1, source_target_pairs={{0,16},{8,24},{16,0},{24,8},{1,17},{9,25},{17,1},{25,9},{2,18},{10... | collective-permute-start | bytes 1572872 | tf_op jit(solution)/shard_map/ppermute | solution.py:32
  63.3 29.8 %collective-permute-start.11 = (bf16[128,2048]{1,0:T(8,128)(2,1)}, bf16[128,2048]{1,0:T(8,128)(2,1)}, u32[]{:S(2)}, u32[]{:S(2)}) collective-permute-start(bf16[128,2048]{1,0:T(8,128)(2,1)} %bitcast.7), channel_id=1, source_target_pairs={{0,8},{8,16},{16,24},{1,9},{9,17},{17,25},{2,10},{10,18},{18,26},{... | collective-permute-start | bytes 1572872 | tf_op jit(solution)/shard_map/ppermute | solution.py:32
  93.0 1.6 copy-start.10
  93.0 6.3 %collective-permute-start.15 = (bf16[4,64,6656]{2,1,0:T(8,128)(2,1)}, bf16[4,64,6656]{2,1,0:T(8,128)(2,1)S(1)}, u32[]{:S(2)}, u32[]{:S(2)}) collective-permute-start(bf16[4,64,6656]{2,1,0:T(8,128)(2,1)} %get-tuple-element.36.refs_0_), channel_id=1, source_target_pairs={{0,1},{1,0},{2,3},{3,2},{4,5},{5,4},{6,7},{7,6},{8,9},{9,8},{10,11... | collective-permute-start | bytes 10223624 | tf_op jit(solution)/shard_map/ppermute | solution.py:27
  93.1 1.5 copy-start.11
  93.1 16.3 %collective-permute-start.14 = (bf16[128,2048]{1,0:T(8,128)(2,1)S(1)}, bf16[128,2048]{1,0:T(8,128)(2,1)}, u32[]{:S(2)}, u32[]{:S(2)}) collective-permute-start(bf16[128,2048]{1,0:T(8,128)(2,1)S(1)} %collective-permute-done.12.refs_2_.refs_1_), channel_id=1, source_target_pairs={{16,24},{8,0},{17,25},{9,1},{18,26},{10,2},{19,27},{11,3},{20,28},... | collective-permute-start | bytes 1572872 | tf_op jit(solution)/shard_map/ppermute | solution.py:39
  99.3 1.7 copy-start.4
  104.0 36.6 %collective-permute-start.17 = (bf16[2,64,6656]{2,1,0:T(8,128)(2,1)}, bf16[2,64,6656]{2,1,0:T(8,128)(2,1)}, u32[]{:S(2)}, u32[]{:S(2)}) collective-permute-start(bf16[2,64,6656]{2,1,0:T(8,128)(2,1)} %sums.5.refs_4_.refs_0_), channel_id=1, source_target_pairs={{0,2},{1,5},{2,0},{3,7},{4,6},{5,1},{6,4},{7,3},{8,10},{9,13},{10,... | collective-permute-start | bytes 5111816 | tf_op jit(solution)/shard_map/ppermute | solution.py:27
  104.6 4.8 %copy-start.5 = (bf16[128,6656]{1,0:T(8,128)(2,1)}, bf16[128,6656]{1,0:T(8,128)(2,1)S(1)}, u32[]{:S(2)}) copy-start(bf16[128,6656]{1,0:T(8,128)(2,1)S(1)} %collective-permute-done.3.refs_5_.refs_4_) | copy-start | bytes 5111812
  113.6 13.9 %copy-start.1 = (bf16[128,6656]{1,0:T(8,128)(2,1)S(1)}, bf16[128,6656]{1,0:T(8,128)(2,1)}, u32[]{:S(2)}) copy-start(bf16[128,6656]{1,0:T(8,128)(2,1)} %copy-done) | copy-start | bytes 5111812
  113.6 14.5 %copy-start.3 = (bf16[128,6656]{1,0:T(8,128)(2,1)S(1)}, bf16[128,6656]{1,0:T(8,128)(2,1)}, u32[]{:S(2)}) copy-start(bf16[128,6656]{1,0:T(8,128)(2,1)} %copy-done.2) | copy-start | bytes 5111812
  127.5 13.2 %collective-permute-start.16 = (bf16[4,64,3584]{2,1,0:T(8,128)(2,1)}, bf16[4,64,3584]{2,1,0:T(8,128)(2,1)S(1)}, u32[]{:S(2)}, u32[]{:S(2)}) collective-permute-start(bf16[4,64,3584]{2,1,0:T(8,128)(2,1)} %get-tuple-element.40.refs_0_), channel_id=1, source_target_pairs={{0,1},{1,0},{2,3},{3,2},{4,5},{5,4},{6,7},{7,6},{8,9},{9,8},{10,11... | collective-permute-start | bytes 5505032 | tf_op jit(solution)/shard_map/ppermute | solution.py:27
  127.5 18.2 %collective-permute-start.5 = (bf16[128,6656]{1,0:T(8,128)(2,1)S(1)}, bf16[128,6656]{1,0:T(8,128)(2,1)}, u32[]{:S(2)}, u32[]{:S(2)}) collective-permute-start(bf16[128,6656]{1,0:T(8,128)(2,1)S(1)} %copy-done.1), channel_id=1, source_target_pairs={{0,1},{1,0},{2,3},{3,2},{4,5},{5,4},{6,7},{7,6},{8,9},{9,8},{10,11... | collective-permute-start | bytes 5111816 | tf_op jit(solution)/shard_map/ppermute | solution.py:27
  128.0 18.3 %collective-permute-start.4 = (bf16[128,6656]{1,0:T(8,128)(2,1)S(1)}, bf16[128,6656]{1,0:T(8,128)(2,1)}, u32[]{:S(2)}, u32[]{:S(2)}) collective-permute-start(bf16[128,6656]{1,0:T(8,128)(2,1)S(1)} %copy-done.3), channel_id=1, source_target_pairs={{0,1},{1,0},{2,3},{3,2},{4,5},{5,4},{6,7},{7,6},{8,9},{9,8},{10,11... | collective-permute-start | bytes 5111816 | tf_op jit(solution)/shard_map/ppermute | solution.py:27
  128.1 18.2 %collective-permute-start.6 = (bf16[128,6656]{1,0:T(8,128)(2,1)}, bf16[128,6656]{1,0:T(8,128)(2,1)}, u32[]{:S(2)}, u32[]{:S(2)}) collective-permute-start(bf16[128,6656]{1,0:T(8,128)(2,1)} %collective-permute-done.2.refs_4_.refs_3_), channel_id=1, source_target_pairs={{0,1},{1,0},{2,3},{3,2},{4,5},{5,4},{6,7},{7,6},{8,9},{9,8},{10,11... | collective-permute-start | bytes 5111816 | tf_op jit(solution)/shard_map/ppermute | solution.py:27
  140.7 15.4 %collective-permute-start.19 = (bf16[4,64,3072]{2,1,0:T(8,128)(2,1)}, bf16[4,64,3072]{2,1,0:T(8,128)(2,1)}, u32[]{:S(2)}, u32[]{:S(2)}) collective-permute-start(bf16[4,64,3072]{2,1,0:T(8,128)(2,1)} %get-tuple-element.41.refs_5_), channel_id=1, source_target_pairs={{0,1},{1,0},{2,3},{3,2},{4,5},{5,4},{6,7},{7,6},{8,9},{9,8},{10,11... | collective-permute-start | bytes 4718600 | tf_op jit(solution)/shard_map/ppermute | solution.py:27
  140.7 1.3 copy-start.6
  145.3 34.2 %collective-permute-start.21 = (bf16[1,64,6656]{2,1,0:T(8,128)(2,1)}, bf16[1,64,6656]{2,1,0:T(8,128)(2,1)S(1)}, u32[]{:S(2)}, u32[]{:S(2)}) collective-permute-start(bf16[1,64,6656]{2,1,0:T(8,128)(2,1)} %get-tuple-element.44.refs_10_), channel_id=1, source_target_pairs={{0,4},{1,3},{2,6},{3,1},{4,0},{5,7},{6,2},{7,5},{8,12},{9,11},{10,... | collective-permute-start | bytes 2555912 | tf_op jit(solution)/shard_map/ppermute | solution.py:27
  145.7 33.8 %collective-permute-start.18 = (bf16[2,64,3584]{2,1,0:T(8,128)(2,1)}, bf16[2,64,3584]{2,1,0:T(8,128)(2,1)S(1)}, u32[]{:S(2)}, u32[]{:S(2)}) collective-permute-start(bf16[2,64,3584]{2,1,0:T(8,128)(2,1)} %get-tuple-element.42), channel_id=1, source_target_pairs={{0,2},{1,5},{2,0},{3,7},{4,6},{5,1},{6,4},{7,3},{8,10},{9,13},{10,... | collective-permute-start | bytes 2752520 | tf_op jit(solution)/shard_map/ppermute | solution.py:27
  158.3 21.2 %collective-permute-start.20 = (bf16[2,64,3072]{2,1,0:T(8,128)(2,1)}, bf16[2,64,3072]{2,1,0:T(8,128)(2,1)S(1)}, u32[]{:S(2)}, u32[]{:S(2)}) collective-permute-start(bf16[2,64,3072]{2,1,0:T(8,128)(2,1)} %sums.7.refs_10_), channel_id=1, source_target_pairs={{0,2},{1,5},{2,0},{3,7},{4,6},{5,1},{6,4},{7,3},{8,10},{9,13},{10,... | collective-permute-start | bytes 2359304 | tf_op jit(solution)/shard_map/ppermute | solution.py:27
  179.5 0.9 copy-start.8
  179.5 1.2 copy-start.9
  180.7 0.9 copy-start.7
  185.7 19.3 %collective-permute-start.23 = (bf16[1,64,3072]{2,1,0:T(8,128)(2,1)}, bf16[1,64,3072]{2,1,0:T(8,128)(2,1)S(1)}, u32[]{:S(2)}, u32[]{:S(2)}) collective-permute-start(bf16[1,64,3072]{2,1,0:T(8,128)(2,1)} %get-tuple-element.46), channel_id=1, source_target_pairs={{0,4},{1,3},{2,6},{3,1},{4,0},{5,7},{6,2},{7,5},{8,12},{9,11},{10,... | collective-permute-start | bytes 1179656 | tf_op jit(solution)/shard_map/ppermute | solution.py:27
  187.3 17.7 %collective-permute-start.22 = (bf16[1,64,3584]{2,1,0:T(8,128)(2,1)}, bf16[1,64,3584]{2,1,0:T(8,128)(2,1)S(1)}, u32[]{:S(2)}, u32[]{:S(2)}) collective-permute-start(bf16[1,64,3584]{2,1,0:T(8,128)(2,1)} %get-tuple-element.45.refs_10_), channel_id=1, source_target_pairs={{0,4},{1,3},{2,6},{3,1},{4,0},{5,7},{6,2},{7,5},{8,12},{9,11},{10,... | collective-permute-start | bytes 1376264 | tf_op jit(solution)/shard_map/ppermute | solution.py:27
  205.0 0.8 copy-start.13
  205.0 0.9 copy-start.12

commit v3 on v0

v3 whole, which is shorter than its diff:
```python
import functools

import jax
import jax.numpy as jnp
from jax import lax
from jax.experimental import pallas as pl
from jax.experimental.pallas import tpu as pltpu
from jax.sharding import PartitionSpec as P

F32, BF16 = jnp.float32, jnp.bfloat16
ANYWHERE = pl.BlockSpec(memory_space=pl.ANY)
PARAMS = pltpu.CompilerParams(vmem_limit_bytes=58 * 1024 * 1024)


def cost(flops, values):
    return pl.CostEstimate(flops=flops, bytes_accessed=2 * values, transcendentals=0)


def once(shape, index):
    return pl.BlockSpec(shape, lambda *_: index, pipeline_mode=pl.Buffered(1))


def halving_order(bits):
    if not bits:
        return [0]
    keep = halving_order(bits[1:])
    return [o ^ bits[0] for o in keep] + keep


def flip(x, bits, n):
    return lax.ppermute(x, "col", [(i, i ^ bits[i & 1]) for i in range(n)])


def near_shift(x, s, n):
    pairs = [(i, (i + s) % n) for i in range(n)]
    return lax.ppermute(x, "row", [(i, j) for i, j in pairs if abs(i - j) <= n // 2])


def far_shift(x, e, n):
    half = n // 2
    up = [(i, i + e) for i in range(half, n - e)]
    down = [(i, i - e) for i in range(e, half)]
    return lax.ppermute(x, "row", up + down)


def slot_of(row, owner, n_row):
    return lax.rem(row - owner // 2 - 1 + n_row, n_row)


def turn_kernel(c, where_ref, own_ref, w_ref, turned_ref, *refs):
    outs, mine = refs[:-1], refs[-1]
    core = where_ref[0] & 1

    @pl.when(pl.program_id(0) == 0)
    def _():
        for p in range(4):
            h = core if p % 2 else 1 - core
            mine[pl.ds(p * c, c), :] = own_ref[h, pl.ds(p // 2 * c, c), :]

    turned = w_ref[...].T
    turned_ref[0] = turned
    res = jnp.dot(mine[...], turned, preferred_element_type=F32).astype(BF16)
    for p, ref in enumerate(outs):
        ref[0] = res[p * c : (p + 1) * c]


def turn_weights(where, own, weight, c, n_row, tile):
    units, depth = weight.shape
    tiles = units // tile
    part = jax.ShapeDtypeStruct((n_row, c, units), BF16)
    part_spec = pl.BlockSpec((1, c, tile), lambda i, s: (n_row - 1, 0, i))
    return pl.pallas_call(
        functools.partial(turn_kernel, c),
        out_shape=(jax.ShapeDtypeStruct((tiles, depth, tile), BF16),) + (part,) * 4,
        grid_spec=pltpu.PrefetchScalarGridSpec(
            num_scalar_prefetch=1,
            grid=(tiles,),
            in_specs=[once(own.shape, (0, 0, 0)), pl.BlockSpec((tile, depth), lambda i, s: (i, 0))],
            out_specs=(pl.BlockSpec((1, depth, tile), lambda i, s: (i, 0, 0)),) + (part_spec,) * 4,
            scratch_shapes=[pltpu.VMEM((4 * c, depth), BF16)],
        ),
        compiler_params=PARAMS,
        cost_estimate=cost(8 * c * depth * units, 2 * units * depth + 4 * c * units),
        name="turn_weights",
    )(where, own, weight)


def partial_kernel(n_row, c, where_ref, w_ref, *refs):
    half = n_row // 2
    near, far = refs[: n_row - 1], refs[n_row - 1 : n_row + half - 2]
    send_ref, keep_ref, rows_ref, lhs = refs[-4:]
    core, row = where_ref[0] & 1, where_ref[1]
    count = (n_row - 1) * c

    def put(s, ref):
        lhs[pl.ds((s - 1) * c, c), :] = ref[1 - core]
        lhs[pl.ds(count + (s - 1) * c, c), :] = ref[core]

    @pl.when(pl.program_id(0) == 0)
    def _():
        for s in range(1, n_row):
            if s == half:
                put(s, near[s - 1])
                continue
            came_far = (row < s) if s < half else (row >= s)
            pl.when(came_far)(functools.partial(put, s, far[abs(s - half) - 1]))
            pl.when(jnp.logical_not(came_far))(functools.partial(put, s, near[s - 1]))
        rows_ref[...] = lhs[...]

    res = jnp.dot(lhs[...], w_ref[0], preferred_element_type=F32).astype(BF16)
    send_ref[...] = res[:count].reshape(send_ref.shape)
    keep_ref[...] = res[count:].reshape(keep_ref.shape)


def partial_sums(where, turned, near, far, send, keep, k, after):
    n_row, c, units = send.shape
    tiles, depth, tile = turned.shape
    count = 2 * (n_row - 1) * c
    blocks = near + far
    in_specs = [pl.BlockSpec((1, depth, tile), lambda i, s: (i, 0, 0))]
    in_specs += [once((2, c, depth), (0, k if a.shape[1] > c else 0, 0)) for a in blocks]
    in_specs += [ANYWHERE] * (2 + len(after))
    part = jax.ShapeDtypeStruct(send.shape, BF16)
    part_spec = pl.BlockSpec((n_row - 1, c, tile), lambda i, s: (0, 0, i))
    return pl.pallas_call(
        functools.partial(partial_kernel, n_row, c),
        out_shape=(part, part, jax.ShapeDtypeStruct((count, depth), BF16)),
        grid_spec=pltpu.PrefetchScalarGridSpec(
            num_scalar_prefetch=1,
            grid=(tiles,),
            in_specs=in_specs,
            out_specs=(part_spec, part_spec, pl.BlockSpec((count, depth), lambda i, s: (0, 0))),
            scratch_shapes=[pltpu.VMEM((count, depth), BF16)],
        ),
        input_output_aliases={2 + len(blocks): 0, 3 + len(blocks): 1},
        compiler_params=PARAMS,
        cost_estimate=cost(
            2 * count * depth * units, 2 * count * depth + units * depth + count * units
        ),
        name="partial_sums",
    )(where, turned, *blocks, send, keep, *after)


def weight_kernel(places, n_row, c, where_ref, *refs):
    acts_refs, refs = refs[: len(places)], refs[len(places):]
    own_ref, grads_refs, out_ref, acts = refs[0], refs[1:3], refs[-2], refs[-1]
    me, row = where_ref[0], where_ref[1]
    core, tokens, count = me & 1, 2 * c, 2 * (n_row - 1) * c
    for (j0, j1), ref in zip(places, acts_refs):
        owner = me ^ jnp.where(core == 1, j1, j0)
        h = owner & 1
        slot = slot_of(row, owner, n_row) + jnp.where(h == core, n_row - 1, 0)
        for k in range(2):
            start = jnp.where(
                owner // 2 == row, 2 * count + h * tokens + k * c, k * count + slot * c
            )
            acts[pl.ds(pl.multiple_of(start, c), c), :] = ref[pl.ds(k * c, c), :]
    terms = [(0, grads_refs[0][...]), (count, grads_refs[1][...])]
    terms.append((2 * count, own_ref[...].reshape(2 * tokens, own_ref.shape[2])))
    total = None
    for start, rows in terms:
        term = lax.dot_general(
            acts[pl.ds(start, rows.shape[0]), :], rows,
            (((0,), (0,)), ((), ())), preferred_element_type=F32,
        )
        total = term if total is None else total + term
    out_ref[...] = total.astype(BF16)


def weight_rows(where, pieces, own, grads, before, shape, n_row, c, tile, first, count, after):
    places = [place for place, _ in pieces]
    rows, width = 2 * n_row * 2 * c, shape[1]
    in_specs = [pl.BlockSpec((a.shape[0], tile), lambda i, s: (0, first + i)) for _, a in pieces]
    in_specs += [once(own.shape, (0, 0, 0))] + [once(g.shape, (0, 0)) for g in grads]
    args = [a for _, a in pieces] + [own, *grads, *after]
    in_specs += [ANYWHERE] * len(after)
    aliases = {}
    if before is not None:
        in_specs.append(ANYWHERE)
        args.append(before)
        aliases = {len(args): 0}
    return pl.pallas_call(
        functools.partial(weight_kernel, places, n_row, c),
        out_shape=jax.ShapeDtypeStruct(shape, BF16),
        grid_spec=pltpu.PrefetchScalarGridSpec(
            num_scalar_prefetch=1,
            grid=(count,),
            in_specs=in_specs,
            out_specs=pl.BlockSpec((tile, width), lambda i, s: (first + i, 0)),
            scratch_shapes=[pltpu.VMEM((rows, tile), BF16)],
        ),
        input_output_aliases=aliases,
        compiler_params=PARAMS,
        cost_estimate=cost(
            2 * rows * width * count * tile, rows * width + (rows + width) * count * tile
        ),
        name="weight_rows",
    )(where, *args)


def sums_kernel(counts, table_ref, *refs):
    at = 0
    for job, count in enumerate(counts):
        total = refs[at][...].astype(F32)
        for ref in refs[at + 1 : at + count]:
            total = total + ref[...].astype(F32)
        out_ref = refs[job - len(counts)]
        out_ref[...] = total.astype(BF16).reshape(out_ref.shape)
        at += count


def sums(table, going, ended, at, shape, before, after):
    parts = going + ended
    jobs = [part.job() for part in parts]
    steps = max(2, *(size for _, size in jobs)) if len(jobs) > 1 else max(2, jobs[0][1])
    in_specs, args, out_specs, out_shape, values = [], [], [], [], 0
    for part, (terms, size) in zip(parts, jobs):
        c, cuts = part.c, steps // size
        if c % (16 * cuts):
            cuts = 1
        block = (1, c // cuts, part.width)

        def index(i, table, first=0, by_slot=False, size=size, cuts=cuts):
            at = first + i * size // steps
            return (table[at] if by_slot else at, lax.rem(i, cuts), 0)

        for array, first, by_slot in terms:
            in_specs.append(
                pl.BlockSpec(block, functools.partial(index, first=first, by_slot=by_slot))
            )
            args.append(array)
        values += (len(terms) + 1) * size * c * part.width
        if part in going:
            out_specs.append(pl.BlockSpec(block, index))
            out_shape.append(jax.ShapeDtypeStruct((size, c, part.width), BF16))
        else:
            out_specs.append(
                pl.BlockSpec(
                    block[1:],
                    lambda i, table, h=block[1], cuts=cuts: (at // h + lax.rem(i, cuts), 0),
                )
            )
            out_shape.append(jax.ShapeDtypeStruct(shape, BF16))
    args += after
    in_specs += [ANYWHERE] * len(after)
    aliases = {}
    if ended and before is not None:
        args.append(before)
        in_specs.append(ANYWHERE)
        aliases = {len(args): len(going)}
    outs = pl.pallas_call(
        functools.partial(sums_kernel, [len(terms) for terms, _ in jobs]),
        out_shape=out_shape,
        grid_spec=pltpu.PrefetchScalarGridSpec(
            num_scalar_prefetch=1, grid=(steps,), in_specs=in_specs, out_specs=out_specs,
        ),
        input_output_aliases=aliases,
        compiler_params=PARAMS,
        cost_estimate=cost(values, values),
        name="sums",
    )(table, *args)
    for part, out in zip(going, outs):
        part.take(out)
    return outs[-1] if ended else before, [outs[0]]


class Halving:
    def __init__(self, send, keep, levels, n):
        self.levels, self.n = list(levels), n
        self.half, self.c, self.width = keep.shape
        received = flip(send, self.levels.pop(0), n)
        self.terms = [[keep, 0, True], [received, 0, True]]

    def take(self, out):
        self.terms.append([flip(out, self.levels.pop(0), self.n), 0, False])

    def job(self):
        size = self.half = self.half // 2 if self.levels else 1
        job = ([tuple(term) for term in self.terms], size)
        self.terms = [[array, first + size, by_slot] for array, first, by_slot in self.terms]
        return job


def hold_kernel(*refs):
    refs[-1][...] = jnp.zeros_like(refs[-1])


def hold(after):
    return pl.pallas_call(
        hold_kernel,
        out_shape=jax.ShapeDtypeStruct((8, 128), F32),
        grid=(1,),
        in_specs=[ANYWHERE] * len(after),
        out_specs=pl.BlockSpec((8, 128), lambda i: (0, 0)),
        compiler_params=PARAMS,
        cost_estimate=cost(50 * 10**9, 8 * 128),
        name="hold",
    )(*after)


def per_device(n_row, n_col, hidden_acts, out_grad, down_weight):
    tokens, units = hidden_acts.shape
    features = out_grad.shape[1]
    assert n_col == 2 * n_row and tokens % 32 == 0
    further = [1 << b for b in range(1, n_col.bit_length() - 1)]
    levels = [(1, 1), *zip(further, further[::-1])]
    kept = [halving_order([bits[h] for bits in levels[1:]]) for h in (0, 1)]
    c = tokens // 2
    tile = 128 * max(d for d in (1, 2, 4) if units % (128 * d) == 0)
    tiles = units // tile
    col, row = (lax.axis_index(axis).astype(jnp.int32) for axis in ("col", "row"))
    where = jnp.stack([col, row])
    order = jnp.where(col & 1, jnp.array(kept[1], jnp.int32), jnp.array(kept[0], jnp.int32))
    table = slot_of(row, col ^ order, n_row)

    own = out_grad.reshape(2, tokens, features)
    half = n_row // 2
    chunks = [own[:, :c], own[:, c:]]
    middle = [near_shift(chunks[0], half, n_row), None]
    others = {s: near_shift(own, s, n_row) for s in range(1, n_row) if s != half}

    whole = {bit: flip(hidden_acts, (bit, bit), n_col) for bit in further}

    turned, send0, keep0, send1, keep1 = turn_weights(where, own, down_weight, c, n_row, tile)
    middle[0], turned, chunks[1], arrived = lax.optimization_barrier(
        (middle[0], turned, chunks[1], list(whole.values()))
    )
    whole = dict(zip(whole, arrived))
    far0 = [far_shift(middle[0], e, n_row) for e in range(1, half)]
    middle[1] = near_shift(chunks[1], half, n_row)

    def near(k):
        return [middle[k] if s == half else others[s] for s in range(1, n_row)]

    corners = []
    for t, bits in enumerate(levels[1:]):
        passed = [((j0 ^ bits[0], j1 ^ bits[1]), flip(a, bits, n_col)) for (j0, j1), a in corners]
        corners = corners + passed
        if t < len(further) - 1:
            corners.append((bits, jnp.where(col & 1, whole[bits[1]], whole[bits[0]])))
    corners = [((j0, j1), a) for (j0, j1), a in corners if j0 not in whole]

    send0, keep0, grads0 = partial_sums(
        where, turned, near(0), far0, send0, keep0, 0, list(whole.values())
    )
    zero = Halving(send0, keep0, levels, n_col)

    middle[1], tied = lax.optimization_barrier((middle[1], send0))
    far1 = [far_shift(middle[1], e, n_row) for e in range(1, half)]
    pieces = [((0, 0), hidden_acts)] + [((j, j), a) for j, a in whole.items()] + corners
    pieces += [((j1 ^ 1, j0 ^ 1), flip(a, (1, 1), n_col)) for (j0, j1), a in pieces]
    exchanged = [a for _, a in pieces[n_col // 2 :]]

    hidden_grad, weight_grad, done = None, None, 0

    def advance(going, ended, at, after):
        nonlocal hidden_grad
        hidden_grad, after = sums(table, going, ended, at, (tokens, units), hidden_grad, after)
        return after

    def work(count, after):
        nonlocal weight_grad, done
        count = min(tiles - done, count)
        if count:
            weight_grad = weight_rows(
                where, pieces, own, [grads0, grads1], weight_grad, (units, features), n_row, c,
                tile, done, count, after,
            )
            done += count
        return [weight_grad]

    after = [hold([tied, middle[1]] + [a for _, a in corners])]
    after = advance([zero], [], 0, after)
    send1, keep1, grads1 = partial_sums(
        where, turned, near(1), far1, send1, keep1, 1, after + exchanged[:1]
    )
    one = Halving(send1, keep1, levels, n_col)
    after = work(3, [send1])
    parts, steps = [zero, one], len(levels) - 1
    for step in range(steps):
        going, ended = [p for p in parts if p.levels], [p for p in parts if not p.levels]
        after = advance(going, ended, 0, after)
        parts = going
        after = work(-(-(tiles - done) * 3 // (5 * (steps - step) - 4 if step < steps - 1 else 3)), after)
    advance([], [one], c, after)
    return weight_grad, hidden_grad


def solution(mesh):
    in_specs = (P("col", "row"), P("row", "col"), P("row", "col"))
    out_specs = (P("row", "col"), P("col", "row"))
    return jax.shard_map(
        functools.partial(per_device, mesh.shape["row"], mesh.shape["col"]),
        mesh=mesh, in_specs=in_specs, out_specs=out_specs, check_vma=False,
    )
```

time: 279 us -> 232 us (0.83)
  waiting for transfers between devices: 191 us -> 43.6 us
  Pallas kernels: 0 us -> 143 us
  matrix products: 73.4 us -> 0 us
  starting transfers between devices: 0.11 us -> 28.7 us
  between operations: 13.7 us -> 0.79 us
  local copies, waits for them, and re-layouts: 0 us -> 11 us
    pallas_call x0 -> x11, Pallas kernels: none -> 143 us  [the longest x3 54.3 us: weight_rows(): pl.pallas_call(functools.partial(weight_kernel, places, n_row, c), out_sh...]
    all_gather x2 -> x0, waiting for transfers between devices: 124 us -> none  [the longest x1 84.4 us: per_device(): grad_full = lax.all_gather(out_grad, 'row', axis=0, tiled=True)]
    dot_general x2 -> x0, matrix products: 73.4 us -> none  [the longest x1 37.5 us: per_device(): lax.dot_general(grad_full, down_weight, (((1,), (1,)), ((), ())), preferr...]
    reduce_scatter x1 -> x0, waiting for transfers between devices: 66.2 us -> none  [per_device(): lax.psum_scatter(partial_grad.astype(jnp.bfloat16), 'col', scatter_dimens...]
    ppermute x0 -> x19, waiting for transfers between devices: none -> 43.6 us  [the longest x13 23.4 us: flip(): return lax.ppermute(x, 'col', [(i, i ^ bits[i & 1]) for i in range(n)])]
    ppermute x0 -> x19, starting transfers between devices: none -> 28.7 us  [the longest x4 15.3 us: near_shift(): lax.ppermute(x, 'row', [(i, j) for i, j in pairs if abs(i - j) <= n // 2])]
    unnamed x0 -> x34, local copies, waits for them, and re-layouts: none -> 8.69 us
  transfers between devices with their start and end apart: 3 -> 19, of which waited for: 3 -> 8; matrix products, arithmetic and copies ran while one was open for 26% -> 2% of each run, Pallas kernels for 0% -> 47%
where the time goes in v3:
time: 232 us; the launch traced here: 230 us
  Pallas kernels  143 us (62%)
  waiting for transfers between devices  43.6 us (19%)
  starting transfers between devices  28.7 us (12%)
  local copies, waits for them, and re-layouts  11 us (5%)
  other arithmetic  2.67 us (1%)
    pallas_call x3, Pallas kernels, weight_rows(): pl.pallas_call(functools.partial(weight_kernel, places, n_row, c), out_sh...  54.3 us
    pallas_call x2, Pallas kernels, partial_sums(): pl.pallas_call(functools.partial(partial_kernel, n_row, c), out_shape=(pa...  43.2 us
    pallas_call x1, Pallas kernels, turn_weights(): pl.pallas_call(functools.partial(turn_kernel, c), out_shape=(jax.ShapeDty...  28.3 us
    ppermute x13, waiting for transfers between devices, flip(): return lax.ppermute(x, 'col', [(i, i ^ bits[i & 1]) for i in range(n)])  23.4 us
    pallas_call x4, Pallas kernels, sums(): pl.pallas_call(functools.partial(sums_kernel, [len(terms) for terms, _ in...  16.6 us
    ppermute x4, starting transfers between devices, near_shift(): lax.ppermute(x, 'row', [(i, j) for i, j in pairs if abs(i - j) <= n // 2])  15.3 us
    ppermute x2, waiting for transfers between devices, far_shift(): return lax.ppermute(x, 'row', up + down)  10.8 us
    ppermute x13, starting transfers between devices, flip(): return lax.ppermute(x, 'col', [(i, i ^ bits[i & 1]) for i in range(n)])  10.7 us
  transfers between devices with their start and end apart: 19, of which 8 were waited for; matrix products, arithmetic and copies ran while one was open for 2% of the time, Pallas kernels for 47%

profile of v3, /device:TPU:0, one launch (start us, length us, event | category | flops | bytes accessed | tf_op | source)
XLA Modules:
  0.0 229.6 jit_solution(10542063221362416609)
XLA Ops:
  0.6 3.0 %collective-permute-start.2 = (bf16[128,6656]{1,0:T(8,128)(2,1)}, bf16[128,6656]{1,0:T(8,128)(2,1)S(1)}, u32[]{:S(2)}, u32[]{:S(2)}) collective-permute-start(bf16[128,6656]{1,0:T(8,128)(2,1)} %refs_0_.5), channel_id=1, source_target_pairs={{0,4},{1,5},{2,6},{3,7},{4,0},{5,1},{6,2},{7,3},{8,12},{9,13},{10,... | collective-permute-start | bytes 5111816 | tf_op jit(solution)/shard_map/ppermute | solution.py:31
  3.7 1.5 collective-permute-start.1
  5.2 1.3 collective-permute-start.9
  6.4 5.6 %collective-permute-start.8 = (bf16[2,128,2048]{2,1,0:T(8,128)(2,1)}, bf16[2,128,2048]{2,1,0:T(8,128)(2,1)}, u32[]{:S(2)}, u32[]{:S(2)}) collective-permute-start(bf16[2,128,2048]{2,1,0:T(8,128)(2,1)} %bitcast.4), channel_id=1, source_target_pairs={{0,8},{8,16},{16,24},{1,9},{9,17},{17,25},{2,10},{10,18},{18,26},{... | collective-permute-start | bytes 3145736 | tf_op jit(solution)/shard_map/ppermute | solution.py:36
  12.1 2.3 fusion.2
  14.3 2.6 %collective-permute-start = (bf16[2,64,2048]{2,1,0:T(8,128)(2,1)}, bf16[2,64,2048]{2,1,0:T(8,128)(2,1)}, u32[]{:S(2)}, u32[]{:S(2)}) collective-permute-start(bf16[2,64,2048]{2,1,0:T(8,128)(2,1)} %get-tuple-element.47), channel_id=1, source_target_pairs={{0,16},{8,24},{16,0},{24,8},{1,17},{9,25},{17,1},{25,9},{2,18},{10... | collective-permute-start | bytes 1572872 | tf_op jit(solution)/shard_map/ppermute | solution.py:36
  16.9 0.6 pad_add_fusion.where_ref
  17.5 28.3 %turn_weights.1 = (bf16[13,2048,512]{2,1,0:T(8,128)(2,1)}, bf16[4,64,6656]{2,1,0:T(8,128)(2,1)}, bf16[4,64,6656]{2,1,0:T(8,128)(2,1)}, bf16[4,64,6656]{2,1,0:T(8,128)(2,1)}, bf16[4,64,6656]{2,1,0:T(8,128)(2,1)}) custom-call(s32[2]{0:T(128)} %pad_add_fusion.where_ref, bf16[2,128,2048]{2,1,0:T(8,128)(2,1)} %bitcast.6, bf16[6656,2048]{1,0:T(8,128)(2,1)} %w_ref.1), custom_call_target="tpu_custom_call" | custom-call | flops 6979321856 | bytes 57933824 | tf_op jit(solution)/shard_map/turn_weights/pallas_call | solution.py:72
  45.8 9.4 %collective-permute-done.refs_1_ = bf16[2,64,2048]{2,1,0:T(8,128)(2,1)} collective-permute-done((bf16[2,64,2048]{2,1,0:T(8,128)(2,1)}, bf16[2,64,2048]{2,1,0:T(8,128)(2,1)}, u32[]{:S(2)}, u32[]{:S(2)}) %collective-permute-start) | collective-permute-done | bytes 524320 | tf_op jit(solution)/shard_map/ppermute | solution.py:36
  55.2 1.5 broadcast_select_fusion
  56.7 0.2 copy-done
  56.9 0.6 copy-done.2
  57.5 0.5 collective-permute-start.3
  58.0 1.3 collective-permute-start.10
  59.3 0.1 collective-permute-start.4
  59.4 0.6 compare_select_fusion.table_ref
  60.0 5.8 %collective-permute-start.11 = (bf16[2,64,2048]{2,1,0:T(8,128)(2,1)}, bf16[2,64,2048]{2,1,0:T(8,128)(2,1)S(1)}, u32[]{:S(2)}, u32[]{:S(2)}) collective-permute-start(bf16[2,64,2048]{2,1,0:T(8,128)(2,1)} %get-tuple-element.32), channel_id=1, source_target_pairs={{0,16},{8,24},{16,0},{24,8},{1,17},{9,25},{17,1},{25,9},{2,18},{10... | collective-permute-start | bytes 1572872 | tf_op jit(solution)/shard_map/ppermute | solution.py:36
  65.7 6.3 %collective-permute-done.10.refs_3_ = bf16[2,64,2048]{2,1,0:T(8,128)(2,1)S(1)} collective-permute-done((bf16[2,64,2048]{2,1,0:T(8,128)(2,1)}, bf16[2,64,2048]{2,1,0:T(8,128)(2,1)S(1)}, u32[]{:S(2)}, u32[]{:S(2)}) %collective-permute-start.10) | collective-permute-done | bytes 524320 | tf_op jit(solution)/shard_map/ppermute | solution.py:43
  72.1 0.8 copy-done.13
  72.9 21.4 %partial_sums.2 = (bf16[4,64,6656]{2,1,0:T(8,128)(2,1)}, bf16[4,64,6656]{2,1,0:T(8,128)(2,1)}, bf16[384,2048]{1,0:T(8,128)(2,1)}) custom-call(s32[2]{0:T(128)} %pad_add_fusion.where_ref, bf16[13,2048,512]{2,1,0:T(8,128)(2,1)} %get-tuple-element.27.w_ref, ...), custom_call_target="tpu_custom_call", output_to_operand_aliasing={{0}: (6, {}), {1}: (7, {})} | custom-call | flops 10468982784 | bytes 35520512 | tf_op jit(solution)/shard_map/partial_sums/pallas_call | solution.py:125
  94.3 1.5 collective-permute-start.12
  95.8 0.6 hold.1.refs_2_
  96.4 4.1 %collective-permute-done.13.refs_1_.refs_4_ = bf16[4,64,6656]{2,1,0:T(8,128)(2,1)S(1)} collective-permute-done((bf16[4,64,6656]{2,1,0:T(8,128)(2,1)}, bf16[4,64,6656]{2,1,0:T(8,128)(2,1)S(1)}, u32[]{:S(2)}, u32[]{:S(2)}) %collective-permute-start.13) | collective-permute-done | bytes 3407904 | tf_op jit(solution)/shard_map/ppermute | solution.py:31
  100.5 1.8 copy-done.4
  102.3 3.7 %sums.4.refs_6_ = bf16[2,64,6656]{2,1,0:T(8,128)(2,1)} custom-call(s32[4]{0:T(128)} %compare_select_fusion.table_ref, bf16[4,64,6656]{2,1,0:T(8,128)(2,1)} %get-tuple-element.37.refs_0_.refs_3_, bf16[4,64,6656]{2,1,0:T(8,128)(2,1)} %copy-done.4, f32[8,128]{1,0:T(8,128)} %hold.1.refs_2_), custom_call_target="tpu_custom_call" | custom-call | flops 2555904 | bytes 5111808 | tf_op jit(solution)/shard_map/sums/pallas_call | solution.py:251
  106.1 4.4 %collective-permute-done.12.refs_3_ = bf16[2,64,2048]{2,1,0:T(8,128)(2,1)S(1)} collective-permute-done((bf16[2,64,2048]{2,1,0:T(8,128)(2,1)S(1)}, bf16[2,64,2048]{2,1,0:T(8,128)(2,1)S(1)}, u32[]{:S(2)}, u32[]{:S(2)}) %collective-permute-start.12) | collective-permute-done | bytes 524320 | tf_op jit(solution)/shard_map/ppermute | solution.py:43
  110.5 0.8 copy-done.14
  111.3 21.8 %partial_sums.3 = (bf16[4,64,6656]{2,1,0:T(8,128)(2,1)}, bf16[4,64,6656]{2,1,0:T(8,128)(2,1)}, bf16[384,2048]{1,0:T(8,128)(2,1)}) custom-call(s32[2]{0:T(128)} %pad_add_fusion.where_ref, bf16[13,2048,512]{2,1,0:T(8,128)(2,1)} %get-tuple-element.27.w_ref, ...), custom_call_target="tpu_custom_call", output_to_operand_aliasing={{0}: (6, {}), {1}: (7, {})} | custom-call | flops 10468982784 | bytes 35520512 | tf_op jit(solution)/shard_map/partial_sums/pallas_call | solution.py:125
  133.1 0.5 collective-permute-start.5
  133.6 0.4 collective-permute-start.7
  134.1 1.5 collective-permute-start.15
  135.6 8.0 %collective-permute-done.5.refs_5_ = bf16[128,6656]{1,0:T(8,128)(2,1)S(1)} collective-permute-done((bf16[128,6656]{1,0:T(8,128)(2,1)S(1)}, bf16[128,6656]{1,0:T(8,128)(2,1)S(1)}, u32[]{:S(2)}, u32[]{:S(2)}) %collective-permute-start.5) | collective-permute-done | bytes 1703968 | tf_op jit(solution)/shard_map/ppermute | solution.py:31
  143.6 2.8 %collective-permute-done.6.refs_6_ = bf16[128,6656]{1,0:T(8,128)(2,1)S(1)} collective-permute-done((bf16[128,6656]{1,0:T(8,128)(2,1)S(1)}, bf16[128,6656]{1,0:T(8,128)(2,1)S(1)}, u32[]{:S(2)}, u32[]{:S(2)}) %collective-permute-start.6) | collective-permute-done | bytes 1703968 | tf_op jit(solution)/shard_map/ppermute | solution.py:31
  146.4 1.2 copy-done.7
  147.6 1.2 copy-done.8
  148.8 14.0 %weight_rows.3.refs_5_.refs_12_ = bf16[6656,2048]{1,0:T(8,128)(2,1)} custom-call(s32[2]{0:T(128)} %pad_add_fusion.where_ref, bf16[128,6656]{1,0:T(8,128)(2,1)} %refs_0_.5, bf16[128,6656]{1,0:T(8,128)(2,1)} %copy-done.2, bf16[128,6656]{1,0:T(8,128)(2,1)} %copy-done, bf16[128,6656]{1,0:T(8,128)(2,1)} %collective-permute-done.3.refs_2_.refs_3_, ...), custom_call_target="tpu_custom_call" | custom-call | flops 6442450944 | bytes 13631488 | tf_op jit(solution)/shard_map/weight_rows/pallas_call | solution.py:182
  162.8 4.7 %sums.5 = (bf16[1,64,6656]{2,1,0:T(8,128)(2,1)}, bf16[2,64,6656]{2,1,0:T(8,128)(2,1)}) custom-call(s32[4]{0:T(128)} %compare_select_fusion.table_ref, bf16[4,64,6656]{2,1,0:T(8,128)(2,1)} %get-tuple-element.37.refs_0_.refs_3_, bf16[4,64,6656]{2,1,0:T(8,128)(2,1)} %copy-done.4, bf16[2,64,6656]{2,1,0:T(8,128)(2,1)} %collective-permute-done.15.refs_2_.refs_5_, ...), custom_call_target="tpu_custom_call" | custom-call | flops 4259840 | bytes 8519680 | tf_op jit(solution)/shard_map/sums/pallas_call | solution.py:251
  167.5 1.5 collective-permute-start.16
  169.0 0.5 collective-permute-start.17
  169.5 20.2 %weight_rows.4.refs_7_.refs_12_ = bf16[6656,2048]{1,0:T(8,128)(2,1)} custom-call(s32[2]{0:T(128)} %pad_add_fusion.where_ref, bf16[128,6656]{1,0:T(8,128)(2,1)} %refs_0_.5, bf16[128,6656]{1,0:T(8,128)(2,1)} %copy-done.2, bf16[128,6656]{1,0:T(8,128)(2,1)} %copy-done, ...), custom_call_target="tpu_custom_call", output_to_operand_aliasing={{}: (13, {})} | custom-call | flops 10737418240 | bytes 19922944 | tf_op jit(solution)/shard_map/weight_rows/pallas_call | solution.py:182
  189.6 1.4 collective-permute-done.17.refs_6_
  191.1 7.0 %collective-permute-done.16.refs_2_ = bf16[2,64,6656]{2,1,0:T(8,128)(2,1)S(1)} collective-permute-done((bf16[2,64,6656]{2,1,0:T(8,128)(2,1)}, bf16[2,64,6656]{2,1,0:T(8,128)(2,1)S(1)}, u32[]{:S(2)}, u32[]{:S(2)}) %collective-permute-start.16) | collective-permute-done | bytes 1703968 | tf_op jit(solution)/shard_map/ppermute | solution.py:31
  198.0 1.2 copy-done.9
  199.3 4.6 %sums.6 = (bf16[1,64,6656]{2,1,0:T(8,128)(2,1)}, bf16[128,6656]{1,0:T(8,128)(2,1)}) custom-call(s32[4]{0:T(128)} %compare_select_fusion.table_ref, bf16[4,64,6656]{2,1,0:T(8,128)(2,1)} %get-tuple-element.40.refs_3_.refs_0_, bf16[4,64,6656]{2,1,0:T(8,128)(2,1)} %collective-permute-done.14.refs_4_.refs_1_, bf16[2,64,6656]{2,1,0:T(8,128)(2,1)} %copy-done.9, ...), custom_call_target="tpu_custom_call" | custom-call | flops 3833856 | bytes 7667712 | tf_op jit(solution)/shard_map/sums/pallas_call | solution.py:251
  203.9 1.1 collective-permute-start.18
  205.0 20.2 %weight_rows.5.refs_4_ = bf16[6656,2048]{1,0:T(8,128)(2,1)} custom-call(s32[2]{0:T(128)} %pad_add_fusion.where_ref, bf16[128,6656]{1,0:T(8,128)(2,1)} %refs_0_.5, bf16[128,6656]{1,0:T(8,128)(2,1)} %copy-done.2, bf16[128,6656]{1,0:T(8,128)(2,1)} %copy-done, bf16[128,6656]{1,0:T(8,128)(2,1)} %collective-permute-done.3.refs_2_.refs_3_, ...), custom_call_target="tpu_custom_call", output_to_operand_aliasing={{}: (13, {})} | custom-call | flops 10737418240 | bytes 19922944 | tf_op jit(solution)/shard_map/weight_rows/pallas_call | solution.py:182
  225.2 0.9 copy-done.10
  226.1 3.6 %sums.7 = bf16[128,6656]{1,0:T(8,128)(2,1)} custom-call(s32[4]{0:T(128)} %compare_select_fusion.table_ref, bf16[4,64,6656]{2,1,0:T(8,128)(2,1)} %get-tuple-element.40.refs_3_.refs_0_, bf16[4,64,6656]{2,1,0:T(8,128)(2,1)} %collective-permute-done.14.refs_4_.refs_1_, bf16[2,64,6656]{2,1,0:T(8,128)(2,1)} %copy-done.9, ...), custom_call_target="tpu_custom_call", output_to_operand_aliasing={{}: (6, {})} | custom-call | flops 2129920 | bytes 4259840 | tf_op jit(solution)/shard_map/sums/pallas_call | solution.py:251
  (39 shorter events, 0.2 us)
Async XLA Ops:
  0.6 54.5 %collective-permute-start.2 = (bf16[128,6656]{1,0:T(8,128)(2,1)}, bf16[128,6656]{1,0:T(8,128)(2,1)S(1)}, u32[]{:S(2)}, u32[]{:S(2)}) collective-permute-start(bf16[128,6656]{1,0:T(8,128)(2,1)} %refs_0_.5), channel_id=1, source_target_pairs={{0,4},{1,5},{2,6},{3,7},{4,0},{5,1},{6,2},{7,3},{8,12},{9,13},{10,... | collective-permute-start | bytes 5111816 | tf_op jit(solution)/shard_map/ppermute | solution.py:31
  3.7 51.5 %collective-permute-start.1 = (bf16[128,6656]{1,0:T(8,128)(2,1)}, bf16[128,6656]{1,0:T(8,128)(2,1)S(1)}, u32[]{:S(2)}, u32[]{:S(2)}) collective-permute-start(bf16[128,6656]{1,0:T(8,128)(2,1)} %refs_0_.5), channel_id=1, source_target_pairs={{0,2},{1,3},{2,0},{3,1},{4,6},{5,7},{6,4},{7,5},{8,10},{9,11},{10,... | collective-permute-start | bytes 5111816 | tf_op jit(solution)/shard_map/ppermute | solution.py:31
  5.2 54.8 %collective-permute-start.9 = (bf16[2,128,2048]{2,1,0:T(8,128)(2,1)}, bf16[2,128,2048]{2,1,0:T(8,128)(2,1)}, u32[]{:S(2)}, u32[]{:S(2)}) collective-permute-start(bf16[2,128,2048]{2,1,0:T(8,128)(2,1)} %bitcast.3), channel_id=1, source_target_pairs={{8,0},{16,8},{24,16},{9,1},{17,9},{25,17},{10,2},{18,10},{26,18},{... | collective-permute-start | bytes 3145736 | tf_op jit(solution)/shard_map/ppermute | solution.py:36
  6.4 59.3 %collective-permute-start.8 = (bf16[2,128,2048]{2,1,0:T(8,128)(2,1)}, bf16[2,128,2048]{2,1,0:T(8,128)(2,1)}, u32[]{:S(2)}, u32[]{:S(2)}) collective-permute-start(bf16[2,128,2048]{2,1,0:T(8,128)(2,1)} %bitcast.4), channel_id=1, source_target_pairs={{0,8},{8,16},{16,24},{1,9},{9,17},{17,25},{2,10},{10,18},{18,26},{... | collective-permute-start | bytes 3145736 | tf_op jit(solution)/shard_map/ppermute | solution.py:36
  14.3 40.8 %collective-permute-start = (bf16[2,64,2048]{2,1,0:T(8,128)(2,1)}, bf16[2,64,2048]{2,1,0:T(8,128)(2,1)}, u32[]{:S(2)}, u32[]{:S(2)}) collective-permute-start(bf16[2,64,2048]{2,1,0:T(8,128)(2,1)} %get-tuple-element.47), channel_id=1, source_target_pairs={{0,16},{8,24},{16,0},{24,8},{1,17},{9,25},{17,1},{25,9},{2,18},{10... | collective-permute-start | bytes 1572872 | tf_op jit(solution)/shard_map/ppermute | solution.py:36
  55.2 1.7 copy-start
  55.2 2.3 copy-start.2
  55.2 4.2 %copy-start.15 = (s32[4]{0:T(128)S(1)}, s32[4]{0:T(128)}, u32[]{:S(2)}) copy-start(s32[4]{0:T(128)} %constant.39.clone) | copy-start | bytes 52
  55.2 4.1 %copy-start.16 = (s32[4]{0:T(128)S(1)}, s32[4]{0:T(128)}, u32[]{:S(2)}) copy-start(s32[4]{0:T(128)} %constant.38.clone) | copy-start | bytes 52
  57.5 38.3 %collective-permute-start.3 = (bf16[128,6656]{1,0:T(8,128)(2,1)}, bf16[128,6656]{1,0:T(8,128)(2,1)}, u32[]{:S(2)}, u32[]{:S(2)}) collective-permute-start(bf16[128,6656]{1,0:T(8,128)(2,1)} %broadcast_select_fusion), channel_id=1, source_target_pairs={{0,4},{1,3},{2,6},{3,1},{4,0},{5,7},{6,2},{7,5},{8,12},{9,11},{10,... | collective-permute-start | bytes 5111816 | tf_op jit(solution)/shard_map/ppermute | solution.py:31
  58.0 14.1 %collective-permute-start.10 = (bf16[2,64,2048]{2,1,0:T(8,128)(2,1)}, bf16[2,64,2048]{2,1,0:T(8,128)(2,1)S(1)}, u32[]{:S(2)}, u32[]{:S(2)}) collective-permute-start(bf16[2,64,2048]{2,1,0:T(8,128)(2,1)} %collective-permute-done.refs_1_), channel_id=1, source_target_pairs={{16,24},{8,0},{17,25},{9,1},{18,26},{10,2},{19,27},{11,3},{20,28},... | collective-permute-start | bytes 1572872 | tf_op jit(solution)/shard_map/ppermute | solution.py:43
  59.3 46.8 %collective-permute-start.4 = (bf16[128,6656]{1,0:T(8,128)(2,1)}, bf16[128,6656]{1,0:T(8,128)(2,1)S(1)}, u32[]{:S(2)}, u32[]{:S(2)}) collective-permute-start(bf16[128,6656]{1,0:T(8,128)(2,1)} %refs_0_.5), channel_id=1, source_target_pairs={{0,1},{1,0},{2,3},{3,2},{4,5},{5,4},{6,7},{7,6},{8,9},{9,8},{10,11... | collective-permute-start | bytes 5111816 | tf_op jit(solution)/shard_map/ppermute | solution.py:31
  60.0 34.3 %collective-permute-start.11 = (bf16[2,64,2048]{2,1,0:T(8,128)(2,1)}, bf16[2,64,2048]{2,1,0:T(8,128)(2,1)S(1)}, u32[]{:S(2)}, u32[]{:S(2)}) collective-permute-start(bf16[2,64,2048]{2,1,0:T(8,128)(2,1)} %get-tuple-element.32), channel_id=1, source_target_pairs={{0,16},{8,24},{16,0},{24,8},{1,17},{9,25},{17,1},{25,9},{2,18},{10... | collective-permute-start | bytes 1572872 | tf_op jit(solution)/shard_map/ppermute | solution.py:36
  72.1 0.8 copy-start.13
  94.3 6.2 %collective-permute-start.13 = (bf16[4,64,6656]{2,1,0:T(8,128)(2,1)}, bf16[4,64,6656]{2,1,0:T(8,128)(2,1)S(1)}, u32[]{:S(2)}, u32[]{:S(2)}) collective-permute-start(bf16[4,64,6656]{2,1,0:T(8,128)(2,1)} %get-tuple-element.38.refs_0_), channel_id=1, source_target_pairs={{0,1},{1,0},{2,3},{3,2},{4,5},{5,4},{6,7},{7,6},{8,9},{9,8},{10,11... | collective-permute-start | bytes 10223624 | tf_op jit(solution)/shard_map/ppermute | solution.py:31
  94.3 1.5 copy-start.12
  94.3 16.2 %collective-permute-start.12 = (bf16[2,64,2048]{2,1,0:T(8,128)(2,1)S(1)}, bf16[2,64,2048]{2,1,0:T(8,128)(2,1)S(1)}, u32[]{:S(2)}, u32[]{:S(2)}) collective-permute-start(bf16[2,64,2048]{2,1,0:T(8,128)(2,1)S(1)} %collective-permute-done.11.refs_1_), channel_id=1, source_target_pairs={{16,24},{8,0},{17,25},{9,1},{18,26},{10,2},{19,27},{11,3},{20,28},... | collective-permute-start | bytes 1572872 | tf_op jit(solution)/shard_map/ppermute | solution.py:43
  100.5 1.8 copy-start.4
  106.1 4.4 %copy-start.5 = (bf16[128,6656]{1,0:T(8,128)(2,1)}, bf16[128,6656]{1,0:T(8,128)(2,1)S(1)}, u32[]{:S(2)}) copy-start(bf16[128,6656]{1,0:T(8,128)(2,1)S(1)} %collective-permute-done.4.refs_7_.refs_4_) | copy-start | bytes 5111812
  110.5 0.8 copy-start.14
  111.3 21.8 %copy-start.3 = (bf16[128,6656]{1,0:T(8,128)(2,1)S(1)}, bf16[128,6656]{1,0:T(8,128)(2,1)}, u32[]{:S(2)}) copy-start(bf16[128,6656]{1,0:T(8,128)(2,1)} %copy-done.2) | copy-start | bytes 5111812
  111.3 22.3 %copy-start.1 = (bf16[128,6656]{1,0:T(8,128)(2,1)S(1)}, bf16[128,6656]{1,0:T(8,128)(2,1)}, u32[]{:S(2)}) copy-start(bf16[128,6656]{1,0:T(8,128)(2,1)} %copy-done) | copy-start | bytes 5111812
  133.1 29.7 %collective-permute-start.14 = (bf16[4,64,6656]{2,1,0:T(8,128)(2,1)}, bf16[4,64,6656]{2,1,0:T(8,128)(2,1)}, u32[]{:S(2)}, u32[]{:S(2)}) collective-permute-start(bf16[4,64,6656]{2,1,0:T(8,128)(2,1)} %get-tuple-element.41.refs_11_), channel_id=1, source_target_pairs={{0,1},{1,0},{2,3},{3,2},{4,5},{5,4},{6,7},{7,6},{8,9},{9,8},{10,11... | collective-permute-start | bytes 10223624 | tf_op jit(solution)/shard_map/ppermute | solution.py:31
  133.1 10.5 %collective-permute-start.5 = (bf16[128,6656]{1,0:T(8,128)(2,1)S(1)}, bf16[128,6656]{1,0:T(8,128)(2,1)S(1)}, u32[]{:S(2)}, u32[]{:S(2)}) collective-permute-start(bf16[128,6656]{1,0:T(8,128)(2,1)S(1)} %copy-done.3), channel_id=1, source_target_pairs={{0,1},{1,0},{2,3},{3,2},{4,5},{5,4},{6,7},{7,6},{8,9},{9,8},{10,11... | collective-permute-start | bytes 5111816 | tf_op jit(solution)/shard_map/ppermute | solution.py:31
  133.6 12.8 %collective-permute-start.6 = (bf16[128,6656]{1,0:T(8,128)(2,1)S(1)}, bf16[128,6656]{1,0:T(8,128)(2,1)S(1)}, u32[]{:S(2)}, u32[]{:S(2)}) collective-permute-start(bf16[128,6656]{1,0:T(8,128)(2,1)S(1)} %copy-done.1), channel_id=1, source_target_pairs={{0,1},{1,0},{2,3},{3,2},{4,5},{5,4},{6,7},{7,6},{8,9},{9,8},{10,11... | collective-permute-start | bytes 5111816 | tf_op jit(solution)/shard_map/ppermute | solution.py:31
  133.6 14.0 %collective-permute-start.7 = (bf16[128,6656]{1,0:T(8,128)(2,1)}, bf16[128,6656]{1,0:T(8,128)(2,1)S(1)}, u32[]{:S(2)}, u32[]{:S(2)}) collective-permute-start(bf16[128,6656]{1,0:T(8,128)(2,1)} %collective-permute-done.3.refs_2_.refs_3_), channel_id=1, source_target_pairs={{0,1},{1,0},{2,3},{3,2},{4,5},{5,4},{6,7},{7,6},{8,9},{9,8},{10,11... | collective-permute-start | bytes 5111816 | tf_op jit(solution)/shard_map/ppermute | solution.py:31
  134.1 28.7 %collective-permute-start.15 = (bf16[2,64,6656]{2,1,0:T(8,128)(2,1)}, bf16[2,64,6656]{2,1,0:T(8,128)(2,1)}, u32[]{:S(2)}, u32[]{:S(2)}) collective-permute-start(bf16[2,64,6656]{2,1,0:T(8,128)(2,1)} %sums.4.refs_6_), channel_id=1, source_target_pairs={{0,2},{1,5},{2,0},{3,7},{4,6},{5,1},{6,4},{7,3},{8,10},{9,13},{10,... | collective-permute-start | bytes 5111816 | tf_op jit(solution)/shard_map/ppermute | solution.py:31
  143.6 5.2 %copy-start.6 = (bf16[128,6656]{1,0:T(8,128)(2,1)}, bf16[128,6656]{1,0:T(8,128)(2,1)S(1)}, u32[]{:S(2)}) copy-start(bf16[128,6656]{1,0:T(8,128)(2,1)S(1)} %collective-permute-done.5.refs_5_) | copy-start | bytes 5111812
  146.4 1.2 copy-start.7
  147.6 1.2 copy-start.8
  167.5 30.6 %collective-permute-start.16 = (bf16[2,64,6656]{2,1,0:T(8,128)(2,1)}, bf16[2,64,6656]{2,1,0:T(8,128)(2,1)S(1)}, u32[]{:S(2)}, u32[]{:S(2)}) collective-permute-start(bf16[2,64,6656]{2,1,0:T(8,128)(2,1)} %get-tuple-element.42), channel_id=1, source_target_pairs={{0,2},{1,5},{2,0},{3,7},{4,6},{5,1},{6,4},{7,3},{8,10},{9,13},{10,... | collective-permute-start | bytes 5111816 | tf_op jit(solution)/shard_map/ppermute | solution.py:31
  169.0 22.1 %collective-permute-start.17 = (bf16[1,64,6656]{2,1,0:T(8,128)(2,1)}, bf16[1,64,6656]{2,1,0:T(8,128)(2,1)S(1)}, u32[]{:S(2)}, u32[]{:S(2)}) collective-permute-start(bf16[1,64,6656]{2,1,0:T(8,128)(2,1)} %get-tuple-element.43.refs_11_), channel_id=1, source_target_pairs={{0,4},{1,3},{2,6},{3,1},{4,0},{5,7},{6,2},{7,5},{8,12},{9,11},{10,... | collective-permute-start | bytes 2555912 | tf_op jit(solution)/shard_map/ppermute | solution.py:31
  191.1 7.0 %copy-start.11 = (bf16[1,64,6656]{2,1,0:T(8,128)(2,1)}, bf16[1,64,6656]{2,1,0:T(8,128)(2,1)S(1)}, u32[]{:S(2)}) copy-start(bf16[1,64,6656]{2,1,0:T(8,128)(2,1)S(1)} %collective-permute-done.17.refs_6_) | copy-start | bytes 2555908
  198.0 1.2 copy-start.9
  203.9 21.3 %collective-permute-start.18 = (bf16[1,64,6656]{2,1,0:T(8,128)(2,1)}, bf16[1,64,6656]{2,1,0:T(8,128)(2,1)S(1)}, u32[]{:S(2)}, u32[]{:S(2)}) collective-permute-start(bf16[1,64,6656]{2,1,0:T(8,128)(2,1)} %get-tuple-element.44.refs_11_), channel_id=1, source_target_pairs={{0,4},{1,3},{2,6},{3,1},{4,0},{5,7},{6,2},{7,5},{8,12},{9,11},{10,... | collective-permute-start | bytes 2555912 | tf_op jit(solution)/shard_map/ppermute | solution.py:31
  225.1 0.9 copy-start.10

commit v4 on v3

--- a/solution.py
+++ b/solution.py
@@ -9,6 +9,7 @@
 
 F32, BF16 = jnp.float32, jnp.bfloat16
 ANYWHERE = pl.BlockSpec(memory_space=pl.ANY)
+CUTS = 4
 PARAMS = pltpu.CompilerParams(vmem_limit_bytes=58 * 1024 * 1024)
 
 
@@ -31,24 +32,16 @@
     return lax.ppermute(x, "col", [(i, i ^ bits[i & 1]) for i in range(n)])
 
 
-def near_shift(x, s, n):
-    pairs = [(i, (i + s) % n) for i in range(n)]
-    return lax.ppermute(x, "row", [(i, j) for i, j in pairs if abs(i - j) <= n // 2])
-
-
-def far_shift(x, e, n):
-    half = n // 2
-    up = [(i, i + e) for i in range(half, n - e)]
-    down = [(i, i - e) for i in range(e, half)]
-    return lax.ppermute(x, "row", up + down)
+def shift(x, s, n):
+    return lax.ppermute(x, "row", [(i, (i + s) % n) for i in range(n)])
 
 
 def slot_of(row, owner, n_row):
     return lax.rem(row - owner // 2 - 1 + n_row, n_row)
 
 
-def turn_kernel(c, where_ref, own_ref, w_ref, turned_ref, *refs):
-    outs, mine = refs[:-1], refs[-1]
+def turn_kernel(c, where_ref, own_ref, *refs):
+    w_refs, turned_ref, outs, mine = refs[:CUTS], refs[CUTS], refs[CUTS + 1 : -1], refs[-1]
     core = where_ref[0] & 1
 
     @pl.when(pl.program_id(0) == 0)
@@ -57,9 +50,14 @@
             h = core if p % 2 else 1 - core
             mine[pl.ds(p * c, c), :] = own_ref[h, pl.ds(p // 2 * c, c), :]
 
-    turned = w_ref[...].T
-    turned_ref[0] = turned
-    res = jnp.dot(mine[...], turned, preferred_element_type=F32).astype(BF16)
+    res, width = None, mine.shape[1] // CUTS
+    for q, w_ref in enumerate(w_refs):
+        columns = pl.ds(q * width, width)
+        turned = w_ref[...].T
+        turned_ref[0, columns, :] = turned
+        term = jnp.dot(mine[:, columns], turned, preferred_element_type=F32)
+        res = term if res is None else res + term
+    res = res.astype(BF16)
     for p, ref in enumerate(outs):
         ref[0] = res[p * c : (p + 1) * c]
 
@@ -75,50 +73,52 @@
         grid_spec=pltpu.PrefetchScalarGridSpec(
             num_scalar_prefetch=1,
             grid=(tiles,),
-            in_specs=[once(own.shape, (0, 0, 0)), pl.BlockSpec((tile, depth), lambda i, s: (i, 0))],
+            in_specs=[once(own.shape, (0, 0, 0))]
+            + [pl.BlockSpec((tile, depth // CUTS), lambda i, s, q=q: (i, q)) for q in range(CUTS)],
             out_specs=(pl.BlockSpec((1, depth, tile), lambda i, s: (i, 0, 0)),) + (part_spec,) * 4,
             scratch_shapes=[pltpu.VMEM((4 * c, depth), BF16)],
         ),
         compiler_params=PARAMS,
         cost_estimate=cost(8 * c * depth * units, 2 * units * depth + 4 * c * units),
         name="turn_weights",
-    )(where, own, weight)
-
-
-def partial_kernel(n_row, c, where_ref, w_ref, *refs):
-    half = n_row // 2
-    near, far = refs[: n_row - 1], refs[n_row - 1 : n_row + half - 2]
+    )(where, own, *[weight] * CUTS)
+
+
+def partial_kernel(n_row, c, where_ref, *refs):
+    w_refs, others = refs[:CUTS], refs[CUTS : CUTS + n_row - 1]
     send_ref, keep_ref, rows_ref, lhs = refs[-4:]
-    core, row = where_ref[0] & 1, where_ref[1]
-    count = (n_row - 1) * c
-
-    def put(s, ref):
-        lhs[pl.ds((s - 1) * c, c), :] = ref[1 - core]
-        lhs[pl.ds(count + (s - 1) * c, c), :] = ref[core]
+    core, count = where_ref[0] & 1, (n_row - 1) * c
 
     @pl.when(pl.program_id(0) == 0)
     def _():
-        for s in range(1, n_row):
-            if s == half:
-                put(s, near[s - 1])
-                continue
-            came_far = (row < s) if s < half else (row >= s)
-            pl.when(came_far)(functools.partial(put, s, far[abs(s - half) - 1]))
-            pl.when(jnp.logical_not(came_far))(functools.partial(put, s, near[s - 1]))
+        for s, ref in enumerate(others):
+            lhs[pl.ds(s * c, c), :] = ref[0, 1 - core]
+            lhs[pl.ds(count + s * c, c), :] = ref[0, core]
         rows_ref[...] = lhs[...]
 
-    res = jnp.dot(lhs[...], w_ref[0], preferred_element_type=F32).astype(BF16)
+    res, width = None, lhs.shape[1] // CUTS
+    for q, w_ref in enumerate(w_refs):
+        term = jnp.dot(lhs[:, pl.ds(q * width, width)], w_ref[0], preferred_element_type=F32)
+        res = term if res is None else res + term
+    res = res.astype(BF16)
     send_ref[...] = res[:count].reshape(send_ref.shape)
     keep_ref[...] = res[count:].reshape(keep_ref.shape)
 
 
-def partial_sums(where, turned, near, far, send, keep, k, after):
+def partial_sums(where, turned, others, send, keep, after):
     n_row, c, units = send.shape
     tiles, depth, tile = turned.shape
     count = 2 * (n_row - 1) * c
-    blocks = near + far
-    in_specs = [pl.BlockSpec((1, depth, tile), lambda i, s: (i, 0, 0))]
-    in_specs += [once((2, c, depth), (0, k if a.shape[1] > c else 0, 0)) for a in blocks]
+    in_specs = [
+        pl.BlockSpec((1, depth // CUTS, tile), lambda i, s, q=q: (i, q, 0)) for q in range(CUTS)
+    ]
+    if len(others) == 1:
+        others = others * (n_row - 1)
+        at = [lambda i, s, d=d: (lax.rem(s[1] - d + n_row, n_row), 0, 0, 0) for d in range(1, n_row)]
+    else:
+        others = [a[None] for a in others]
+        at = [lambda i, s: (0, 0, 0, 0)] * len(others)
+    in_specs += [pl.BlockSpec((1, 2, c, depth), index, pipeline_mode=pl.Buffered(1)) for index in at]
     in_specs += [ANYWHERE] * (2 + len(after))
     part = jax.ShapeDtypeStruct(send.shape, BF16)
     part_spec = pl.BlockSpec((n_row - 1, c, tile), lambda i, s: (0, 0, i))
@@ -132,18 +132,19 @@
             out_specs=(part_spec, part_spec, pl.BlockSpec((count, depth), lambda i, s: (0, 0))),
             scratch_shapes=[pltpu.VMEM((count, depth), BF16)],
         ),
-        input_output_aliases={2 + len(blocks): 0, 3 + len(blocks): 1},
+        input_output_aliases={1 + CUTS + len(others): 0, 2 + CUTS + len(others): 1},
         compiler_params=PARAMS,
         cost_estimate=cost(
             2 * count * depth * units, 2 * count * depth + units * depth + count * units
         ),
         name="partial_sums",
-    )(where, turned, *blocks, send, keep, *after)
+    )(where, *[turned] * CUTS, *others, send, keep, *after)
 
 
 def weight_kernel(places, n_row, c, where_ref, *refs):
     acts_refs, refs = refs[: len(places)], refs[len(places):]
-    own_ref, grads_refs, out_ref, acts = refs[0], refs[1:3], refs[-2], refs[-1]
+    own_ref, grads_refs = refs[0], refs[1:3]
+    out_ref, acts, grads, sems = refs[-4:]
     me, row = where_ref[0], where_ref[1]
     core, tokens, count = me & 1, 2 * c, 2 * (n_row - 1) * c
     for (j0, j1), ref in zip(places, acts_refs):
@@ -155,23 +156,30 @@
                 owner // 2 == row, 2 * count + h * tokens + k * c, k * count + slot * c
             )
             acts[pl.ds(pl.multiple_of(start, c), c), :] = ref[pl.ds(k * c, c), :]
-    terms = [(0, grads_refs[0][...]), (count, grads_refs[1][...])]
-    terms.append((2 * count, own_ref[...].reshape(2 * tokens, own_ref.shape[2])))
-    total = None
-    for start, rows in terms:
-        term = lax.dot_general(
-            acts[pl.ds(start, rows.shape[0]), :], rows,
-            (((0,), (0,)), ((), ())), preferred_element_type=F32,
-        )
-        total = term if total is None else total + term
-    out_ref[...] = total.astype(BF16)
+
+    @pl.when(pl.program_id(0) == 0)
+    def _():
+        sources = [ref.at[pl.ds(i * tokens, tokens)] for ref in grads_refs for i in range(n_row - 1)]
+        sources += [own_ref.at[h] for h in range(2)]
+        copies = [
+            pltpu.make_async_copy(source, grads.at[pl.ds(i * tokens, tokens)], sems.at[i])
+            for i, source in enumerate(sources)
+        ]
+        for copy in copies:
+            copy.start()
+        for copy in copies:
+            copy.wait()
+
+    out_ref[...] = lax.dot_general(
+        acts[...], grads[...], (((0,), (0,)), ((), ())), preferred_element_type=F32
+    ).astype(BF16)
 
 
 def weight_rows(where, pieces, own, grads, before, shape, n_row, c, tile, first, count, after):
     places = [place for place, _ in pieces]
     rows, width = 2 * n_row * 2 * c, shape[1]
     in_specs = [pl.BlockSpec((a.shape[0], tile), lambda i, s: (0, first + i)) for _, a in pieces]
-    in_specs += [once(own.shape, (0, 0, 0))] + [once(g.shape, (0, 0)) for g in grads]
+    in_specs += [ANYWHERE] * 3
     args = [a for _, a in pieces] + [own, *grads, *after]
     in_specs += [ANYWHERE] * len(after)
     aliases = {}
@@ -187,7 +195,11 @@
             grid=(count,),
             in_specs=in_specs,
             out_specs=pl.BlockSpec((tile, width), lambda i, s: (first + i, 0)),
-            scratch_shapes=[pltpu.VMEM((rows, tile), BF16)],
+            scratch_shapes=[
+                pltpu.VMEM((rows, tile), BF16),
+                pltpu.VMEM((rows, width), BF16),
+                pltpu.SemaphoreType.DMA((2 * n_row,)),
+            ],
         ),
         input_output_aliases=aliases,
         compiler_params=PARAMS,
@@ -314,23 +326,15 @@
     table = slot_of(row, col ^ order, n_row)
 
     own = out_grad.reshape(2, tokens, features)
-    half = n_row // 2
     chunks = [own[:, :c], own[:, c:]]
-    middle = [near_shift(chunks[0], half, n_row), None]
-    others = {s: near_shift(own, s, n_row) for s in range(1, n_row) if s != half}
+    others0 = [shift(chunks[0], s, n_row) for s in range(1, n_row)]
 
     whole = {bit: flip(hidden_acts, (bit, bit), n_col) for bit in further}
 
     turned, send0, keep0, send1, keep1 = turn_weights(where, own, down_weight, c, n_row, tile)
-    middle[0], turned, chunks[1], arrived = lax.optimization_barrier(
-        (middle[0], turned, chunks[1], list(whole.values()))
-    )
+    turned, chunks[1] = lax.optimization_barrier((turned, chunks[1]))
+    turned, arrived, others0 = lax.optimization_barrier((turned, list(whole.values()), others0))
     whole = dict(zip(whole, arrived))
-    far0 = [far_shift(middle[0], e, n_row) for e in range(1, half)]
-    middle[1] = near_shift(chunks[1], half, n_row)
-
-    def near(k):
-        return [middle[k] if s == half else others[s] for s in range(1, n_row)]
 
     corners = []
     for t, bits in enumerate(levels[1:]):
@@ -340,13 +344,10 @@
             corners.append((bits, jnp.where(col & 1, whole[bits[1]], whole[bits[0]])))
     corners = [((j0, j1), a) for (j0, j1), a in corners if j0 not in whole]
 
-    send0, keep0, grads0 = partial_sums(
-        where, turned, near(0), far0, send0, keep0, 0, list(whole.values())
-    )
+    others1 = [lax.all_gather(chunks[1], "row")]
+    send0, keep0, grads0 = partial_sums(where, turned, others0, send0, keep0, [])
     zero = Halving(send0, keep0, levels, n_col)
 
-    middle[1], tied = lax.optimization_barrier((middle[1], send0))
-    far1 = [far_shift(middle[1], e, n_row) for e in range(1, half)]
     pieces = [((0, 0), hidden_acts)] + [((j, j), a) for j, a in whole.items()] + corners
     pieces += [((j1 ^ 1, j0 ^ 1), flip(a, (1, 1), n_col)) for (j0, j1), a in pieces]
     exchanged = [a for _, a in pieces[n_col // 2 :]]
@@ -369,13 +370,13 @@
             done += count
         return [weight_grad]
 
-    after = [hold([tied, middle[1]] + [a for _, a in corners])]
+    after = [hold([send0] + [a for _, a in corners])]
     after = advance([zero], [], 0, after)
     send1, keep1, grads1 = partial_sums(
-        where, turned, near(1), far1, send1, keep1, 1, after + exchanged[:1]
+        where, turned, others1, send1, keep1, after + exchanged
     )
     one = Halving(send1, keep1, levels, n_col)
-    after = work(3, [send1])
+    after = work(3, [send1, zero.terms[-1][0]])
     parts, steps = [zero, one], len(levels) - 1
     for step in range(steps):
         going, ended = [p for p in parts if p.levels], [p for p in parts if not p.levels]

time: 232 us -> 241 us (1.039)
  waiting for transfers between devices: 43.6 us -> 61.9 us
  between operations: 0.79 us -> 14.2 us
  starting transfers between devices: 28.7 us -> 16 us
  Pallas kernels: 143 us -> 136 us
    ppermute x13, waiting for transfers between devices: 23.4 us -> 38 us  [flip(): return lax.ppermute(x, 'col', [(i, i ^ bits[i & 1]) for i in range(n)])]
    ppermute x6 -> x3, starting transfers between devices: 18 us -> 4.61 us  [shift(): return lax.ppermute(x, 'row', [(i, (i + s) % n) for i in range(n)])]
    all_gather x0 -> x1, waiting for transfers between devices: none -> 9.23 us  [per_device(): others1 = [lax.all_gather(chunks[1], 'row')]]
    ppermute x6 -> x3, waiting for transfers between devices: 20.2 us -> 14.7 us  [shift(): return lax.ppermute(x, 'row', [(i, (i + s) % n) for i in range(n)])]
    pallas_call x3, Pallas kernels: 54.3 us -> 49.4 us  [weight_rows(): pl.pallas_call(functools.partial(weight_kernel, places, n_row, c), out_sh...]
    unnamed x34 -> x22, local copies, waits for them, and re-layouts: 8.69 us -> 6.84 us
  transfers between devices with their start and end apart: 19 -> 17, of which waited for: 8 -> 6; matrix products, arithmetic and copies ran while one was open for 2% -> 1% of each run, Pallas kernels for 47% -> 43%
where the time goes in v4:
time: 241 us; the launch traced here: 240 us
  Pallas kernels  136 us (56%)
  waiting for transfers between devices  61.9 us (26%)
  starting transfers between devices  16 us (7%)
  between operations  14.2 us (6%)
  local copies, waits for them, and re-layouts  8.92 us (4%)
  other arithmetic  3.15 us (1%)
    pallas_call x3, Pallas kernels, weight_rows(): pl.pallas_call(functools.partial(weight_kernel, places, n_row, c), out_sh...  49.4 us
    pallas_call x2, Pallas kernels, partial_sums(): pl.pallas_call(functools.partial(partial_kernel, n_row, c), out_shape=(pa...  41.5 us
    ppermute x13, waiting for transfers between devices, flip(): return lax.ppermute(x, 'col', [(i, i ^ bits[i & 1]) for i in range(n)])  38 us
    pallas_call x1, Pallas kernels, turn_weights(): pl.pallas_call(functools.partial(turn_kernel, c), out_shape=(jax.ShapeDty...  27.9 us
    pallas_call x4, Pallas kernels, sums(): pl.pallas_call(functools.partial(sums_kernel, [len(terms) for terms, _ in...  16.6 us
    ppermute x3, waiting for transfers between devices, shift(): return lax.ppermute(x, 'row', [(i, (i + s) % n) for i in range(n)])  14.7 us
    ppermute x13, starting transfers between devices, flip(): return lax.ppermute(x, 'col', [(i, i ^ bits[i & 1]) for i in range(n)])  11.3 us
    all_gather x1, waiting for transfers between devices, per_device(): others1 = [lax.all_gather(chunks[1], 'row')]  9.23 us
  transfers between devices with their start and end apart: 17, of which 6 were waited for; matrix products, arithmetic and copies ran while one was open for 1% of the time, Pallas kernels for 43%

profile of v4, /device:TPU:0, one launch (start us, length us, event | category | flops | bytes accessed | tf_op | source)
XLA Modules:
  0.0 240.2 jit_solution(5091852086341711219)
XLA Ops:
  7.2 0.0 all-gather.3.cloned.1.call-start
  7.2 3.0 %collective-permute-start.1 = (bf16[128,6656]{1,0:T(8,128)(2,1)}, bf16[128,6656]{1,0:T(8,128)(2,1)}, u32[]{:S(2)}, u32[]{:S(2)}) collective-permute-start(bf16[128,6656]{1,0:T(8,128)(2,1)} %refs_0_.7), channel_id=1, source_target_pairs={{0,4},{1,5},{2,6},{3,7},{4,0},{5,1},{6,2},{7,3},{8,12},{9,13},{10,... | collective-permute-start | bytes 5111816 | tf_op jit(solution)/shard_map/ppermute | solution.py:32
  10.2 1.5 collective-permute-start
  11.7 2.1 fusion.2
  13.8 3.6 %collective-permute-start.4 = (bf16[2,64,2048]{2,1,0:T(8,128)(2,1)S(1)}, bf16[2,64,2048]{2,1,0:T(8,128)(2,1)S(1)}, u32[]{:S(2)}, u32[]{:S(2)}) collective-permute-start(bf16[2,64,2048]{2,1,0:T(8,128)(2,1)S(1)} %get-tuple-element.48), channel_id=1, source_target_pairs={{0,24},{8,0},{16,8},{24,16},{1,25},{9,1},{17,9},{25,17},{2,26},{10... | collective-permute-start | bytes 1572872 | tf_op jit(solution)/shard_map/ppermute | solution.py:36
  17.4 1.0 collective-permute-start.2
  18.4 0.6 pad_add_fusion.where_ref
  19.0 27.9 %turn_weights.1 = (bf16[13,2048,512]{2,1,0:T(8,128)(2,1)}, bf16[4,64,6656]{2,1,0:T(8,128)(2,1)}, bf16[4,64,6656]{2,1,0:T(8,128)(2,1)}, bf16[4,64,6656]{2,1,0:T(8,128)(2,1)}, bf16[4,64,6656]{2,1,0:T(8,128)(2,1)}) custom-call(s32[2]{0:T(128)} %pad_add_fusion.where_ref, bf16[2,128,2048]{2,1,0:T(8,128)(2,1)} %bitcast.8, bf16[6656,2048]{1,0:T(8,128)(2,1)} %refs_3_.1, ...), custom_call_target="tpu_custom_call" | custom-call | flops 6979321856 | bytes 57933824 | tf_op jit(solution)/shard_map/turn_weights/pallas_call | solution.py:70
  46.9 0.0 copy-start.10
  46.9 0.0 collective-permute-done.4
  46.9 14.7 %collective-permute-done.3 = bf16[2,64,2048]{2,1,0:T(8,128)(2,1)S(1)} collective-permute-done((bf16[2,64,2048]{2,1,0:T(8,128)(2,1)S(1)}, bf16[2,64,2048]{2,1,0:T(8,128)(2,1)S(1)}, u32[]{:S(2)}, u32[]{:S(2)}) %collective-permute-start.3) | collective-permute-done | bytes 524320 | tf_op jit(solution)/shard_map/ppermute | solution.py:36
  61.6 0.0 collective-permute-done.2
  61.6 0.0 collective-permute-done.1.refs_2_
  61.7 0.0 collective-permute-done.refs_1_
  61.7 2.0 broadcast_select_fusion
  63.7 0.6 collective-permute-start.5
  64.3 0.0 all-gather.3.cloned.1.call-update
  64.3 0.6 compare_select_fusion.table_ref
  64.9 0.5 collective-permute-start.7
  65.4 0.0 collective-permute-start.8
  65.4 20.8 %partial_sums.2 = (bf16[4,64,6656]{2,1,0:T(8,128)(2,1)}, bf16[4,64,6656]{2,1,0:T(8,128)(2,1)}, bf16[384,2048]{1,0:T(8,128)(2,1)}) custom-call(s32[2]{0:T(128)} %pad_add_fusion.where_ref, bf16[13,2048,512]{2,1,0:T(8,128)(2,1)} %get-tuple-element.29.refs_0_.refs_1_.refs_2_.refs_3_, ...), custom_call_target="tpu_custom_call", output_to_operand_aliasing={{0}: (8, {}), {1}: (9, {})} | custom-call | flops 10468982784 | bytes 35520512 | tf_op jit(solution)/shard_map/partial_sums/pallas_call | solution.py:125
  86.2 0.5 collective-permute-start.10
  86.7 0.0 collective-permute-done.5.refs_1_.refs_3_
  86.7 0.1 collective-permute-start.9
  86.8 0.6 hold.1.refs_2_
  87.4 7.6 %collective-permute-done.10.refs_1_.refs_4_ = bf16[4,64,6656]{2,1,0:T(8,128)(2,1)S(1)} collective-permute-done((bf16[4,64,6656]{2,1,0:T(8,128)(2,1)}, bf16[4,64,6656]{2,1,0:T(8,128)(2,1)S(1)}, u32[]{:S(2)}, u32[]{:S(2)}) %collective-permute-start.10) | collective-permute-done | bytes 3407904 | tf_op jit(solution)/shard_map/ppermute | solution.py:32
  95.0 1.8 copy-done
  96.8 3.7 %sums.4.refs_9_ = bf16[2,64,6656]{2,1,0:T(8,128)(2,1)} custom-call(s32[4]{0:T(128)} %compare_select_fusion.table_ref, bf16[4,64,6656]{2,1,0:T(8,128)(2,1)} %get-tuple-element.39.refs_0_.refs_3_, bf16[4,64,6656]{2,1,0:T(8,128)(2,1)} %copy-done, f32[8,128]{1,0:T(8,128)} %hold.1.refs_2_), custom_call_target="tpu_custom_call" | custom-call | flops 2555904 | bytes 5111808 | tf_op jit(solution)/shard_map/sums/pallas_call | solution.py:263
  100.6 9.2 %all-gather.3.cloned.1.call-done = bf16[8,64,2048]{2,1,0:T(8,128)(2,1)} async-done(((bf16[2,64,2048]{2,1,0:T(8,128)(2,1)}), bf16[8,64,2048]{2,1,0:T(8,128)(2,1)}) %all-gather.3.cloned.1.call-update) | async-done | bytes 2097168 | tf_op jit(solution)/shard_map/all_gather | solution.py:347
  109.8 20.7 %partial_sums.3 = (bf16[4,64,6656]{2,1,0:T(8,128)(2,1)}, bf16[4,64,6656]{2,1,0:T(8,128)(2,1)}, bf16[384,2048]{1,0:T(8,128)(2,1)}) custom-call(s32[2]{0:T(128)} %pad_add_fusion.where_ref, bf16[13,2048,512]{2,1,0:T(8,128)(2,1)} %get-tuple-element.29.refs_0_.refs_1_.refs_2_.refs_3_, ...), custom_call_target="tpu_custom_call", output_to_operand_aliasing={{0}: (8, {}), {1}: (9, {})} | custom-call | flops 10468982784 | bytes 35520512 | tf_op jit(solution)/shard_map/partial_sums/pallas_call | solution.py:125
  130.5 0.0 collective-permute-start.11
  130.5 1.7 collective-permute-start.12
  132.2 20.4 %collective-permute-done.12.refs_12_.refs_2_.refs_5_ = bf16[2,64,6656]{2,1,0:T(8,128)(2,1)S(1)} collective-permute-done((bf16[2,64,6656]{2,1,0:T(8,128)(2,1)}, bf16[2,64,6656]{2,1,0:T(8,128)(2,1)S(1)}, u32[]{:S(2)}, u32[]{:S(2)}) %collective-permute-start.12) | collective-permute-done | bytes 1703968 | tf_op jit(solution)/shard_map/ppermute | solution.py:32
  152.6 1.2 copy-done.2
  153.9 13.1 %weight_rows.3.refs_5_.refs_12_ = bf16[6656,2048]{1,0:T(8,128)(2,1)} custom-call(s32[2]{0:T(128)} %pad_add_fusion.where_ref, bf16[128,6656]{1,0:T(8,128)(2,1)} %refs_0_.7, bf16[128,6656]{1,0:T(8,128)(2,1)} %collective-permute-done.refs_1_, bf16[128,6656]{1,0:T(8,128)(2,1)} %collective-permute-done.1.refs_2_, ...), custom_call_target="tpu_custom_call" | custom-call | flops 6442450944 | bytes 13631488 | tf_op jit(solution)/shard_map/weight_rows/pallas_call | solution.py:190
  167.0 1.7 copy-done.1
  168.7 4.7 %sums.5 = (bf16[1,64,6656]{2,1,0:T(8,128)(2,1)}, bf16[2,64,6656]{2,1,0:T(8,128)(2,1)}) custom-call(s32[4]{0:T(128)} %compare_select_fusion.table_ref, bf16[4,64,6656]{2,1,0:T(8,128)(2,1)} %get-tuple-element.39.refs_0_.refs_3_, bf16[4,64,6656]{2,1,0:T(8,128)(2,1)} %copy-done, bf16[2,64,6656]{2,1,0:T(8,128)(2,1)} %copy-done.2, ...), custom_call_target="tpu_custom_call" | custom-call | flops 4259840 | bytes 8519680 | tf_op jit(solution)/shard_map/sums/pallas_call | solution.py:263
  173.3 1.6 collective-permute-start.13
  175.0 1.5 collective-permute-start.14
  176.4 18.2 %weight_rows.4.refs_7_.refs_12_ = bf16[6656,2048]{1,0:T(8,128)(2,1)} custom-call(s32[2]{0:T(128)} %pad_add_fusion.where_ref, bf16[128,6656]{1,0:T(8,128)(2,1)} %refs_0_.7, bf16[128,6656]{1,0:T(8,128)(2,1)} %collective-permute-done.refs_1_, bf16[128,6656]{1,0:T(8,128)(2,1)} %collective-permute-done.1.refs_2_, ...), custom_call_target="tpu_custom_call", output_to_operand_aliasing={{}: (13, {})} | custom-call | flops 10737418240 | bytes 19922944 | tf_op jit(solution)/shard_map/weight_rows/pallas_call | solution.py:190
  194.6 2.5 %collective-permute-done.14.refs_6_ = bf16[1,64,6656]{2,1,0:T(8,128)(2,1)S(1)} collective-permute-done((bf16[1,64,6656]{2,1,0:T(8,128)(2,1)}, bf16[1,64,6656]{2,1,0:T(8,128)(2,1)S(1)}, u32[]{:S(2)}, u32[]{:S(2)}) %collective-permute-start.14) | collective-permute-done | bytes 852000 | tf_op jit(solution)/shard_map/ppermute | solution.py:32
  197.1 7.4 %collective-permute-done.13.refs_2_ = bf16[2,64,6656]{2,1,0:T(8,128)(2,1)S(1)} collective-permute-done((bf16[2,64,6656]{2,1,0:T(8,128)(2,1)}, bf16[2,64,6656]{2,1,0:T(8,128)(2,1)S(1)}, u32[]{:S(2)}, u32[]{:S(2)}) %collective-permute-start.13) | collective-permute-done | bytes 1703968 | tf_op jit(solution)/shard_map/ppermute | solution.py:32
  204.5 1.2 copy-done.3
  205.7 4.6 %sums.6 = (bf16[1,64,6656]{2,1,0:T(8,128)(2,1)}, bf16[128,6656]{1,0:T(8,128)(2,1)}) custom-call(s32[4]{0:T(128)} %compare_select_fusion.table_ref, bf16[4,64,6656]{2,1,0:T(8,128)(2,1)} %get-tuple-element.42.refs_3_.refs_0_, bf16[4,64,6656]{2,1,0:T(8,128)(2,1)} %copy-done.1, bf16[2,64,6656]{2,1,0:T(8,128)(2,1)} %copy-done.3, ...), custom_call_target="tpu_custom_call" | custom-call | flops 3833856 | bytes 7667712 | tf_op jit(solution)/shard_map/sums/pallas_call | solution.py:263
  210.3 0.4 collective-permute-start.15
  210.7 18.2 %weight_rows.5.refs_4_ = bf16[6656,2048]{1,0:T(8,128)(2,1)} custom-call(s32[2]{0:T(128)} %pad_add_fusion.where_ref, bf16[128,6656]{1,0:T(8,128)(2,1)} %refs_0_.7, bf16[128,6656]{1,0:T(8,128)(2,1)} %collective-permute-done.refs_1_, bf16[128,6656]{1,0:T(8,128)(2,1)} %collective-permute-done.1.refs_2_, ...), custom_call_target="tpu_custom_call", output_to_operand_aliasing={{}: (13, {})} | custom-call | flops 10737418240 | bytes 19922944 | tf_op jit(solution)/shard_map/weight_rows/pallas_call | solution.py:190
  228.8 0.9 copy-done.4
  229.7 3.6 %sums.7 = bf16[128,6656]{1,0:T(8,128)(2,1)} custom-call(s32[4]{0:T(128)} %compare_select_fusion.table_ref, bf16[4,64,6656]{2,1,0:T(8,128)(2,1)} %get-tuple-element.42.refs_3_.refs_0_, bf16[4,64,6656]{2,1,0:T(8,128)(2,1)} %copy-done.1, bf16[2,64,6656]{2,1,0:T(8,128)(2,1)} %copy-done.3, ...), custom_call_target="tpu_custom_call", output_to_operand_aliasing={{}: (6, {})} | custom-call | flops 2129920 | bytes 4259840 | tf_op jit(solution)/shard_map/sums/pallas_call | solution.py:263
  (24 shorter events, 0.1 us)
Async XLA Ops:
  7.2 102.6 %all-gather.3.cloned.1.call-start = ((), (), s32[]{:S(2)}) async-start(), calls=%async_computation | async-start | bytes 2621440 | tf_op jit(solution)/shard_map/all_gather | solution.py:347
  7.2 54.4 %collective-permute-start.1 = (bf16[128,6656]{1,0:T(8,128)(2,1)}, bf16[128,6656]{1,0:T(8,128)(2,1)}, u32[]{:S(2)}, u32[]{:S(2)}) collective-permute-start(bf16[128,6656]{1,0:T(8,128)(2,1)} %refs_0_.7), channel_id=1, source_target_pairs={{0,4},{1,5},{2,6},{3,7},{4,0},{5,1},{6,2},{7,3},{8,12},{9,13},{10,... | collective-permute-start | bytes 5111816 | tf_op jit(solution)/shard_map/ppermute | solution.py:32
  10.2 51.4 %collective-permute-start = (bf16[128,6656]{1,0:T(8,128)(2,1)}, bf16[128,6656]{1,0:T(8,128)(2,1)}, u32[]{:S(2)}, u32[]{:S(2)}) collective-permute-start(bf16[128,6656]{1,0:T(8,128)(2,1)} %refs_0_.7), channel_id=1, source_target_pairs={{0,2},{1,3},{2,0},{3,1},{4,6},{5,7},{6,4},{7,5},{8,10},{9,11},{10,... | collective-permute-start | bytes 5111816 | tf_op jit(solution)/shard_map/ppermute | solution.py:32
  13.8 33.1 %collective-permute-start.4 = (bf16[2,64,2048]{2,1,0:T(8,128)(2,1)S(1)}, bf16[2,64,2048]{2,1,0:T(8,128)(2,1)S(1)}, u32[]{:S(2)}, u32[]{:S(2)}) collective-permute-start(bf16[2,64,2048]{2,1,0:T(8,128)(2,1)S(1)} %get-tuple-element.48), channel_id=1, source_target_pairs={{0,24},{8,0},{16,8},{24,16},{1,25},{9,1},{17,9},{25,17},{2,26},{10... | collective-permute-start | bytes 1572872 | tf_op jit(solution)/shard_map/ppermute | solution.py:36
  17.4 44.2 %collective-permute-start.3 = (bf16[2,64,2048]{2,1,0:T(8,128)(2,1)S(1)}, bf16[2,64,2048]{2,1,0:T(8,128)(2,1)S(1)}, u32[]{:S(2)}, u32[]{:S(2)}) collective-permute-start(bf16[2,64,2048]{2,1,0:T(8,128)(2,1)S(1)} %get-tuple-element.48), channel_id=1, source_target_pairs={{0,16},{8,24},{16,0},{24,8},{1,17},{9,25},{17,1},{25,9},{2,18},{10... | collective-permute-start | bytes 1572872 | tf_op jit(solution)/shard_map/ppermute | solution.py:36
  17.4 44.2 %collective-permute-start.2 = (bf16[2,64,2048]{2,1,0:T(8,128)(2,1)S(1)}, bf16[2,64,2048]{2,1,0:T(8,128)(2,1)S(1)}, u32[]{:S(2)}, u32[]{:S(2)}) collective-permute-start(bf16[2,64,2048]{2,1,0:T(8,128)(2,1)S(1)} %get-tuple-element.48), channel_id=1, source_target_pairs={{0,8},{8,16},{16,24},{24,0},{1,9},{9,17},{17,25},{25,1},{2,10},{10... | collective-permute-start | bytes 1572872 | tf_op jit(solution)/shard_map/ppermute | solution.py:36
  46.9 17.4 %copy-start.9 = (s32[4]{0:T(128)S(1)}, s32[4]{0:T(128)}, u32[]{:S(2)}) copy-start(s32[4]{0:T(128)} %constant.39.clone) | copy-start | bytes 52
  46.9 17.4 %copy-start.10 = (s32[4]{0:T(128)S(1)}, s32[4]{0:T(128)}, u32[]{:S(2)}) copy-start(s32[4]{0:T(128)} %constant.38.clone) | copy-start | bytes 52
  46.9 16.7 %copy-start.6 = (bf16[2,64,2048]{2,1,0:T(8,128)(2,1)}, bf16[2,64,2048]{2,1,0:T(8,128)(2,1)S(1)}, u32[]{:S(2)}) copy-start(bf16[2,64,2048]{2,1,0:T(8,128)(2,1)S(1)} %collective-permute-done.4) | copy-start | bytes 1572868
  61.6 2.0 copy-start.7
  61.6 2.0 copy-start.8
  63.7 23.0 %collective-permute-start.5 = (bf16[128,6656]{1,0:T(8,128)(2,1)S(1)}, bf16[128,6656]{1,0:T(8,128)(2,1)}, u32[]{:S(2)}, u32[]{:S(2)}) collective-permute-start(bf16[128,6656]{1,0:T(8,128)(2,1)S(1)} %broadcast_select_fusion), channel_id=1, source_target_pairs={{0,4},{1,3},{2,6},{3,1},{4,0},{5,7},{6,2},{7,5},{8,12},{9,11},{10,... | collective-permute-start | bytes 5111816 | tf_op jit(solution)/shard_map/ppermute | solution.py:32
  64.3 36.3 %collective-permute-start.6 = (bf16[128,6656]{1,0:T(8,128)(2,1)}, bf16[128,6656]{1,0:T(8,128)(2,1)}, u32[]{:S(2)}, u32[]{:S(2)}) collective-permute-start(bf16[128,6656]{1,0:T(8,128)(2,1)} %refs_0_.7), channel_id=1, source_target_pairs={{0,1},{1,0},{2,3},{3,2},{4,5},{5,4},{6,7},{7,6},{8,9},{9,8},{10,11... | collective-permute-start | bytes 5111816 | tf_op jit(solution)/shard_map/ppermute | solution.py:32
  64.9 44.9 %collective-permute-start.7 = (bf16[128,6656]{1,0:T(8,128)(2,1)}, bf16[128,6656]{1,0:T(8,128)(2,1)}, u32[]{:S(2)}, u32[]{:S(2)}) collective-permute-start(bf16[128,6656]{1,0:T(8,128)(2,1)} %collective-permute-done.refs_1_), channel_id=1, source_target_pairs={{0,1},{1,0},{2,3},{3,2},{4,5},{5,4},{6,7},{7,6},{8,9},{9,8},{10,11... | collective-permute-start | bytes 5111816 | tf_op jit(solution)/shard_map/ppermute | solution.py:32
  65.4 44.4 %collective-permute-start.8 = (bf16[128,6656]{1,0:T(8,128)(2,1)}, bf16[128,6656]{1,0:T(8,128)(2,1)}, u32[]{:S(2)}, u32[]{:S(2)}) collective-permute-start(bf16[128,6656]{1,0:T(8,128)(2,1)} %collective-permute-done.1.refs_2_), channel_id=1, source_target_pairs={{0,1},{1,0},{2,3},{3,2},{4,5},{5,4},{6,7},{7,6},{8,9},{9,8},{10,11... | collective-permute-start | bytes 5111816 | tf_op jit(solution)/shard_map/ppermute | solution.py:32
  86.2 8.8 %collective-permute-start.10 = (bf16[4,64,6656]{2,1,0:T(8,128)(2,1)}, bf16[4,64,6656]{2,1,0:T(8,128)(2,1)S(1)}, u32[]{:S(2)}, u32[]{:S(2)}) collective-permute-start(bf16[4,64,6656]{2,1,0:T(8,128)(2,1)} %get-tuple-element.40.refs_0_), channel_id=1, source_target_pairs={{0,1},{1,0},{2,3},{3,2},{4,5},{5,4},{6,7},{7,6},{8,9},{9,8},{10,11... | collective-permute-start | bytes 10223624 | tf_op jit(solution)/shard_map/ppermute | solution.py:32
  86.7 23.1 %collective-permute-start.9 = (bf16[128,6656]{1,0:T(8,128)(2,1)}, bf16[128,6656]{1,0:T(8,128)(2,1)}, u32[]{:S(2)}, u32[]{:S(2)}) collective-permute-start(bf16[128,6656]{1,0:T(8,128)(2,1)} %collective-permute-done.5.refs_1_.refs_3_), channel_id=1, source_target_pairs={{0,1},{1,0},{2,3},{3,2},{4,5},{5,4},{6,7},{7,6},{8,9},{9,8},{10,11... | collective-permute-start | bytes 5111816 | tf_op jit(solution)/shard_map/ppermute | solution.py:32
  95.0 1.8 copy-start
  130.5 36.5 %collective-permute-start.11 = (bf16[4,64,6656]{2,1,0:T(8,128)(2,1)}, bf16[4,64,6656]{2,1,0:T(8,128)(2,1)S(1)}, u32[]{:S(2)}, u32[]{:S(2)}) collective-permute-start(bf16[4,64,6656]{2,1,0:T(8,128)(2,1)} %get-tuple-element.43.refs_11_), channel_id=1, source_target_pairs={{0,1},{1,0},{2,3},{3,2},{4,5},{5,4},{6,7},{7,6},{8,9},{9,8},{10,11... | collective-permute-start | bytes 10223624 | tf_op jit(solution)/shard_map/ppermute | solution.py:32
  130.5 22.1 %collective-permute-start.12 = (bf16[2,64,6656]{2,1,0:T(8,128)(2,1)}, bf16[2,64,6656]{2,1,0:T(8,128)(2,1)S(1)}, u32[]{:S(2)}, u32[]{:S(2)}) collective-permute-start(bf16[2,64,6656]{2,1,0:T(8,128)(2,1)} %sums.4.refs_9_), channel_id=1, source_target_pairs={{0,2},{1,5},{2,0},{3,7},{4,6},{5,1},{6,4},{7,3},{8,10},{9,13},{10,... | collective-permute-start | bytes 5111816 | tf_op jit(solution)/shard_map/ppermute | solution.py:32
  152.6 1.2 copy-start.2
  167.0 1.7 copy-start.1
  173.3 31.2 %collective-permute-start.13 = (bf16[2,64,6656]{2,1,0:T(8,128)(2,1)}, bf16[2,64,6656]{2,1,0:T(8,128)(2,1)S(1)}, u32[]{:S(2)}, u32[]{:S(2)}) collective-permute-start(bf16[2,64,6656]{2,1,0:T(8,128)(2,1)} %get-tuple-element.44), channel_id=1, source_target_pairs={{0,2},{1,5},{2,0},{3,7},{4,6},{5,1},{6,4},{7,3},{8,10},{9,13},{10,... | collective-permute-start | bytes 5111816 | tf_op jit(solution)/shard_map/ppermute | solution.py:32
  175.0 22.1 %collective-permute-start.14 = (bf16[1,64,6656]{2,1,0:T(8,128)(2,1)}, bf16[1,64,6656]{2,1,0:T(8,128)(2,1)S(1)}, u32[]{:S(2)}, u32[]{:S(2)}) collective-permute-start(bf16[1,64,6656]{2,1,0:T(8,128)(2,1)} %get-tuple-element.45.refs_11_), channel_id=1, source_target_pairs={{0,4},{1,3},{2,6},{3,1},{4,0},{5,7},{6,2},{7,5},{8,12},{9,11},{10,... | collective-permute-start | bytes 2555912 | tf_op jit(solution)/shard_map/ppermute | solution.py:32
  197.1 7.4 %copy-start.5 = (bf16[1,64,6656]{2,1,0:T(8,128)(2,1)}, bf16[1,64,6656]{2,1,0:T(8,128)(2,1)S(1)}, u32[]{:S(2)}) copy-start(bf16[1,64,6656]{2,1,0:T(8,128)(2,1)S(1)} %collective-permute-done.14.refs_6_) | copy-start | bytes 2555908
  204.5 1.2 copy-start.3
  210.3 18.5 %collective-permute-start.15 = (bf16[1,64,6656]{2,1,0:T(8,128)(2,1)}, bf16[1,64,6656]{2,1,0:T(8,128)(2,1)S(1)}, u32[]{:S(2)}, u32[]{:S(2)}) collective-permute-start(bf16[1,64,6656]{2,1,0:T(8,128)(2,1)} %get-tuple-element.46.refs_11_), channel_id=1, source_target_pairs={{0,4},{1,3},{2,6},{3,1},{4,0},{5,7},{6,2},{7,5},{8,12},{9,11},{10,... | collective-permute-start | bytes 2555912 | tf_op jit(solution)/shard_map/ppermute | solution.py:32
  228.8 0.9 copy-start.4
Sparse Core Ops, SparseCore 0:
  64.4 45.3 all-gather.2

commit v5 on v2

--- a/solution.py
+++ b/solution.py
@@ -9,7 +9,7 @@
 
 F32, BF16 = jnp.float32, jnp.bfloat16
 ANYWHERE = pl.BlockSpec(memory_space=pl.ANY)
-PARAMS = pltpu.CompilerParams(vmem_limit_bytes=58 * 1024 * 1024)
+PARAMS = pltpu.CompilerParams(vmem_limit_bytes=40 * 1024 * 1024)
 
 
 def cost(flops, values):
@@ -27,50 +27,34 @@
     return lax.ppermute(x, "col", [(i, i ^ bits[i & 1]) for i in range(n)])
 
 
-def near_shift(x, s, n):
-    pairs = [(i, (i + s) % n) for i in range(n)]
-    return lax.ppermute(x, "row", [(i, j) for i, j in pairs if abs(i - j) <= n // 2])
-
-
-def far_shift(x, e, n):
-    half = n // 2
-    up = [(i, i + e) for i in range(half, n - e)]
-    down = [(i, i - e) for i in range(e, half)]
-    return lax.ppermute(x, "row", up + down)
-
-
-def assemble_kernel(n_row, orders, c, where_ref, own_ref, *refs):
-    half = n_row // 2
-    near, far = refs[: n_row - 1], refs[n_row - 1 : n_row + half - 2]
+def doubled(x, bits, n):
+    held = {0: x}
+    for bit in bits:
+        pairs = [(i, i ^ bit) for i in range(n)]
+        for j in list(held):
+            held[j ^ bit] = lax.ppermute(held[j], "row", pairs)
+    return held
+
+
+def assemble_kernel(rows_of, orders, c, where_ref, *refs):
     grads_ref, turned_ref, rel = refs[-3:]
     me, row = where_ref[0], where_ref[1]
-    rows = own_ref.shape[0]
-
-    def put(s, ref):
-        start = pl.multiple_of(lax.rem(row - s + n_row, n_row) * rows, rows)
-        grads_ref[pl.ds(start, rows), :] = ref[...]
-
-    put(0, own_ref)
-    for s in range(1, n_row):
-        if s == half:
-            put(s, near[s - 1])
-            continue
-        came_far = (row < s) if s < half else (row >= s)
-        pl.when(came_far)(functools.partial(put, s, far[abs(s - half) - 1]))
-        pl.when(jnp.logical_not(came_far))(functools.partial(put, s, near[s - 1]))
+    for j, ref in zip(rows_of, refs):
+        rows = ref.shape[0]
+        grads_ref[pl.ds(pl.multiple_of((row ^ j) * rows, rows), rows), :] = ref[...]
     for p, (j0, j1) in enumerate(zip(*orders)):
         start = pl.multiple_of((me ^ jnp.where(me & 1, j1, j0)) * c, c)
         rel[pl.ds(p * c, c), :] = grads_ref[pl.ds(start, c), :]
     turned_ref[...] = rel[...].T
 
 
-def assemble(where, own, near, far, orders, c, after):
-    n_row, depth, rows = len(near) + 1, own.shape[1], len(orders[0]) * c
+def assemble(where, blocks, orders, c, after):
+    rows_of, arrays = list(blocks), list(blocks.values())
+    depth, rows = arrays[0].shape[1], len(orders[0]) * c
     steps = 2
-    part = pl.BlockSpec((own.shape[0], depth // steps), lambda i, s: (0, i))
-    arrays = [own, *near, *far]
+    part = pl.BlockSpec((arrays[0].shape[0], depth // steps), lambda i, s: (0, i))
     return pl.pallas_call(
-        functools.partial(assemble_kernel, n_row, orders, c),
+        functools.partial(assemble_kernel, rows_of, orders, c),
         out_shape=(
             jax.ShapeDtypeStruct((rows, depth), BF16),
             jax.ShapeDtypeStruct((depth, rows), BF16),
@@ -302,19 +286,32 @@
     whole = {bit: flip(hidden_acts, (bit, bit), n_col) for bit in further}
 
     by_owner = out_grad.reshape(owners, tokens, features)
-    own = [by_owner[:, at : at + c].reshape(owners * c, features) for at, c in chunks]
-
-    def near_blocks(x):
-        return [near_shift(x, s, n_row) for s in range(1, n_row)]
-
-    def far_blocks(near):
-        return [far_shift(near[n_row // 2 - 1], e, n_row) for e in range(1, n_row // 2)]
-
-    near0 = near_blocks(own[0])
-    *near0, own[1] = lax.optimization_barrier((*near0, own[1]))
-    far0 = far_blocks(near0)
-    near1 = near_blocks(own[1])
-    grads0, turned0 = assemble(where, own[0], near0, far0, orders, c, list(whole.values()))
+
+    def chunk(grads, k):
+        at, c = chunks[k]
+        return grads[:, at : at + c].reshape(owners * c, features)
+
+    own = [chunk(by_owner, 0)]
+
+    row_bits = [1 << b for b in reversed(range(n_row.bit_length() - 1))]
+    last = [(i, i ^ row_bits[-1]) for i in range(n_row)]
+
+    def most(x):
+        held = doubled(x, row_bits[:-1], n_row)
+        return {**held, row_bits[-1]: lax.ppermute(x, "row", last)}
+
+    def rest(held):
+        more = {j ^ row_bits[-1]: a for j, a in held.items() if j not in (0, row_bits[-1])}
+        return {**held, **{j: lax.ppermute(a, "row", last) for j, a in more.items()}}
+
+    first = most(own[0])
+    far, later = lax.optimization_barrier((first[row_bits[0]], by_owner))
+    own.append(chunk(later, 1))
+    first[row_bits[0]] = far
+    first = rest(first)
+    second = most(own[1])
+
+    grads0, turned0 = assemble(where, first, orders, c, list(whole.values()))
 
     corners = []
     for t, bits in enumerate(levels[1:]):
@@ -333,8 +330,9 @@
     send, keep, after = partials(turned0, 0, tiles, [])
     zero = Halving([send], [keep], levels, n_col)
 
-    *near1, tied = lax.optimization_barrier((*near1, after[0]))
-    far1 = far_blocks(near1)
+    second, tied = lax.optimization_barrier((second, after[0]))
+    arrived = [a for j, a in second.items() if j]
+    second = rest(second)
     pieces = [((0, 0), hidden_acts)] + [((j, j), a) for j, a in whole.items()] + corners
     pieces += [((j1 ^ 1, j0 ^ 1), flip(a, (1, 1), n_col)) for (j0, j1), a in pieces]
 
@@ -356,10 +354,10 @@
             done += count
         return [weight_grad]
 
-    after = [hold([tied] + near1 + [a for _, a in corners])]
+    after = [hold([tied] + arrived + [a for _, a in corners])]
     after = advance([zero], [], 0, after)
     exchanged = [a for _, a in pieces[n_col // 2 :]]
-    grads1, turned1 = assemble(where, own[1], near1, far1, orders, c, after + exchanged[:1])
+    grads1, turned1 = assemble(where, second, orders, c, after + exchanged[:1])
     grads = [grads0, grads1]
     send_a, keep_a, after = partials(turned1, 0, cut, after)
     a1 = Halving([send_a], [keep_a], levels, n_col)

time: 210 us -> 190 us (0.905)
  Pallas kernels: 120 us -> 104 us
  starting transfers between devices: 33.2 us -> 22.7 us
  local copies, waits for them, and re-layouts: 9.05 us -> 18.7 us
  waiting for transfers between devices: 43.1 us -> 40.8 us
    ppermute x8 -> x6, waiting for transfers between devices: 39 us -> 26.6 us  [the longest x2 21.5 us: doubled(): held[j ^ bit] = lax.ppermute(held[j], 'row', pairs)]
    ppermute x8 -> x6, starting transfers between devices: 21.9 us -> 9.63 us  [the longest x2 5.39 us: doubled(): held[j ^ bit] = lax.ppermute(held[j], 'row', pairs)]
    ppermute x16, waiting for transfers between devices: 4.13 us -> 14.2 us  [flip(): return lax.ppermute(x, 'col', [(i, i ^ bits[i & 1]) for i in range(n)])]
    unnamed x28 -> x56, local copies, waits for them, and re-layouts: 6.77 us -> 15.7 us
    pallas_call x5, Pallas kernels: 15.6 us -> 8.55 us  [sums(): pl.pallas_call(functools.partial(sums_kernel, layout, len(ended)), out_sh...]
    pallas_call x2, Pallas kernels: 8.4 us -> 4.39 us  [assemble(): pl.pallas_call(functools.partial(assemble_kernel, rows_of, orders, c), ou...]
    pallas_call x3, Pallas kernels: 49.2 us -> 45.6 us  [partial_sums(): pl.pallas_call(partial_kernel, out_shape=(out, out), grid=(count,), in_sp...]
  transfers between devices with their start and end apart: 24 -> 22, of which waited for: 5 -> 5; matrix products, arithmetic and copies ran while one was open for 2% -> 2% of each run, Pallas kernels for 54% -> 53%
where the time goes in v5:
time: 190 us; the launch traced here: 189 us
  Pallas kernels  104 us (55%)
  waiting for transfers between devices  40.8 us (21%)
  starting transfers between devices  22.7 us (12%)
  local copies, waits for them, and re-layouts  18.7 us (10%)
    pallas_call x3, Pallas kernels, weight_rows(): pl.pallas_call(functools.partial(weight_kernel, places, chunks, n), out_s...  45.7 us
    pallas_call x3, Pallas kernels, partial_sums(): pl.pallas_call(partial_kernel, out_shape=(out, out), grid=(count,), in_sp...  45.6 us
    ppermute x2, waiting for transfers between devices, doubled(): held[j ^ bit] = lax.ppermute(held[j], 'row', pairs)  21.5 us
    unnamed x56, local copies, waits for them, and re-layouts  15.7 us
    ppermute x16, waiting for transfers between devices, flip(): return lax.ppermute(x, 'col', [(i, i ^ bits[i & 1]) for i in range(n)])  14.2 us
    ppermute x16, starting transfers between devices, flip(): return lax.ppermute(x, 'col', [(i, i ^ bits[i & 1]) for i in range(n)])  13.1 us
    pallas_call x5, Pallas kernels, sums(): pl.pallas_call(functools.partial(sums_kernel, layout, len(ended)), out_sh...  8.55 us
    ppermute x2, starting transfers between devices, doubled(): held[j ^ bit] = lax.ppermute(held[j], 'row', pairs)  5.39 us
  transfers between devices with their start and end apart: 22, of which 5 were waited for; matrix products, arithmetic and copies ran while one was open for 2% of the time, Pallas kernels for 53%

profile of v5, /device:TPU:0, one launch (start us, length us, event | category | flops | bytes accessed | tf_op | source)
XLA Modules:
  0.0 188.8 jit_solution(18107525880217828162)
XLA Ops:
  0.6 3.0 %collective-permute-start.1 = (bf16[128,6656]{1,0:T(8,128)(2,1)}, bf16[128,6656]{1,0:T(8,128)(2,1)S(1)}, u32[]{:S(2)}, u32[]{:S(2)}) collective-permute-start(bf16[128,6656]{1,0:T(8,128)(2,1)} %refs_0_.5), channel_id=1, source_target_pairs={{0,4},{1,5},{2,6},{3,7},{4,0},{5,1},{6,2},{7,3},{8,12},{9,13},{10,... | collective-permute-start | bytes 5111816 | tf_op jit(solution)/shard_map/ppermute | solution.py:27
  3.7 1.5 collective-permute-start
  5.2 1.9 slice.8
  7.0 2.6 %collective-permute-start.7 = (bf16[128,2048]{1,0:T(8,128)(2,1)}, bf16[128,2048]{1,0:T(8,128)(2,1)}, u32[]{:S(2)}, u32[]{:S(2)}) collective-permute-start(bf16[128,2048]{1,0:T(8,128)(2,1)} %bitcast.3.refs_0_), channel_id=1, source_target_pairs={{0,16},{8,24},{16,0},{24,8},{1,17},{9,25},{17,1},{25,9},{2,18},{10... | collective-permute-start | bytes 1572872 | tf_op jit(solution)/shard_map/ppermute | solution.py:35
  9.6 1.6 collective-permute-start.8
  11.2 21.5 %collective-permute-done.7.refs_1_ = bf16[128,2048]{1,0:T(8,128)(2,1)} collective-permute-done((bf16[128,2048]{1,0:T(8,128)(2,1)}, bf16[128,2048]{1,0:T(8,128)(2,1)}, u32[]{:S(2)}, u32[]{:S(2)}) %collective-permute-start.7) | collective-permute-done | bytes 524320 | tf_op jit(solution)/shard_map/ppermute | solution.py:35
  32.7 0.6 collective-permute-start.9
  33.3 7.8 %collective-permute-done.1.refs_5_.refs_2_ = bf16[128,6656]{1,0:T(8,128)(2,1)S(1)} collective-permute-done((bf16[128,6656]{1,0:T(8,128)(2,1)}, bf16[128,6656]{1,0:T(8,128)(2,1)S(1)}, u32[]{:S(2)}, u32[]{:S(2)}) %collective-permute-start.1) | collective-permute-done | bytes 1703968 | tf_op jit(solution)/shard_map/ppermute | solution.py:27
  41.1 1.5 collective-permute-done.refs_4_.refs_1_
  42.5 1.4 broadcast_select_fusion
  44.3 1.1 slice.7
  45.4 2.8 %collective-permute-start.11 = (bf16[128,2048]{1,0:T(8,128)(2,1)S(1)}, bf16[128,2048]{1,0:T(8,128)(2,1)S(1)}, u32[]{:S(2)}, u32[]{:S(2)}) collective-permute-start(bf16[128,2048]{1,0:T(8,128)(2,1)S(1)} %bitcast.5), channel_id=1, source_target_pairs={{0,16},{8,24},{16,0},{24,8},{1,17},{9,25},{17,1},{25,9},{2,18},{10... | collective-permute-start | bytes 1572872 | tf_op jit(solution)/shard_map/ppermute | solution.py:35
  48.2 1.6 collective-permute-start.10
  49.8 2.7 %assemble.2 = (bf16[512,2048]{1,0:T(8,128)(2,1)S(1)}, bf16[2048,512]{1,0:T(8,128)(2,1)S(1)}) custom-call(s32[2]{0:T(128)S(1)} %pad_add_fusion.where_ref, bf16[128,2048]{1,0:T(8,128)(2,1)} %bitcast.3.refs_0_, bf16[128,2048]{1,0:T(8,128)(2,1)} %collective-permute-done.7.refs_1_, bf16[128,2048]{1,0:T(8,128)(2,1)} %collective-permute-done.8.refs_2_, ...), custom_call_target="tpu_custom_call" | custom-call | bytes 6291456 | tf_op jit(solution)/shard_map/assemble/pallas_call | solution.py:56
  52.6 1.4 copy-done.2
  53.9 20.9 %partial_sums.3 = (bf16[4,64,6656]{2,1,0:T(8,128)(2,1)S(1)}, bf16[4,64,6656]{2,1,0:T(8,128)(2,1)S(1)}) custom-call(bf16[6656,2048]{1,0:T(8,128)(2,1)} %w_ref.5, bf16[2048,512]{1,0:T(8,128)(2,1)S(1)} %get-tuple-element.26.g_ref), custom_call_target="tpu_custom_call" | custom-call | flops 13958643712 | bytes 36175872 | tf_op jit(solution)/shard_map/partial_sums/pallas_call | solution.py:90
  74.9 0.5 collective-permute-start.12
  76.0 4.9 %collective-permute-done.13.refs_1_.refs_7_ = bf16[4,64,6656]{2,1,0:T(8,128)(2,1)S(1)} collective-permute-done((bf16[4,64,6656]{2,1,0:T(8,128)(2,1)S(1)}, bf16[4,64,6656]{2,1,0:T(8,128)(2,1)S(1)}, u32[]{:S(2)}, u32[]{:S(2)}) %collective-permute-start.13) | collective-permute-done | bytes 3407904 | tf_op jit(solution)/shard_map/ppermute | solution.py:27
  80.9 0.8 sums.5.refs_4_.refs_0_
  81.7 1.0 copy-done.1
  82.7 1.5 collective-permute-start.15
  84.2 5.1 %collective-permute-done.12.refs_3_ = bf16[128,2048]{1,0:T(8,128)(2,1)S(1)} collective-permute-done((bf16[128,2048]{1,0:T(8,128)(2,1)S(1)}, bf16[128,2048]{1,0:T(8,128)(2,1)S(1)}, u32[]{:S(2)}, u32[]{:S(2)}) %collective-permute-start.12) | collective-permute-done | bytes 524320 | tf_op jit(solution)/shard_map/ppermute | solution.py:305
  89.3 1.7 assemble.3
  91.0 1.3 copy-done.3
  92.3 13.5 %partial_sums.4 = (bf16[4,64,3584]{2,1,0:T(8,128)(2,1)}, bf16[4,64,3584]{2,1,0:T(8,128)(2,1)S(1)}) custom-call(bf16[6656,2048]{1,0:T(8,128)(2,1)} %w_ref.5, bf16[2048,512]{1,0:T(8,128)(2,1)S(1)} %get-tuple-element.34.g_ref, bf16[2,64,6656]{2,1,0:T(8,128)(2,1)S(1)} %sums.5.refs_4_.refs_0_), custom_call_target="tpu_custom_call" | custom-call | flops 7516192768 | bytes 20447232 | tf_op jit(solution)/shard_map/partial_sums/pallas_call | solution.py:90
  105.9 0.5 collective-permute-start.5
  106.4 0.5 collective-permute-start.6
  106.9 1.6 copy-done.16
  108.5 11.2 %partial_sums.5 = (bf16[4,64,3072]{2,1,0:T(8,128)(2,1)}, bf16[4,64,3072]{2,1,0:T(8,128)(2,1)S(1)}) custom-call(bf16[6656,2048]{1,0:T(8,128)(2,1)} %w_ref.5, bf16[2048,512]{1,0:T(8,128)(2,1)S(1)} %copy-done.16, bf16[4,64,3584]{2,1,0:T(8,128)(2,1)} %get-tuple-element.36.refs_0_), custom_call_target="tpu_custom_call" | custom-call | flops 6442450944 | bytes 17825792 | tf_op jit(solution)/shard_map/partial_sums/pallas_call | solution.py:90
  119.7 1.2 copy-done.10
  120.9 3.2 %sums.6 = (bf16[1,64,6656]{2,1,0:T(8,128)(2,1)}, bf16[2,64,3584]{2,1,0:T(8,128)(2,1)}) custom-call(bf16[4,64,6656]{2,1,0:T(8,128)(2,1)S(1)} %get-tuple-element.31.refs_0_.refs_6_, bf16[4,64,6656]{2,1,0:T(8,128)(2,1)} %copy-done.1, bf16[2,64,6656]{2,1,0:T(8,128)(2,1)} %collective-permute-done.15.refs_2_.refs_8_, ...), custom_call_target="tpu_custom_call" | custom-call | flops 3080192 | bytes 6160384 | tf_op jit(solution)/shard_map/sums/pallas_call | solution.py:214
  124.0 1.5 collective-permute-start.19
  125.6 1.5 collective-permute-start.16
  127.0 1.2 copy-done.6
  128.2 1.5 copy-done.7
  129.7 9.3 %weight_rows.3.refs_2_.refs_11_ = bf16[6656,2048]{1,0:T(8,128)(2,1)} custom-call(s32[2]{0:T(128)S(1)} %pad_add_fusion.where_ref, bf16[128,6656]{1,0:T(8,128)(2,1)} %refs_0_.5, bf16[128,6656]{1,0:T(8,128)(2,1)S(1)} %collective-permute-done.refs_4_.refs_1_, bf16[128,6656]{1,0:T(8,128)(2,1)S(1)} %collective-permute-done.1.refs_5_.refs_2_, ...), custom_call_target="tpu_custom_call" | custom-call | flops 4294967296 | bytes 10485760 | tf_op jit(solution)/shard_map/weight_rows/pallas_call | solution.py:142
  139.0 1.1 copy-done.12
  140.2 1.4 copy-done.13
  142.0 0.6 collective-permute-start.18
  143.0 19.4 %weight_rows.4.refs_10_.refs_11_ = bf16[6656,2048]{1,0:T(8,128)(2,1)} custom-call(s32[2]{0:T(128)S(1)} %pad_add_fusion.where_ref, bf16[128,6656]{1,0:T(8,128)(2,1)} %refs_0_.5, bf16[128,6656]{1,0:T(8,128)(2,1)S(1)} %collective-permute-done.refs_4_.refs_1_, ...), custom_call_target="tpu_custom_call", output_to_operand_aliasing={{}: (12, {})} | custom-call | flops 12884901888 | bytes 23068672 | tf_op jit(solution)/shard_map/weight_rows/pallas_call | solution.py:142
  162.5 0.9 copy-done.17
  163.5 1.2 copy-done.18
  164.7 3.0 %sums.8 = (bf16[1,64,3584]{2,1,0:T(8,128)(2,1)S(1)}, bf16[1,64,3072]{2,1,0:T(8,128)(2,1)S(1)}, bf16[128,6656]{1,0:T(8,128)(2,1)}) custom-call(bf16[4,64,3584]{2,1,0:T(8,128)(2,1)S(1)} %get-tuple-element.35.refs_3_.refs_0_, bf16[4,64,3584]{2,1,0:T(8,128)(2,1)S(1)} %copy-done.5, bf16[2,64,3584]{2,1,0:T(8,128)(2,1)S(1)} %copy-done.18, ...), custom_call_target="tpu_custom_call" | custom-call | flops 3833856 | bytes 7667712 | tf_op jit(solution)/shard_map/sums/pallas_call | solution.py:214
  167.6 0.9 copy-done.20
  168.6 0.5 collective-permute-start.21
  169.1 1.5 collective-permute-start.20
  170.6 16.9 %weight_rows.5.refs_8_ = bf16[6656,2048]{1,0:T(8,128)(2,1)} custom-call(s32[2]{0:T(128)S(1)} %pad_add_fusion.where_ref, bf16[128,6656]{1,0:T(8,128)(2,1)} %refs_0_.5, bf16[128,6656]{1,0:T(8,128)(2,1)S(1)} %collective-permute-done.refs_4_.refs_1_, bf16[128,6656]{1,0:T(8,128)(2,1)S(1)} %collective-permute-done.1.refs_5_.refs_2_, ...), custom_call_target="tpu_custom_call", output_to_operand_aliasing={{}: (12, {})} | custom-call | flops 10737418240 | bytes 19922944 | tf_op jit(solution)/shard_map/weight_rows/pallas_call | solution.py:142
  187.6 1.2 sums.9
  (70 shorter events, 2.0 us)
Async XLA Ops:
  0.6 40.4 %collective-permute-start.1 = (bf16[128,6656]{1,0:T(8,128)(2,1)}, bf16[128,6656]{1,0:T(8,128)(2,1)S(1)}, u32[]{:S(2)}, u32[]{:S(2)}) collective-permute-start(bf16[128,6656]{1,0:T(8,128)(2,1)} %refs_0_.5), channel_id=1, source_target_pairs={{0,4},{1,5},{2,6},{3,7},{4,0},{5,1},{6,2},{7,3},{8,12},{9,13},{10,... | collective-permute-start | bytes 5111816 | tf_op jit(solution)/shard_map/ppermute | solution.py:27
  3.7 38.9 %collective-permute-start = (bf16[128,6656]{1,0:T(8,128)(2,1)}, bf16[128,6656]{1,0:T(8,128)(2,1)S(1)}, u32[]{:S(2)}, u32[]{:S(2)}) collective-permute-start(bf16[128,6656]{1,0:T(8,128)(2,1)} %refs_0_.5), channel_id=1, source_target_pairs={{0,2},{1,3},{2,0},{3,1},{4,6},{5,7},{6,4},{7,5},{8,10},{9,11},{10,... | collective-permute-start | bytes 5111816 | tf_op jit(solution)/shard_map/ppermute | solution.py:27
  7.0 25.7 %collective-permute-start.7 = (bf16[128,2048]{1,0:T(8,128)(2,1)}, bf16[128,2048]{1,0:T(8,128)(2,1)}, u32[]{:S(2)}, u32[]{:S(2)}) collective-permute-start(bf16[128,2048]{1,0:T(8,128)(2,1)} %bitcast.3.refs_0_), channel_id=1, source_target_pairs={{0,16},{8,24},{16,0},{24,8},{1,17},{9,25},{17,1},{25,9},{2,18},{10... | collective-permute-start | bytes 1572872 | tf_op jit(solution)/shard_map/ppermute | solution.py:35
  9.6 38.6 %collective-permute-start.8 = (bf16[128,2048]{1,0:T(8,128)(2,1)}, bf16[128,2048]{1,0:T(8,128)(2,1)}, u32[]{:S(2)}, u32[]{:S(2)}) collective-permute-start(bf16[128,2048]{1,0:T(8,128)(2,1)} %bitcast.3.refs_0_), channel_id=1, source_target_pairs={{0,8},{8,0},{16,24},{24,16},{1,9},{9,1},{17,25},{25,17},{2,10},{10... | collective-permute-start | bytes 1572872 | tf_op jit(solution)/shard_map/ppermute | solution.py:301
  32.7 17.1 %collective-permute-start.9 = (bf16[128,2048]{1,0:T(8,128)(2,1)}, bf16[128,2048]{1,0:T(8,128)(2,1)}, u32[]{:S(2)}, u32[]{:S(2)}) collective-permute-start(bf16[128,2048]{1,0:T(8,128)(2,1)} %collective-permute-done.7.refs_1_), channel_id=1, source_target_pairs={{0,8},{8,0},{16,24},{24,16},{1,9},{9,1},{17,25},{25,17},{2,10},{10... | collective-permute-start | bytes 1572872 | tf_op jit(solution)/shard_map/ppermute | solution.py:305
  43.9 31.6 %collective-permute-start.2 = (bf16[128,6656]{1,0:T(8,128)(2,1)}, bf16[128,6656]{1,0:T(8,128)(2,1)}, u32[]{:S(2)}, u32[]{:S(2)}) collective-permute-start(bf16[128,6656]{1,0:T(8,128)(2,1)} %broadcast_select_fusion), channel_id=1, source_target_pairs={{0,4},{1,3},{2,6},{3,1},{4,0},{5,7},{6,2},{7,5},{8,12},{9,11},{10,... | collective-permute-start | bytes 5111816 | tf_op jit(solution)/shard_map/ppermute | solution.py:27
  44.3 39.9 %collective-permute-start.3 = (bf16[128,6656]{1,0:T(8,128)(2,1)}, bf16[128,6656]{1,0:T(8,128)(2,1)}, u32[]{:S(2)}, u32[]{:S(2)}) collective-permute-start(bf16[128,6656]{1,0:T(8,128)(2,1)} %refs_0_.5), channel_id=1, source_target_pairs={{0,1},{1,0},{2,3},{3,2},{4,5},{5,4},{6,7},{7,6},{8,9},{9,8},{10,11... | collective-permute-start | bytes 5111816 | tf_op jit(solution)/shard_map/ppermute | solution.py:27
  45.4 7.1 %copy-start.22 = (bf16[2,64,2048]{2,1,0:T(8,128)(2,1)}, bf16[2,64,2048]{2,1,0:T(8,128)(2,1)S(1)}, u32[]{:S(2)}) copy-start(bf16[2,64,2048]{2,1,0:T(8,128)(2,1)S(1)} %slice.7) | copy-start | bytes 1572868
  45.4 29.5 %collective-permute-start.11 = (bf16[128,2048]{1,0:T(8,128)(2,1)S(1)}, bf16[128,2048]{1,0:T(8,128)(2,1)S(1)}, u32[]{:S(2)}, u32[]{:S(2)}) collective-permute-start(bf16[128,2048]{1,0:T(8,128)(2,1)S(1)} %bitcast.5), channel_id=1, source_target_pairs={{0,16},{8,24},{16,0},{24,8},{1,17},{9,25},{17,1},{25,9},{2,18},{10... | collective-permute-start | bytes 1572872 | tf_op jit(solution)/shard_map/ppermute | solution.py:35
  48.2 26.7 %collective-permute-start.10 = (bf16[128,2048]{1,0:T(8,128)(2,1)S(1)}, bf16[128,2048]{1,0:T(8,128)(2,1)S(1)}, u32[]{:S(2)}, u32[]{:S(2)}) collective-permute-start(bf16[128,2048]{1,0:T(8,128)(2,1)S(1)} %bitcast.6), channel_id=1, source_target_pairs={{0,8},{8,0},{16,24},{24,16},{1,9},{9,1},{17,25},{25,17},{2,10},{10... | collective-permute-start | bytes 1572872 | tf_op jit(solution)/shard_map/ppermute | solution.py:301
  52.6 1.4 copy-start.2
  74.8 46.0 %copy-start = (bf16[4,64,6656]{2,1,0:T(8,128)(2,1)}, bf16[4,64,6656]{2,1,0:T(8,128)(2,1)S(1)}, u32[]{:S(2)}) copy-start(bf16[4,64,6656]{2,1,0:T(8,128)(2,1)S(1)} %get-tuple-element.31.refs_0_.refs_6_) | copy-start | bytes 10223620
  74.8 6.1 %collective-permute-start.13 = (bf16[4,64,6656]{2,1,0:T(8,128)(2,1)S(1)}, bf16[4,64,6656]{2,1,0:T(8,128)(2,1)S(1)}, u32[]{:S(2)}, u32[]{:S(2)}) collective-permute-start(bf16[4,64,6656]{2,1,0:T(8,128)(2,1)S(1)} %get-tuple-element.32.refs_0_), channel_id=1, source_target_pairs={{0,1},{1,0},{2,3},{3,2},{4,5},{5,4},{6,7},{7,6},{8,9},{9,8},{10,11... | collective-permute-start | bytes 10223624 | tf_op jit(solution)/shard_map/ppermute | solution.py:27
  74.9 1.1 copy-start.26
  74.9 14.4 %collective-permute-start.12 = (bf16[128,2048]{1,0:T(8,128)(2,1)S(1)}, bf16[128,2048]{1,0:T(8,128)(2,1)S(1)}, u32[]{:S(2)}, u32[]{:S(2)}) collective-permute-start(bf16[128,2048]{1,0:T(8,128)(2,1)S(1)} %collective-permute-done.11.refs_2_), channel_id=1, source_target_pairs={{0,8},{8,0},{16,24},{24,16},{1,9},{9,1},{17,25},{25,17},{2,10},{10... | collective-permute-start | bytes 1572872 | tf_op jit(solution)/shard_map/ppermute | solution.py:305
  80.9 1.8 copy-start.1
  80.9 8.4 %copy-start.23 = (bf16[2,64,2048]{2,1,0:T(8,128)(2,1)S(1)}, bf16[2,64,2048]{2,1,0:T(8,128)(2,1)}, u32[]{:S(2)}) copy-start(bf16[2,64,2048]{2,1,0:T(8,128)(2,1)} %copy-done.22) | copy-start | bytes 1572868
  80.9 8.4 %copy-start.25 = (bf16[128,2048]{1,0:T(8,128)(2,1)S(1)}, bf16[128,2048]{1,0:T(8,128)(2,1)}, u32[]{:S(2)}) copy-start(bf16[128,2048]{1,0:T(8,128)(2,1)} %copy-done.24) | copy-start | bytes 1572868
  80.9 8.4 %copy-start.27 = (bf16[128,2048]{1,0:T(8,128)(2,1)S(1)}, bf16[128,2048]{1,0:T(8,128)(2,1)}, u32[]{:S(2)}) copy-start(bf16[128,2048]{1,0:T(8,128)(2,1)} %copy-done.26) | copy-start | bytes 1572868
  82.7 38.2 %collective-permute-start.15 = (bf16[2,64,6656]{2,1,0:T(8,128)(2,1)S(1)}, bf16[2,64,6656]{2,1,0:T(8,128)(2,1)}, u32[]{:S(2)}, u32[]{:S(2)}) collective-permute-start(bf16[2,64,6656]{2,1,0:T(8,128)(2,1)S(1)} %sums.5.refs_4_.refs_0_), channel_id=1, source_target_pairs={{0,2},{1,5},{2,0},{3,7},{4,6},{5,1},{6,4},{7,3},{8,10},{9,13},{10,... | collective-permute-start | bytes 5111816 | tf_op jit(solution)/shard_map/ppermute | solution.py:27
  91.0 1.3 copy-start.3
  92.3 13.6 %copy-start.15 = (bf16[2048,512]{1,0:T(8,128)(2,1)}, bf16[2048,512]{1,0:T(8,128)(2,1)S(1)}, u32[]{:S(2)}) copy-start(bf16[2048,512]{1,0:T(8,128)(2,1)S(1)} %get-tuple-element.34.g_ref) | copy-start | bytes 6291460
  105.9 15.0 %collective-permute-start.14 = (bf16[4,64,3584]{2,1,0:T(8,128)(2,1)}, bf16[4,64,3584]{2,1,0:T(8,128)(2,1)S(1)}, u32[]{:S(2)}, u32[]{:S(2)}) collective-permute-start(bf16[4,64,3584]{2,1,0:T(8,128)(2,1)} %get-tuple-element.36.refs_0_), channel_id=1, source_target_pairs={{0,1},{1,0},{2,3},{3,2},{4,5},{5,4},{6,7},{7,6},{8,9},{9,8},{10,11... | collective-permute-start | bytes 5505032 | tf_op jit(solution)/shard_map/ppermute | solution.py:27
  105.9 19.7 %collective-permute-start.5 = (bf16[128,6656]{1,0:T(8,128)(2,1)S(1)}, bf16[128,6656]{1,0:T(8,128)(2,1)S(1)}, u32[]{:S(2)}, u32[]{:S(2)}) collective-permute-start(bf16[128,6656]{1,0:T(8,128)(2,1)S(1)} %collective-permute-done.1.refs_5_.refs_2_), channel_id=1, source_target_pairs={{0,1},{1,0},{2,3},{3,2},{4,5},{5,4},{6,7},{7,6},{8,9},{9,8},{10,11... | collective-permute-start | bytes 5111816 | tf_op jit(solution)/shard_map/ppermute | solution.py:27
  106.4 20.7 %collective-permute-start.4 = (bf16[128,6656]{1,0:T(8,128)(2,1)S(1)}, bf16[128,6656]{1,0:T(8,128)(2,1)S(1)}, u32[]{:S(2)}, u32[]{:S(2)}) collective-permute-start(bf16[128,6656]{1,0:T(8,128)(2,1)S(1)} %collective-permute-done.refs_4_.refs_1_), channel_id=1, source_target_pairs={{0,1},{1,0},{2,3},{3,2},{4,5},{5,4},{6,7},{7,6},{8,9},{9,8},{10,11... | collective-permute-start | bytes 5111816 | tf_op jit(solution)/shard_map/ppermute | solution.py:27
  106.4 21.9 %collective-permute-start.6 = (bf16[128,6656]{1,0:T(8,128)(2,1)}, bf16[128,6656]{1,0:T(8,128)(2,1)}, u32[]{:S(2)}, u32[]{:S(2)}) collective-permute-start(bf16[128,6656]{1,0:T(8,128)(2,1)} %collective-permute-done.2.refs_3_), channel_id=1, source_target_pairs={{0,1},{1,0},{2,3},{3,2},{4,5},{5,4},{6,7},{7,6},{8,9},{9,8},{10,11... | collective-permute-start | bytes 5111816 | tf_op jit(solution)/shard_map/ppermute | solution.py:27
  106.9 1.6 copy-start.16
  119.7 1.2 copy-start.10
  120.8 18.2 %collective-permute-start.17 = (bf16[4,64,3072]{2,1,0:T(8,128)(2,1)}, bf16[4,64,3072]{2,1,0:T(8,128)(2,1)S(1)}, u32[]{:S(2)}, u32[]{:S(2)}) collective-permute-start(bf16[4,64,3072]{2,1,0:T(8,128)(2,1)} %get-tuple-element.37.refs_5_), channel_id=1, source_target_pairs={{0,1},{1,0},{2,3},{3,2},{4,5},{5,4},{6,7},{7,6},{8,9},{9,8},{10,11... | collective-permute-start | bytes 4718600 | tf_op jit(solution)/shard_map/ppermute | solution.py:27
  120.8 3.2 %copy-start.4 = (bf16[4,64,3584]{2,1,0:T(8,128)(2,1)}, bf16[4,64,3584]{2,1,0:T(8,128)(2,1)S(1)}, u32[]{:S(2)}) copy-start(bf16[4,64,3584]{2,1,0:T(8,128)(2,1)S(1)} %collective-permute-done.14.refs_4_.refs_1_) | copy-start | bytes 5505028
  124.0 38.5 %collective-permute-start.19 = (bf16[1,64,6656]{2,1,0:T(8,128)(2,1)}, bf16[1,64,6656]{2,1,0:T(8,128)(2,1)}, u32[]{:S(2)}, u32[]{:S(2)}) collective-permute-start(bf16[1,64,6656]{2,1,0:T(8,128)(2,1)} %get-tuple-element.40.refs_10_), channel_id=1, source_target_pairs={{0,4},{1,3},{2,6},{3,1},{4,0},{5,7},{6,2},{7,5},{8,12},{9,11},{10,... | collective-permute-start | bytes 2555912 | tf_op jit(solution)/shard_map/ppermute | solution.py:27
  125.6 37.0 %collective-permute-start.16 = (bf16[2,64,3584]{2,1,0:T(8,128)(2,1)}, bf16[2,64,3584]{2,1,0:T(8,128)(2,1)S(1)}, u32[]{:S(2)}, u32[]{:S(2)}) collective-permute-start(bf16[2,64,3584]{2,1,0:T(8,128)(2,1)} %get-tuple-element.38), channel_id=1, source_target_pairs={{0,2},{1,5},{2,0},{3,7},{4,6},{5,1},{6,4},{7,3},{8,10},{9,13},{10,... | collective-permute-start | bytes 2752520 | tf_op jit(solution)/shard_map/ppermute | solution.py:27
  127.0 1.2 copy-start.6
  128.2 1.5 copy-start.7
  129.7 10.5 %copy-start.11 = (bf16[4,64,3072]{2,1,0:T(8,128)(2,1)S(1)}, bf16[4,64,3072]{2,1,0:T(8,128)(2,1)}, u32[]{:S(2)}) copy-start(bf16[4,64,3072]{2,1,0:T(8,128)(2,1)} %copy-done.10) | copy-start | bytes 4718596
  139.0 1.1 copy-start.12
  140.2 1.4 copy-start.13
  141.6 1.5 copy-start.8
  142.0 21.5 %copy-start.5 = (bf16[4,64,3584]{2,1,0:T(8,128)(2,1)S(1)}, bf16[4,64,3584]{2,1,0:T(8,128)(2,1)}, u32[]{:S(2)}) copy-start(bf16[4,64,3584]{2,1,0:T(8,128)(2,1)} %copy-done.4) | copy-start | bytes 5505028
  142.0 21.5 %copy-start.14 = (bf16[4,64,3072]{2,1,0:T(8,128)(2,1)S(1)}, bf16[4,64,3072]{2,1,0:T(8,128)(2,1)}, u32[]{:S(2)}) copy-start(bf16[4,64,3072]{2,1,0:T(8,128)(2,1)} %copy-done.12) | copy-start | bytes 4718596
  142.0 20.5 %collective-permute-start.18 = (bf16[2,64,3072]{2,1,0:T(8,128)(2,1)S(1)}, bf16[2,64,3072]{2,1,0:T(8,128)(2,1)S(1)}, u32[]{:S(2)}, u32[]{:S(2)}) collective-permute-start(bf16[2,64,3072]{2,1,0:T(8,128)(2,1)S(1)} %sums.7.refs_10_), channel_id=1, source_target_pairs={{0,2},{1,5},{2,0},{3,7},{4,6},{5,1},{6,4},{7,3},{8,10},{9,13},{10,... | collective-permute-start | bytes 2359304 | tf_op jit(solution)/shard_map/ppermute | solution.py:27
  162.5 8.1 %copy-start.9 = (bf16[128,6656]{1,0:T(8,128)(2,1)S(1)}, bf16[128,6656]{1,0:T(8,128)(2,1)}, u32[]{:S(2)}) copy-start(bf16[128,6656]{1,0:T(8,128)(2,1)} %copy-done.6) | copy-start | bytes 5111812
  162.5 1.0 copy-start.17
  163.5 1.2 copy-start.18
  168.6 19.0 %collective-permute-start.21 = (bf16[1,64,3072]{2,1,0:T(8,128)(2,1)S(1)}, bf16[1,64,3072]{2,1,0:T(8,128)(2,1)S(1)}, u32[]{:S(2)}, u32[]{:S(2)}) collective-permute-start(bf16[1,64,3072]{2,1,0:T(8,128)(2,1)S(1)} %get-tuple-element.42), channel_id=1, source_target_pairs={{0,4},{1,3},{2,6},{3,1},{4,0},{5,7},{6,2},{7,5},{8,12},{9,11},{10,... | collective-permute-start | bytes 1179656 | tf_op jit(solution)/shard_map/ppermute | solution.py:27
  169.1 18.4 %copy-start.19 = (bf16[2,64,3584]{2,1,0:T(8,128)(2,1)S(1)}, bf16[2,64,3584]{2,1,0:T(8,128)(2,1)}, u32[]{:S(2)}) copy-start(bf16[2,64,3584]{2,1,0:T(8,128)(2,1)} %copy-done.17) | copy-start | bytes 2752516
  169.1 18.5 %copy-start.21 = (bf16[2,64,3072]{2,1,0:T(8,128)(2,1)S(1)}, bf16[2,64,3072]{2,1,0:T(8,128)(2,1)}, u32[]{:S(2)}) copy-start(bf16[2,64,3072]{2,1,0:T(8,128)(2,1)} %copy-done.20) | copy-start | bytes 2359300
  169.1 18.4 %collective-permute-start.20 = (bf16[1,64,3584]{2,1,0:T(8,128)(2,1)S(1)}, bf16[1,64,3584]{2,1,0:T(8,128)(2,1)S(1)}, u32[]{:S(2)}, u32[]{:S(2)}) collective-permute-start(bf16[1,64,3584]{2,1,0:T(8,128)(2,1)S(1)} %get-tuple-element.41.refs_10_), channel_id=1, source_target_pairs={{0,4},{1,3},{2,6},{3,1},{4,0},{5,7},{6,2},{7,5},{8,12},{9,11},{10,... | collective-permute-start | bytes 1376264 | tf_op jit(solution)/shard_map/ppermute | solution.py:27
  (2 other events, 1.9 us)

commit v6 on v5

--- a/solution.py
+++ b/solution.py
@@ -9,7 +9,7 @@
 
 F32, BF16 = jnp.float32, jnp.bfloat16
 ANYWHERE = pl.BlockSpec(memory_space=pl.ANY)
-PARAMS = pltpu.CompilerParams(vmem_limit_bytes=40 * 1024 * 1024)
+PARAMS = pltpu.CompilerParams(vmem_limit_bytes=60 * 1024 * 1024)
 
 
 def cost(flops, values):
@@ -277,9 +277,9 @@
     orders = [[o ^ 1 for o in kept[1 - h]] + kept[h] for h in (0, 1)]
     c = tokens // 2
     chunks = [(0, c), (c, c)]
-    tile = 128 * max(d for d in (1, 2, 4) if units % (128 * d) == 0)
+    lanes = units // 128
+    tile, wide = (128 * max(d for d in range(1, most + 1) if lanes % d == 0) for most in (4, 13))
     tiles = units // tile
-    cut = (tiles + 1) // 2
     col, row = lax.axis_index("col"), lax.axis_index("row")
     where = jnp.stack([col, row]).astype(jnp.int32)
 
@@ -324,10 +324,12 @@
     corners = [((j0, j1), a) for (j0, j1), a in corners if j0 not in whole]
 
     def partials(turned, first, count, after):
-        send, keep = partial_sums(turned, down_weight, n_col, c, tile, first, count, after)
+        send, keep = partial_sums(turned, down_weight, n_col, c, wide, first, count, after)
         return send, keep, [send]
 
-    send, keep, after = partials(turned0, 0, tiles, [])
+    count = units // wide
+    cut = (count + 1) // 2
+    send, keep, after = partials(turned0, 0, count, [])
     zero = Halving([send], [keep], levels, n_col)
 
     second, tied = lax.optimization_barrier((second, after[0]))
@@ -359,19 +361,22 @@
     exchanged = [a for _, a in pieces[n_col // 2 :]]
     grads1, turned1 = assemble(where, second, orders, c, after + exchanged[:1])
     grads = [grads0, grads1]
-    send_a, keep_a, after = partials(turned1, 0, cut, after)
-    a1 = Halving([send_a], [keep_a], levels, n_col)
-    send_b, keep_b, after = partials(turned1, cut, tiles - cut, after)
-    b1 = Halving([send_b], [keep_b], levels, n_col)
-    after = advance([zero, a1], [], 0, after)
-    after = work(2, after)
-    after = advance([b1], [], 0, after)
-    parts, steps = [zero, a1, b1], len(levels) - 1
+    sends, keeps = [], []
+    for first, last in ((0, cut), (cut, count)):
+        if first < last:
+            send, keep, after = partials(turned1, first, last - first, after)
+            sends.append(send)
+            keeps.append(keep)
+    one = Halving(sends, keeps, levels, n_col)
+    after = work(3, after)
+    parts, steps = [zero, one], len(levels) - 1
     for step in range(steps):
-        after = work(-(-(tiles - done) // (steps - step)), after)
         going, ended = [p for p in parts if p.levels], [p for p in parts if not p.levels]
-        after = advance(going, ended, 0 if zero in ended else c, after)
+        after = advance(going, ended, 0, after)
         parts = going
+        left = tiles - done
+        after = work(left if step == steps - 1 else -(-left * 2 // 3), after)
+    advance([], [one], c, after)
     return weight_grad, hidden_grad
 
 

time: 190 us -> 192 us (1.011)
  local copies, waits for them, and re-layouts: 18.7 us -> 7.5 us
  Pallas kernels: 104 us -> 114 us
  waiting for transfers between devices: 40.8 us -> 45.3 us
    unnamed x56 -> x20, local copies, waits for them, and re-layouts: 15.7 us -> 4.54 us
    ppermute x16 -> x14, waiting for transfers between devices: 14.2 us -> 20.3 us  [flip(): return lax.ppermute(x, 'col', [(i, i ^ bits[i & 1]) for i in range(n)])]
    pallas_call x5 -> x4, Pallas kernels: 8.55 us -> 13.9 us  [sums(): pl.pallas_call(functools.partial(sums_kernel, layout, len(ended)), out_sh...]
    pallas_call x2, Pallas kernels: 4.39 us -> 8.47 us  [assemble(): pl.pallas_call(functools.partial(assemble_kernel, rows_of, orders, c), ou...]
    ppermute x16 -> x14, starting transfers between devices: 13.1 us -> 11.6 us  [flip(): return lax.ppermute(x, 'col', [(i, i ^ bits[i & 1]) for i in range(n)])]
  transfers between devices with their start and end apart: 22 -> 20, of which waited for: 5 -> 6; matrix products, arithmetic and copies ran while one was open for 2% -> 3% of each run, Pallas kernels for 53% -> 54%
where the time goes in v6:
time: 192 us; the launch traced here: 191 us
  Pallas kernels  114 us (59%)
  waiting for transfers between devices  45.3 us (24%)
  starting transfers between devices  21 us (11%)
  local copies, waits for them, and re-layouts  7.5 us (4%)
  other arithmetic  2.13 us (1%)
    pallas_call x3, Pallas kernels, weight_rows(): pl.pallas_call(functools.partial(weight_kernel, places, chunks, n), out_s...  46.7 us
    pallas_call x3, Pallas kernels, partial_sums(): pl.pallas_call(partial_kernel, out_shape=(out, out), grid=(count,), in_sp...  44.7 us
    ppermute x2, waiting for transfers between devices, doubled(): held[j ^ bit] = lax.ppermute(held[j], 'row', pairs)  21.5 us
    ppermute x14, waiting for transfers between devices, flip(): return lax.ppermute(x, 'col', [(i, i ^ bits[i & 1]) for i in range(n)])  20.3 us
    pallas_call x4, Pallas kernels, sums(): pl.pallas_call(functools.partial(sums_kernel, layout, len(ended)), out_sh...  13.9 us
    ppermute x14, starting transfers between devices, flip(): return lax.ppermute(x, 'col', [(i, i ^ bits[i & 1]) for i in range(n)])  11.6 us
    pallas_call x2, Pallas kernels, assemble(): pl.pallas_call(functools.partial(assemble_kernel, rows_of, orders, c), ou...  8.47 us
    ppermute x2, starting transfers between devices, doubled(): held[j ^ bit] = lax.ppermute(held[j], 'row', pairs)  5.23 us
  transfers between devices with their start and end apart: 20, of which 6 were waited for; matrix products, arithmetic and copies ran while one was open for 3% of the time, Pallas kernels for 54%

profile of v6, /device:TPU:0, one launch (start us, length us, event | category | flops | bytes accessed | tf_op | source)
XLA Modules:
  0.0 191.2 jit_solution(6725481534957335572)
XLA Ops:
  0.6 3.0 %collective-permute-start.1 = (bf16[128,6656]{1,0:T(8,128)(2,1)}, bf16[128,6656]{1,0:T(8,128)(2,1)S(1)}, u32[]{:S(2)}, u32[]{:S(2)}) collective-permute-start(bf16[128,6656]{1,0:T(8,128)(2,1)} %refs_0_.5), channel_id=1, source_target_pairs={{0,4},{1,5},{2,6},{3,7},{4,0},{5,1},{6,2},{7,3},{8,12},{9,13},{10,... | collective-permute-start | bytes 5111816 | tf_op jit(solution)/shard_map/ppermute | solution.py:27
  3.7 1.5 collective-permute-start
  5.2 1.9 slice.8
  7.0 2.6 %collective-permute-start.7 = (bf16[128,2048]{1,0:T(8,128)(2,1)}, bf16[128,2048]{1,0:T(8,128)(2,1)}, u32[]{:S(2)}, u32[]{:S(2)}) collective-permute-start(bf16[128,2048]{1,0:T(8,128)(2,1)} %bitcast.3.refs_0_), channel_id=1, source_target_pairs={{0,16},{8,24},{16,0},{24,8},{1,17},{9,25},{17,1},{25,9},{2,18},{10... | collective-permute-start | bytes 1572872 | tf_op jit(solution)/shard_map/ppermute | solution.py:35
  9.6 1.6 collective-permute-start.8
  11.2 21.5 %collective-permute-done.7.refs_1_ = bf16[128,2048]{1,0:T(8,128)(2,1)} collective-permute-done((bf16[128,2048]{1,0:T(8,128)(2,1)}, bf16[128,2048]{1,0:T(8,128)(2,1)}, u32[]{:S(2)}, u32[]{:S(2)}) %collective-permute-start.7) | collective-permute-done | bytes 524320 | tf_op jit(solution)/shard_map/ppermute | solution.py:35
  32.7 0.6 collective-permute-start.9
  33.3 7.8 %collective-permute-done.1.refs_5_.refs_2_ = bf16[128,6656]{1,0:T(8,128)(2,1)S(1)} collective-permute-done((bf16[128,6656]{1,0:T(8,128)(2,1)}, bf16[128,6656]{1,0:T(8,128)(2,1)S(1)}, u32[]{:S(2)}, u32[]{:S(2)}) %collective-permute-start.1) | collective-permute-done | bytes 1703968 | tf_op jit(solution)/shard_map/ppermute | solution.py:27
  41.1 1.5 collective-permute-done.refs_4_.refs_1_
  42.5 1.5 broadcast_select_fusion
  44.0 0.3 copy-done.2
  44.3 0.8 collective-permute-start.2
  45.2 0.0 collective-permute-start.3
  45.2 0.6 pad_add_fusion.where_ref
  45.8 1.1 slice.7
  46.9 2.6 %collective-permute-start.11 = (bf16[128,2048]{1,0:T(8,128)(2,1)S(1)}, bf16[128,2048]{1,0:T(8,128)(2,1)}, u32[]{:S(2)}, u32[]{:S(2)}) collective-permute-start(bf16[128,2048]{1,0:T(8,128)(2,1)S(1)} %bitcast.5), channel_id=1, source_target_pairs={{0,16},{8,24},{16,0},{24,8},{1,17},{9,25},{17,1},{25,9},{2,18},{10... | collective-permute-start | bytes 1572872 | tf_op jit(solution)/shard_map/ppermute | solution.py:35
  49.6 0.0 collective-permute-done.8.refs_2_
  49.6 1.6 collective-permute-start.10
  51.1 4.3 %assemble.2 = (bf16[512,2048]{1,0:T(8,128)(2,1)}, bf16[2048,512]{1,0:T(8,128)(2,1)}) custom-call(s32[2]{0:T(128)} %pad_add_fusion.where_ref, bf16[128,2048]{1,0:T(8,128)(2,1)} %bitcast.3.refs_0_, bf16[128,2048]{1,0:T(8,128)(2,1)} %collective-permute-done.7.refs_1_, bf16[128,2048]{1,0:T(8,128)(2,1)} %collective-permute-done.8.refs_2_, ...), custom_call_target="tpu_custom_call" | custom-call | bytes 6291456 | tf_op jit(solution)/shard_map/assemble/pallas_call | solution.py:56
  55.4 20.0 %partial_sums.3 = (bf16[4,64,6656]{2,1,0:T(8,128)(2,1)}, bf16[4,64,6656]{2,1,0:T(8,128)(2,1)}) custom-call(bf16[6656,2048]{1,0:T(8,128)(2,1)} %w_ref.5, bf16[2048,512]{1,0:T(8,128)(2,1)} %get-tuple-element.25.g_ref), custom_call_target="tpu_custom_call" | custom-call | flops 13958643712 | bytes 36175872 | tf_op jit(solution)/shard_map/partial_sums/pallas_call | solution.py:90
  75.5 0.0 collective-permute-start.13
  75.5 0.5 collective-permute-start.12
  76.0 0.2 collective-permute-start.5
  76.2 0.3 collective-permute-start.4
  76.5 0.6 hold.1.refs_2_
  77.1 4.7 %collective-permute-done.13.refs_1_.refs_6_ = bf16[4,64,6656]{2,1,0:T(8,128)(2,1)} collective-permute-done((bf16[4,64,6656]{2,1,0:T(8,128)(2,1)}, bf16[4,64,6656]{2,1,0:T(8,128)(2,1)}, u32[]{:S(2)}, u32[]{:S(2)}) %collective-permute-start.13) | collective-permute-done | bytes 3407904 | tf_op jit(solution)/shard_map/ppermute | solution.py:27
  81.9 0.1 collective-permute-start.6
  82.0 3.0 %sums.4.refs_4_.refs_0_ = bf16[2,64,6656]{2,1,0:T(8,128)(2,1)} custom-call(bf16[4,64,6656]{2,1,0:T(8,128)(2,1)} %get-tuple-element.30.refs_0_.refs_5_, bf16[4,64,6656]{2,1,0:T(8,128)(2,1)} %collective-permute-done.13.refs_1_.refs_6_, f32[8,128]{1,0:T(8,128)} %hold.1.refs_2_), custom_call_target="tpu_custom_call" | custom-call | flops 2555904 | bytes 5111808 | tf_op jit(solution)/shard_map/sums/pallas_call | solution.py:214
  85.0 1.5 collective-permute-start.16
  86.5 3.5 %collective-permute-done.12.refs_3_ = bf16[128,2048]{1,0:T(8,128)(2,1)S(1)} collective-permute-done((bf16[128,2048]{1,0:T(8,128)(2,1)}, bf16[128,2048]{1,0:T(8,128)(2,1)S(1)}, u32[]{:S(2)}, u32[]{:S(2)}) %collective-permute-start.12) | collective-permute-done | bytes 524320 | tf_op jit(solution)/shard_map/ppermute | solution.py:305
  90.1 0.9 copy-done.9
  90.9 4.2 %assemble.3 = (bf16[512,2048]{1,0:T(8,128)(2,1)}, bf16[2048,512]{1,0:T(8,128)(2,1)}) custom-call(s32[2]{0:T(128)} %pad_add_fusion.where_ref, bf16[128,2048]{1,0:T(8,128)(2,1)} %bitcast.7, bf16[128,2048]{1,0:T(8,128)(2,1)} %collective-permute-done.10.refs_1_, bf16[128,2048]{1,0:T(8,128)(2,1)} %collective-permute-done.11.refs_2_, bf16[128,2048]{1,0:T(8,128)(2,1)} %copy-done.9, ...), custom_call_target="tpu_custom_call" | custom-call | bytes 6291456 | tf_op jit(solution)/shard_map/assemble/pallas_call | solution.py:56
  95.1 12.3 %partial_sums.4 = (bf16[4,64,3328]{2,1,0:T(8,128)(2,1)}, bf16[4,64,3328]{2,1,0:T(8,128)(2,1)}) custom-call(bf16[6656,2048]{1,0:T(8,128)(2,1)} %w_ref.5, bf16[2048,512]{1,0:T(8,128)(2,1)} %get-tuple-element.33.g_ref, bf16[2,64,6656]{2,1,0:T(8,128)(2,1)} %sums.4.refs_4_.refs_0_), custom_call_target="tpu_custom_call" | custom-call | flops 6979321856 | bytes 19136512 | tf_op jit(solution)/shard_map/partial_sums/pallas_call | solution.py:90
  107.4 12.4 %partial_sums.5 = (bf16[4,64,3328]{2,1,0:T(8,128)(2,1)}, bf16[4,64,3328]{2,1,0:T(8,128)(2,1)}) custom-call(bf16[6656,2048]{1,0:T(8,128)(2,1)} %w_ref.5, bf16[2048,512]{1,0:T(8,128)(2,1)} %get-tuple-element.33.g_ref, bf16[4,64,3328]{2,1,0:T(8,128)(2,1)} %get-tuple-element.35.refs_0_), custom_call_target="tpu_custom_call" | custom-call | flops 6979321856 | bytes 19136512 | tf_op jit(solution)/shard_map/partial_sums/pallas_call | solution.py:90
  119.8 0.5 collective-permute-start.14
  120.3 12.2 %weight_rows.3.refs_7_.refs_11_ = bf16[6656,2048]{1,0:T(8,128)(2,1)} custom-call(s32[2]{0:T(128)} %pad_add_fusion.where_ref, bf16[128,6656]{1,0:T(8,128)(2,1)} %refs_0_.5, bf16[128,6656]{1,0:T(8,128)(2,1)} %copy-done.2, bf16[128,6656]{1,0:T(8,128)(2,1)} %copy-done, bf16[128,6656]{1,0:T(8,128)(2,1)} %collective-permute-done.2.refs_3_, ...), custom_call_target="tpu_custom_call" | custom-call | flops 6442450944 | bytes 13631488 | tf_op jit(solution)/shard_map/weight_rows/pallas_call | solution.py:142
  132.6 1.3 copy-done.4
  133.9 3.9 %sums.5 = (bf16[1,64,6656]{2,1,0:T(8,128)(2,1)}, bf16[2,64,6656]{2,1,0:T(8,128)(2,1)}) custom-call(bf16[4,64,6656]{2,1,0:T(8,128)(2,1)} %get-tuple-element.30.refs_0_.refs_5_, bf16[4,64,6656]{2,1,0:T(8,128)(2,1)} %collective-permute-done.13.refs_1_.refs_6_, bf16[2,64,6656]{2,1,0:T(8,128)(2,1)} %collective-permute-done.16.refs_2_.refs_7_, ...), custom_call_target="tpu_custom_call" | custom-call | flops 5963776 | bytes 11927552 | tf_op jit(solution)/shard_map/sums/pallas_call | solution.py:214
  137.8 1.5 collective-permute-start.17
  139.3 1.2 collective-permute-start.18
  140.5 22.2 %weight_rows.4.refs_9_.refs_11_ = bf16[6656,2048]{1,0:T(8,128)(2,1)} custom-call(s32[2]{0:T(128)} %pad_add_fusion.where_ref, bf16[128,6656]{1,0:T(8,128)(2,1)} %refs_0_.5, bf16[128,6656]{1,0:T(8,128)(2,1)} %copy-done.2, bf16[128,6656]{1,0:T(8,128)(2,1)} %copy-done, ...), custom_call_target="tpu_custom_call", output_to_operand_aliasing={{}: (12, {})} | custom-call | flops 15032385536 | bytes 26214400 | tf_op jit(solution)/shard_map/weight_rows/pallas_call | solution.py:142
  162.8 6.2 %collective-permute-done.17.refs_4_ = bf16[2,64,6656]{2,1,0:T(8,128)(2,1)S(1)} collective-permute-done((bf16[2,64,6656]{2,1,0:T(8,128)(2,1)}, bf16[2,64,6656]{2,1,0:T(8,128)(2,1)S(1)}, u32[]{:S(2)}, u32[]{:S(2)}) %collective-permute-start.17) | collective-permute-done | bytes 1703968 | tf_op jit(solution)/shard_map/ppermute | solution.py:27
  169.0 1.2 copy-done.5
  170.2 4.0 %sums.6 = (bf16[1,64,6656]{2,1,0:T(8,128)(2,1)}, bf16[128,6656]{1,0:T(8,128)(2,1)}) custom-call(bf16[4,64,3328]{2,1,0:T(8,128)(2,1)} %get-tuple-element.34.refs_3_.refs_0_, bf16[4,64,3328]{2,1,0:T(8,128)(2,1)} %get-tuple-element.36.refs_4_.refs_1_, bf16[4,64,3328]{2,1,0:T(8,128)(2,1)} %copy-done.4, ...), custom_call_target="tpu_custom_call" | custom-call | flops 4685824 | bytes 9371648 | tf_op jit(solution)/shard_map/sums/pallas_call | solution.py:214
  174.1 0.9 collective-permute-start.19
  175.0 12.2 %weight_rows.5.refs_6_ = bf16[6656,2048]{1,0:T(8,128)(2,1)} custom-call(s32[2]{0:T(128)} %pad_add_fusion.where_ref, bf16[128,6656]{1,0:T(8,128)(2,1)} %refs_0_.5, bf16[128,6656]{1,0:T(8,128)(2,1)} %copy-done.2, bf16[128,6656]{1,0:T(8,128)(2,1)} %copy-done, bf16[128,6656]{1,0:T(8,128)(2,1)} %collective-permute-done.2.refs_3_, ...), custom_call_target="tpu_custom_call", output_to_operand_aliasing={{}: (12, {})} | custom-call | flops 6442450944 | bytes 13631488 | tf_op jit(solution)/shard_map/weight_rows/pallas_call | solution.py:142
  187.3 0.9 copy-done.7
  188.1 3.0 %sums.7 = bf16[128,6656]{1,0:T(8,128)(2,1)} custom-call(bf16[4,64,3328]{2,1,0:T(8,128)(2,1)} %get-tuple-element.34.refs_3_.refs_0_, bf16[4,64,3328]{2,1,0:T(8,128)(2,1)} %get-tuple-element.36.refs_4_.refs_1_, bf16[4,64,3328]{2,1,0:T(8,128)(2,1)} %copy-done.4, ...), custom_call_target="tpu_custom_call", output_to_operand_aliasing={{}: (7, {})} | custom-call | flops 2981888 | bytes 5963776 | tf_op jit(solution)/shard_map/sums/pallas_call | solution.py:214
  (29 shorter events, 0.1 us)
Async XLA Ops:
  0.6 40.4 %collective-permute-start.1 = (bf16[128,6656]{1,0:T(8,128)(2,1)}, bf16[128,6656]{1,0:T(8,128)(2,1)S(1)}, u32[]{:S(2)}, u32[]{:S(2)}) collective-permute-start(bf16[128,6656]{1,0:T(8,128)(2,1)} %refs_0_.5), channel_id=1, source_target_pairs={{0,4},{1,5},{2,6},{3,7},{4,0},{5,1},{6,2},{7,3},{8,12},{9,13},{10,... | collective-permute-start | bytes 5111816 | tf_op jit(solution)/shard_map/ppermute | solution.py:27
  3.7 38.9 %collective-permute-start = (bf16[128,6656]{1,0:T(8,128)(2,1)}, bf16[128,6656]{1,0:T(8,128)(2,1)S(1)}, u32[]{:S(2)}, u32[]{:S(2)}) collective-permute-start(bf16[128,6656]{1,0:T(8,128)(2,1)} %refs_0_.5), channel_id=1, source_target_pairs={{0,2},{1,3},{2,0},{3,1},{4,6},{5,7},{6,4},{7,5},{8,10},{9,11},{10,... | collective-permute-start | bytes 5111816 | tf_op jit(solution)/shard_map/ppermute | solution.py:27
  7.0 25.7 %collective-permute-start.7 = (bf16[128,2048]{1,0:T(8,128)(2,1)}, bf16[128,2048]{1,0:T(8,128)(2,1)}, u32[]{:S(2)}, u32[]{:S(2)}) collective-permute-start(bf16[128,2048]{1,0:T(8,128)(2,1)} %bitcast.3.refs_0_), channel_id=1, source_target_pairs={{0,16},{8,24},{16,0},{24,8},{1,17},{9,25},{17,1},{25,9},{2,18},{10... | collective-permute-start | bytes 1572872 | tf_op jit(solution)/shard_map/ppermute | solution.py:35
  9.6 39.9 %collective-permute-start.8 = (bf16[128,2048]{1,0:T(8,128)(2,1)}, bf16[128,2048]{1,0:T(8,128)(2,1)}, u32[]{:S(2)}, u32[]{:S(2)}) collective-permute-start(bf16[128,2048]{1,0:T(8,128)(2,1)} %bitcast.3.refs_0_), channel_id=1, source_target_pairs={{0,8},{8,0},{16,24},{24,16},{1,9},{9,1},{17,25},{25,17},{2,10},{10... | collective-permute-start | bytes 1572872 | tf_op jit(solution)/shard_map/ppermute | solution.py:301
  32.7 18.5 %collective-permute-start.9 = (bf16[128,2048]{1,0:T(8,128)(2,1)}, bf16[128,2048]{1,0:T(8,128)(2,1)}, u32[]{:S(2)}, u32[]{:S(2)}) collective-permute-start(bf16[128,2048]{1,0:T(8,128)(2,1)} %collective-permute-done.7.refs_1_), channel_id=1, source_target_pairs={{0,8},{8,0},{16,24},{24,16},{1,9},{9,1},{17,25},{25,17},{2,10},{10... | collective-permute-start | bytes 1572872 | tf_op jit(solution)/shard_map/ppermute | solution.py:305
  41.1 2.9 %copy-start = (bf16[128,6656]{1,0:T(8,128)(2,1)}, bf16[128,6656]{1,0:T(8,128)(2,1)S(1)}, u32[]{:S(2)}) copy-start(bf16[128,6656]{1,0:T(8,128)(2,1)S(1)} %collective-permute-done.1.refs_5_.refs_2_) | copy-start | bytes 5111812
  42.5 1.8 copy-start.2
  44.3 31.9 %collective-permute-start.2 = (bf16[128,6656]{1,0:T(8,128)(2,1)}, bf16[128,6656]{1,0:T(8,128)(2,1)}, u32[]{:S(2)}, u32[]{:S(2)}) collective-permute-start(bf16[128,6656]{1,0:T(8,128)(2,1)} %broadcast_select_fusion), channel_id=1, source_target_pairs={{0,4},{1,3},{2,6},{3,1},{4,0},{5,7},{6,2},{7,5},{8,12},{9,11},{10,... | collective-permute-start | bytes 5111816 | tf_op jit(solution)/shard_map/ppermute | solution.py:27
  45.2 39.9 %collective-permute-start.3 = (bf16[128,6656]{1,0:T(8,128)(2,1)}, bf16[128,6656]{1,0:T(8,128)(2,1)}, u32[]{:S(2)}, u32[]{:S(2)}) collective-permute-start(bf16[128,6656]{1,0:T(8,128)(2,1)} %refs_0_.5), channel_id=1, source_target_pairs={{0,1},{1,0},{2,3},{3,2},{4,5},{5,4},{6,7},{7,6},{8,9},{9,8},{10,11... | collective-permute-start | bytes 5111816 | tf_op jit(solution)/shard_map/ppermute | solution.py:27
  46.9 8.5 %copy-start.6 = (bf16[2,64,2048]{2,1,0:T(8,128)(2,1)}, bf16[2,64,2048]{2,1,0:T(8,128)(2,1)S(1)}, u32[]{:S(2)}) copy-start(bf16[2,64,2048]{2,1,0:T(8,128)(2,1)S(1)} %slice.7) | copy-start | bytes 1572868
  46.9 28.6 %collective-permute-start.11 = (bf16[128,2048]{1,0:T(8,128)(2,1)S(1)}, bf16[128,2048]{1,0:T(8,128)(2,1)}, u32[]{:S(2)}, u32[]{:S(2)}) collective-permute-start(bf16[128,2048]{1,0:T(8,128)(2,1)S(1)} %bitcast.5), channel_id=1, source_target_pairs={{0,16},{8,24},{16,0},{24,8},{1,17},{9,25},{17,1},{25,9},{2,18},{10... | collective-permute-start | bytes 1572872 | tf_op jit(solution)/shard_map/ppermute | solution.py:35
  49.6 25.9 %collective-permute-start.10 = (bf16[128,2048]{1,0:T(8,128)(2,1)S(1)}, bf16[128,2048]{1,0:T(8,128)(2,1)}, u32[]{:S(2)}, u32[]{:S(2)}) collective-permute-start(bf16[128,2048]{1,0:T(8,128)(2,1)S(1)} %bitcast.6), channel_id=1, source_target_pairs={{0,8},{8,0},{16,24},{24,16},{1,9},{9,1},{17,25},{25,17},{2,10},{10... | collective-permute-start | bytes 1572872 | tf_op jit(solution)/shard_map/ppermute | solution.py:301
  55.4 20.6 %copy-start.1 = (bf16[128,6656]{1,0:T(8,128)(2,1)S(1)}, bf16[128,6656]{1,0:T(8,128)(2,1)}, u32[]{:S(2)}) copy-start(bf16[128,6656]{1,0:T(8,128)(2,1)} %copy-done) | copy-start | bytes 5111812
  55.4 20.8 %copy-start.3 = (bf16[128,6656]{1,0:T(8,128)(2,1)S(1)}, bf16[128,6656]{1,0:T(8,128)(2,1)}, u32[]{:S(2)}) copy-start(bf16[128,6656]{1,0:T(8,128)(2,1)} %copy-done.2) | copy-start | bytes 5111812
  75.5 6.4 %collective-permute-start.13 = (bf16[4,64,6656]{2,1,0:T(8,128)(2,1)}, bf16[4,64,6656]{2,1,0:T(8,128)(2,1)}, u32[]{:S(2)}, u32[]{:S(2)}) collective-permute-start(bf16[4,64,6656]{2,1,0:T(8,128)(2,1)} %get-tuple-element.31.refs_0_), channel_id=1, source_target_pairs={{0,1},{1,0},{2,3},{3,2},{4,5},{5,4},{6,7},{7,6},{8,9},{9,8},{10,11... | collective-permute-start | bytes 10223624 | tf_op jit(solution)/shard_map/ppermute | solution.py:27
  75.5 14.6 %collective-permute-start.12 = (bf16[128,2048]{1,0:T(8,128)(2,1)}, bf16[128,2048]{1,0:T(8,128)(2,1)S(1)}, u32[]{:S(2)}, u32[]{:S(2)}) collective-permute-start(bf16[128,2048]{1,0:T(8,128)(2,1)} %collective-permute-done.11.refs_2_), channel_id=1, source_target_pairs={{0,8},{8,0},{16,24},{24,16},{1,9},{9,1},{17,25},{25,17},{2,10},{10... | collective-permute-start | bytes 1572872 | tf_op jit(solution)/shard_map/ppermute | solution.py:305
  76.0 43.8 %collective-permute-start.5 = (bf16[128,6656]{1,0:T(8,128)(2,1)S(1)}, bf16[128,6656]{1,0:T(8,128)(2,1)}, u32[]{:S(2)}, u32[]{:S(2)}) collective-permute-start(bf16[128,6656]{1,0:T(8,128)(2,1)S(1)} %copy-done.1), channel_id=1, source_target_pairs={{0,1},{1,0},{2,3},{3,2},{4,5},{5,4},{6,7},{7,6},{8,9},{9,8},{10,11... | collective-permute-start | bytes 5111816 | tf_op jit(solution)/shard_map/ppermute | solution.py:27
  76.2 44.1 %collective-permute-start.4 = (bf16[128,6656]{1,0:T(8,128)(2,1)S(1)}, bf16[128,6656]{1,0:T(8,128)(2,1)}, u32[]{:S(2)}, u32[]{:S(2)}) collective-permute-start(bf16[128,6656]{1,0:T(8,128)(2,1)S(1)} %copy-done.3), channel_id=1, source_target_pairs={{0,1},{1,0},{2,3},{3,2},{4,5},{5,4},{6,7},{7,6},{8,9},{9,8},{10,11... | collective-permute-start | bytes 5111816 | tf_op jit(solution)/shard_map/ppermute | solution.py:27
  81.9 38.5 %collective-permute-start.6 = (bf16[128,6656]{1,0:T(8,128)(2,1)}, bf16[128,6656]{1,0:T(8,128)(2,1)}, u32[]{:S(2)}, u32[]{:S(2)}) collective-permute-start(bf16[128,6656]{1,0:T(8,128)(2,1)} %collective-permute-done.2.refs_3_), channel_id=1, source_target_pairs={{0,1},{1,0},{2,3},{3,2},{4,5},{5,4},{6,7},{7,6},{8,9},{9,8},{10,11... | collective-permute-start | bytes 5111816 | tf_op jit(solution)/shard_map/ppermute | solution.py:27
  85.0 47.5 %collective-permute-start.16 = (bf16[2,64,6656]{2,1,0:T(8,128)(2,1)}, bf16[2,64,6656]{2,1,0:T(8,128)(2,1)}, u32[]{:S(2)}, u32[]{:S(2)}) collective-permute-start(bf16[2,64,6656]{2,1,0:T(8,128)(2,1)} %sums.4.refs_4_.refs_0_), channel_id=1, source_target_pairs={{0,2},{1,5},{2,0},{3,7},{4,6},{5,1},{6,4},{7,3},{8,10},{9,13},{10,... | collective-permute-start | bytes 5111816 | tf_op jit(solution)/shard_map/ppermute | solution.py:27
  90.1 0.9 copy-start.9
  119.8 12.8 %collective-permute-start.15 = (bf16[4,64,3328]{2,1,0:T(8,128)(2,1)}, bf16[4,64,3328]{2,1,0:T(8,128)(2,1)}, u32[]{:S(2)}, u32[]{:S(2)}) collective-permute-start(bf16[4,64,3328]{2,1,0:T(8,128)(2,1)} %get-tuple-element.37.refs_10_), channel_id=1, source_target_pairs={{0,1},{1,0},{2,3},{3,2},{4,5},{5,4},{6,7},{7,6},{8,9},{9,8},{10,11... | collective-permute-start | bytes 5111816 | tf_op jit(solution)/shard_map/ppermute | solution.py:27
  119.8 12.8 %collective-permute-start.14 = (bf16[4,64,3328]{2,1,0:T(8,128)(2,1)}, bf16[4,64,3328]{2,1,0:T(8,128)(2,1)S(1)}, u32[]{:S(2)}, u32[]{:S(2)}) collective-permute-start(bf16[4,64,3328]{2,1,0:T(8,128)(2,1)} %get-tuple-element.35.refs_0_), channel_id=1, source_target_pairs={{0,1},{1,0},{2,3},{3,2},{4,5},{5,4},{6,7},{7,6},{8,9},{9,8},{10,11... | collective-permute-start | bytes 5111816 | tf_op jit(solution)/shard_map/ppermute | solution.py:27
  132.6 1.3 copy-start.4
  137.8 31.2 %collective-permute-start.17 = (bf16[2,64,6656]{2,1,0:T(8,128)(2,1)}, bf16[2,64,6656]{2,1,0:T(8,128)(2,1)S(1)}, u32[]{:S(2)}, u32[]{:S(2)}) collective-permute-start(bf16[2,64,6656]{2,1,0:T(8,128)(2,1)} %get-tuple-element.38), channel_id=1, source_target_pairs={{0,2},{1,5},{2,0},{3,7},{4,6},{5,1},{6,4},{7,3},{8,10},{9,13},{10,... | collective-permute-start | bytes 5111816 | tf_op jit(solution)/shard_map/ppermute | solution.py:27
  139.3 23.4 %collective-permute-start.18 = (bf16[1,64,6656]{2,1,0:T(8,128)(2,1)}, bf16[1,64,6656]{2,1,0:T(8,128)(2,1)S(1)}, u32[]{:S(2)}, u32[]{:S(2)}) collective-permute-start(bf16[1,64,6656]{2,1,0:T(8,128)(2,1)} %get-tuple-element.39.refs_10_), channel_id=1, source_target_pairs={{0,4},{1,3},{2,6},{3,1},{4,0},{5,7},{6,2},{7,5},{8,12},{9,11},{10,... | collective-permute-start | bytes 2555912 | tf_op jit(solution)/shard_map/ppermute | solution.py:27
  162.7 6.3 %copy-start.8 = (bf16[1,64,6656]{2,1,0:T(8,128)(2,1)}, bf16[1,64,6656]{2,1,0:T(8,128)(2,1)S(1)}, u32[]{:S(2)}) copy-start(bf16[1,64,6656]{2,1,0:T(8,128)(2,1)S(1)} %collective-permute-done.18.refs_8_) | copy-start | bytes 2555908
  169.0 1.2 copy-start.5
  174.1 13.1 %collective-permute-start.19 = (bf16[1,64,6656]{2,1,0:T(8,128)(2,1)}, bf16[1,64,6656]{2,1,0:T(8,128)(2,1)S(1)}, u32[]{:S(2)}, u32[]{:S(2)}) collective-permute-start(bf16[1,64,6656]{2,1,0:T(8,128)(2,1)} %get-tuple-element.40.refs_10_), channel_id=1, source_target_pairs={{0,4},{1,3},{2,6},{3,1},{4,0},{5,7},{6,2},{7,5},{8,12},{9,11},{10,... | collective-permute-start | bytes 2555912 | tf_op jit(solution)/shard_map/ppermute | solution.py:27
  187.2 0.9 copy-start.7

commit v7 on v6

--- a/solution.py
+++ b/solution.py
@@ -51,7 +51,7 @@
 def assemble(where, blocks, orders, c, after):
     rows_of, arrays = list(blocks), list(blocks.values())
     depth, rows = arrays[0].shape[1], len(orders[0]) * c
-    steps = 2
+    steps = 4
     part = pl.BlockSpec((arrays[0].shape[0], depth // steps), lambda i, s: (0, i))
     return pl.pallas_call(
         functools.partial(assemble_kernel, rows_of, orders, c),
@@ -368,14 +368,14 @@
             sends.append(send)
             keeps.append(keep)
     one = Halving(sends, keeps, levels, n_col)
-    after = work(3, after)
+    after = work(2, after)
     parts, steps = [zero, one], len(levels) - 1
     for step in range(steps):
         going, ended = [p for p in parts if p.levels], [p for p in parts if not p.levels]
         after = advance(going, ended, 0, after)
         parts = going
         left = tiles - done
-        after = work(left if step == steps - 1 else -(-left * 2 // 3), after)
+        after = work(left if step == steps - 1 else left * 9 // 11, after)
     advance([], [one], c, after)
     return weight_grad, hidden_grad
 

time: 192 us -> 190 us (0.990)
  waiting for transfers between devices: 45.3 us -> 41.6 us
  Pallas kernels: 114 us -> 116 us
    ppermute x14, waiting for transfers between devices: 20.3 us -> 16.5 us  [flip(): return lax.ppermute(x, 'col', [(i, i ^ bits[i & 1]) for i in range(n)])]
  transfers between devices with their start and end apart: 20 -> 20, of which waited for: 6 -> 7; matrix products, arithmetic and copies ran while one was open for 3% -> 3% of each run, Pallas kernels for 54% -> 55%
where the time goes in v7:
time: 190 us
  Pallas kernels  116 us (61%)
  waiting for transfers between devices  41.6 us (22%)
  starting transfers between devices  21 us (11%)
  local copies, waits for them, and re-layouts  8.23 us (4%)
  other arithmetic  2.13 us (1%)
    pallas_call x3, Pallas kernels, weight_rows(): pl.pallas_call(functools.partial(weight_kernel, places, chunks, n), out_s...  46.9 us
    pallas_call x3, Pallas kernels, partial_sums(): pl.pallas_call(partial_kernel, out_shape=(out, out), grid=(count,), in_sp...  44.7 us
    ppermute x2, waiting for transfers between devices, doubled(): held[j ^ bit] = lax.ppermute(held[j], 'row', pairs)  21.5 us
    ppermute x14, waiting for transfers between devices, flip(): return lax.ppermute(x, 'col', [(i, i ^ bits[i & 1]) for i in range(n)])  16.5 us
    pallas_call x4, Pallas kernels, sums(): pl.pallas_call(functools.partial(sums_kernel, layout, len(ended)), out_sh...  13.9 us
    ppermute x14, starting transfers between devices, flip(): return lax.ppermute(x, 'col', [(i, i ^ bits[i & 1]) for i in range(n)])  11.6 us
    pallas_call x2, Pallas kernels, assemble(): pl.pallas_call(functools.partial(assemble_kernel, rows_of, orders, c), ou...  10.2 us
    unnamed x20, local copies, waits for them, and re-layouts  5.27 us
  transfers between devices with their start and end apart: 20, of which 7 were waited for; matrix products, arithmetic and copies ran while one was open for 3% of the time, Pallas kernels for 55%

profile of v7, /device:TPU:0, one launch (start us, length us, event | category | flops | bytes accessed | tf_op | source)
XLA Modules:
  0.0 190.0 jit_solution(6522101781264545631)
XLA Ops:
  0.6 3.0 %collective-permute-start.1 = (bf16[128,6656]{1,0:T(8,128)(2,1)}, bf16[128,6656]{1,0:T(8,128)(2,1)S(1)}, u32[]{:S(2)}, u32[]{:S(2)}) collective-permute-start(bf16[128,6656]{1,0:T(8,128)(2,1)} %refs_0_.5), channel_id=1, source_target_pairs={{0,4},{1,5},{2,6},{3,7},{4,0},{5,1},{6,2},{7,3},{8,12},{9,13},{10,... | collective-permute-start | bytes 5111816 | tf_op jit(solution)/shard_map/ppermute | solution.py:27
  3.7 1.5 collective-permute-start
  5.2 1.9 slice.8
  7.0 2.6 %collective-permute-start.7 = (bf16[128,2048]{1,0:T(8,128)(2,1)}, bf16[128,2048]{1,0:T(8,128)(2,1)}, u32[]{:S(2)}, u32[]{:S(2)}) collective-permute-start(bf16[128,2048]{1,0:T(8,128)(2,1)} %bitcast.3.refs_0_), channel_id=1, source_target_pairs={{0,16},{8,24},{16,0},{24,8},{1,17},{9,25},{17,1},{25,9},{2,18},{10... | collective-permute-start | bytes 1572872 | tf_op jit(solution)/shard_map/ppermute | solution.py:35
  9.6 1.6 collective-permute-start.8
  11.2 21.5 %collective-permute-done.7.refs_1_ = bf16[128,2048]{1,0:T(8,128)(2,1)} collective-permute-done((bf16[128,2048]{1,0:T(8,128)(2,1)}, bf16[128,2048]{1,0:T(8,128)(2,1)}, u32[]{:S(2)}, u32[]{:S(2)}) %collective-permute-start.7) | collective-permute-done | bytes 524320 | tf_op jit(solution)/shard_map/ppermute | solution.py:35
  32.7 0.6 collective-permute-start.9
  33.3 7.8 %collective-permute-done.1.refs_5_.refs_2_ = bf16[128,6656]{1,0:T(8,128)(2,1)S(1)} collective-permute-done((bf16[128,6656]{1,0:T(8,128)(2,1)}, bf16[128,6656]{1,0:T(8,128)(2,1)S(1)}, u32[]{:S(2)}, u32[]{:S(2)}) %collective-permute-start.1) | collective-permute-done | bytes 1703968 | tf_op jit(solution)/shard_map/ppermute | solution.py:27
  41.1 1.5 collective-permute-done.refs_4_.refs_1_
  42.5 1.5 broadcast_select_fusion
  44.0 0.3 copy-done.2
  44.3 0.8 collective-permute-start.2
  45.2 0.6 pad_add_fusion.where_ref
  45.8 1.1 slice.7
  46.9 2.6 %collective-permute-start.11 = (bf16[128,2048]{1,0:T(8,128)(2,1)S(1)}, bf16[128,2048]{1,0:T(8,128)(2,1)}, u32[]{:S(2)}, u32[]{:S(2)}) collective-permute-start(bf16[128,2048]{1,0:T(8,128)(2,1)S(1)} %bitcast.5), channel_id=1, source_target_pairs={{0,16},{8,24},{16,0},{24,8},{1,17},{9,25},{17,1},{25,9},{2,18},{10... | collective-permute-start | bytes 1572872 | tf_op jit(solution)/shard_map/ppermute | solution.py:35
  49.6 1.6 collective-permute-start.10
  51.1 0.0 collective-permute-done.9.refs_3_
  51.1 5.2 %assemble.2 = (bf16[512,2048]{1,0:T(8,128)(2,1)}, bf16[2048,512]{1,0:T(8,128)(2,1)}) custom-call(s32[2]{0:T(128)} %pad_add_fusion.where_ref, bf16[128,2048]{1,0:T(8,128)(2,1)} %bitcast.3.refs_0_, bf16[128,2048]{1,0:T(8,128)(2,1)} %collective-permute-done.7.refs_1_, bf16[128,2048]{1,0:T(8,128)(2,1)} %collective-permute-done.8.refs_2_, ...), custom_call_target="tpu_custom_call" | custom-call | bytes 6291456 | tf_op jit(solution)/shard_map/assemble/pallas_call | solution.py:56
  56.3 20.1 %partial_sums.3 = (bf16[4,64,6656]{2,1,0:T(8,128)(2,1)}, bf16[4,64,6656]{2,1,0:T(8,128)(2,1)}) custom-call(bf16[6656,2048]{1,0:T(8,128)(2,1)} %w_ref.5, bf16[2048,512]{1,0:T(8,128)(2,1)} %get-tuple-element.25.g_ref), custom_call_target="tpu_custom_call" | custom-call | flops 13958643712 | bytes 36175872 | tf_op jit(solution)/shard_map/partial_sums/pallas_call | solution.py:90
  76.4 0.5 collective-permute-start.12
  76.9 0.2 collective-permute-start.5
  77.1 0.3 collective-permute-start.4
  77.4 0.6 hold.1.refs_2_
  78.0 4.7 %collective-permute-done.13.refs_1_.refs_6_ = bf16[4,64,6656]{2,1,0:T(8,128)(2,1)} collective-permute-done((bf16[4,64,6656]{2,1,0:T(8,128)(2,1)}, bf16[4,64,6656]{2,1,0:T(8,128)(2,1)}, u32[]{:S(2)}, u32[]{:S(2)}) %collective-permute-start.13) | collective-permute-done | bytes 3407904 | tf_op jit(solution)/shard_map/ppermute | solution.py:27
  82.8 0.1 collective-permute-start.6
  82.9 3.0 %sums.4.refs_4_.refs_0_ = bf16[2,64,6656]{2,1,0:T(8,128)(2,1)} custom-call(bf16[4,64,6656]{2,1,0:T(8,128)(2,1)} %get-tuple-element.30.refs_0_.refs_5_, bf16[4,64,6656]{2,1,0:T(8,128)(2,1)} %collective-permute-done.13.refs_1_.refs_6_, f32[8,128]{1,0:T(8,128)} %hold.1.refs_2_), custom_call_target="tpu_custom_call" | custom-call | flops 2555904 | bytes 5111808 | tf_op jit(solution)/shard_map/sums/pallas_call | solution.py:214
  85.9 1.5 collective-permute-start.16
  87.4 3.5 %collective-permute-done.12.refs_3_ = bf16[128,2048]{1,0:T(8,128)(2,1)S(1)} collective-permute-done((bf16[128,2048]{1,0:T(8,128)(2,1)}, bf16[128,2048]{1,0:T(8,128)(2,1)S(1)}, u32[]{:S(2)}, u32[]{:S(2)}) %collective-permute-start.12) | collective-permute-done | bytes 524320 | tf_op jit(solution)/shard_map/ppermute | solution.py:305
  91.0 0.9 copy-done.9
  91.8 5.1 %assemble.3 = (bf16[512,2048]{1,0:T(8,128)(2,1)}, bf16[2048,512]{1,0:T(8,128)(2,1)}) custom-call(s32[2]{0:T(128)} %pad_add_fusion.where_ref, bf16[128,2048]{1,0:T(8,128)(2,1)} %bitcast.7, bf16[128,2048]{1,0:T(8,128)(2,1)} %collective-permute-done.10.refs_1_, bf16[128,2048]{1,0:T(8,128)(2,1)} %collective-permute-done.11.refs_2_, bf16[128,2048]{1,0:T(8,128)(2,1)} %copy-done.9, ...), custom_call_target="tpu_custom_call" | custom-call | bytes 6291456 | tf_op jit(solution)/shard_map/assemble/pallas_call | solution.py:56
  96.9 12.3 %partial_sums.4 = (bf16[4,64,3328]{2,1,0:T(8,128)(2,1)}, bf16[4,64,3328]{2,1,0:T(8,128)(2,1)}) custom-call(bf16[6656,2048]{1,0:T(8,128)(2,1)} %w_ref.5, bf16[2048,512]{1,0:T(8,128)(2,1)} %get-tuple-element.33.g_ref, bf16[2,64,6656]{2,1,0:T(8,128)(2,1)} %sums.4.refs_4_.refs_0_), custom_call_target="tpu_custom_call" | custom-call | flops 6979321856 | bytes 19136512 | tf_op jit(solution)/shard_map/partial_sums/pallas_call | solution.py:90
  109.2 12.4 %partial_sums.5 = (bf16[4,64,3328]{2,1,0:T(8,128)(2,1)}, bf16[4,64,3328]{2,1,0:T(8,128)(2,1)}) custom-call(bf16[6656,2048]{1,0:T(8,128)(2,1)} %w_ref.5, bf16[2048,512]{1,0:T(8,128)(2,1)} %get-tuple-element.33.g_ref, bf16[4,64,3328]{2,1,0:T(8,128)(2,1)} %get-tuple-element.35.refs_0_), custom_call_target="tpu_custom_call" | custom-call | flops 6979321856 | bytes 19136512 | tf_op jit(solution)/shard_map/partial_sums/pallas_call | solution.py:90
  121.5 0.5 collective-permute-start.14
  122.1 9.7 %weight_rows.3.refs_7_.refs_11_ = bf16[6656,2048]{1,0:T(8,128)(2,1)} custom-call(s32[2]{0:T(128)} %pad_add_fusion.where_ref, bf16[128,6656]{1,0:T(8,128)(2,1)} %refs_0_.5, bf16[128,6656]{1,0:T(8,128)(2,1)} %copy-done.2, bf16[128,6656]{1,0:T(8,128)(2,1)} %copy-done, bf16[128,6656]{1,0:T(8,128)(2,1)} %collective-permute-done.2.refs_3_, ...), custom_call_target="tpu_custom_call" | custom-call | flops 4294967296 | bytes 10485760 | tf_op jit(solution)/shard_map/weight_rows/pallas_call | solution.py:142
  131.8 1.3 copy-done.4
  133.1 3.9 %sums.5 = (bf16[1,64,6656]{2,1,0:T(8,128)(2,1)}, bf16[2,64,6656]{2,1,0:T(8,128)(2,1)}) custom-call(bf16[4,64,6656]{2,1,0:T(8,128)(2,1)} %get-tuple-element.30.refs_0_.refs_5_, bf16[4,64,6656]{2,1,0:T(8,128)(2,1)} %collective-permute-done.13.refs_1_.refs_6_, bf16[2,64,6656]{2,1,0:T(8,128)(2,1)} %collective-permute-done.16.refs_2_.refs_7_, ...), custom_call_target="tpu_custom_call" | custom-call | flops 5963776 | bytes 11927552 | tf_op jit(solution)/shard_map/sums/pallas_call | solution.py:214
  137.1 1.2 collective-permute-start.18
  138.3 1.5 collective-permute-start.17
  139.7 27.4 %weight_rows.4.refs_9_.refs_11_ = bf16[6656,2048]{1,0:T(8,128)(2,1)} custom-call(s32[2]{0:T(128)} %pad_add_fusion.where_ref, bf16[128,6656]{1,0:T(8,128)(2,1)} %refs_0_.5, bf16[128,6656]{1,0:T(8,128)(2,1)} %copy-done.2, bf16[128,6656]{1,0:T(8,128)(2,1)} %copy-done, ...), custom_call_target="tpu_custom_call", output_to_operand_aliasing={{}: (12, {})} | custom-call | flops 19327352832 | bytes 32505856 | tf_op jit(solution)/shard_map/weight_rows/pallas_call | solution.py:142
  167.2 0.2 collective-permute-done.17.refs_4_
  167.3 0.7 copy-done.8
  168.1 1.2 copy-done.5
  169.2 4.0 %sums.6 = (bf16[1,64,6656]{2,1,0:T(8,128)(2,1)}, bf16[128,6656]{1,0:T(8,128)(2,1)}) custom-call(bf16[4,64,3328]{2,1,0:T(8,128)(2,1)} %get-tuple-element.34.refs_3_.refs_0_, bf16[4,64,3328]{2,1,0:T(8,128)(2,1)} %get-tuple-element.36.refs_4_.refs_1_, bf16[4,64,3328]{2,1,0:T(8,128)(2,1)} %copy-done.4, ...), custom_call_target="tpu_custom_call" | custom-call | flops 4685824 | bytes 9371648 | tf_op jit(solution)/shard_map/sums/pallas_call | solution.py:214
  173.2 0.9 collective-permute-start.19
  174.1 9.7 %weight_rows.5.refs_6_ = bf16[6656,2048]{1,0:T(8,128)(2,1)} custom-call(s32[2]{0:T(128)} %pad_add_fusion.where_ref, bf16[128,6656]{1,0:T(8,128)(2,1)} %refs_0_.5, bf16[128,6656]{1,0:T(8,128)(2,1)} %copy-done.2, bf16[128,6656]{1,0:T(8,128)(2,1)} %copy-done, bf16[128,6656]{1,0:T(8,128)(2,1)} %collective-permute-done.2.refs_3_, ...), custom_call_target="tpu_custom_call", output_to_operand_aliasing={{}: (12, {})} | custom-call | flops 4294967296 | bytes 10485760 | tf_op jit(solution)/shard_map/weight_rows/pallas_call | solution.py:142
  183.8 2.3 %collective-permute-done.19.refs_5_ = bf16[1,64,6656]{2,1,0:T(8,128)(2,1)S(1)} collective-permute-done((bf16[1,64,6656]{2,1,0:T(8,128)(2,1)}, bf16[1,64,6656]{2,1,0:T(8,128)(2,1)S(1)}, u32[]{:S(2)}, u32[]{:S(2)}) %collective-permute-start.19) | collective-permute-done | bytes 852000 | tf_op jit(solution)/shard_map/ppermute | solution.py:27
  186.1 0.9 copy-done.7
  187.0 3.0 %sums.7 = bf16[128,6656]{1,0:T(8,128)(2,1)} custom-call(bf16[4,64,3328]{2,1,0:T(8,128)(2,1)} %get-tuple-element.34.refs_3_.refs_0_, bf16[4,64,3328]{2,1,0:T(8,128)(2,1)} %get-tuple-element.36.refs_4_.refs_1_, bf16[4,64,3328]{2,1,0:T(8,128)(2,1)} %copy-done.4, ...), custom_call_target="tpu_custom_call", output_to_operand_aliasing={{}: (7, {})} | custom-call | flops 2981888 | bytes 5963776 | tf_op jit(solution)/shard_map/sums/pallas_call | solution.py:214
  (29 shorter events, 0.1 us)
Async XLA Ops:
  0.6 40.4 %collective-permute-start.1 = (bf16[128,6656]{1,0:T(8,128)(2,1)}, bf16[128,6656]{1,0:T(8,128)(2,1)S(1)}, u32[]{:S(2)}, u32[]{:S(2)}) collective-permute-start(bf16[128,6656]{1,0:T(8,128)(2,1)} %refs_0_.5), channel_id=1, source_target_pairs={{0,4},{1,5},{2,6},{3,7},{4,0},{5,1},{6,2},{7,3},{8,12},{9,13},{10,... | collective-permute-start | bytes 5111816 | tf_op jit(solution)/shard_map/ppermute | solution.py:27
  3.7 38.9 %collective-permute-start = (bf16[128,6656]{1,0:T(8,128)(2,1)}, bf16[128,6656]{1,0:T(8,128)(2,1)S(1)}, u32[]{:S(2)}, u32[]{:S(2)}) collective-permute-start(bf16[128,6656]{1,0:T(8,128)(2,1)} %refs_0_.5), channel_id=1, source_target_pairs={{0,2},{1,3},{2,0},{3,1},{4,6},{5,7},{6,4},{7,5},{8,10},{9,11},{10,... | collective-permute-start | bytes 5111816 | tf_op jit(solution)/shard_map/ppermute | solution.py:27
  7.0 25.7 %collective-permute-start.7 = (bf16[128,2048]{1,0:T(8,128)(2,1)}, bf16[128,2048]{1,0:T(8,128)(2,1)}, u32[]{:S(2)}, u32[]{:S(2)}) collective-permute-start(bf16[128,2048]{1,0:T(8,128)(2,1)} %bitcast.3.refs_0_), channel_id=1, source_target_pairs={{0,16},{8,24},{16,0},{24,8},{1,17},{9,25},{17,1},{25,9},{2,18},{10... | collective-permute-start | bytes 1572872 | tf_op jit(solution)/shard_map/ppermute | solution.py:35
  9.6 39.9 %collective-permute-start.8 = (bf16[128,2048]{1,0:T(8,128)(2,1)}, bf16[128,2048]{1,0:T(8,128)(2,1)}, u32[]{:S(2)}, u32[]{:S(2)}) collective-permute-start(bf16[128,2048]{1,0:T(8,128)(2,1)} %bitcast.3.refs_0_), channel_id=1, source_target_pairs={{0,8},{8,0},{16,24},{24,16},{1,9},{9,1},{17,25},{25,17},{2,10},{10... | collective-permute-start | bytes 1572872 | tf_op jit(solution)/shard_map/ppermute | solution.py:301
  32.7 18.5 %collective-permute-start.9 = (bf16[128,2048]{1,0:T(8,128)(2,1)}, bf16[128,2048]{1,0:T(8,128)(2,1)}, u32[]{:S(2)}, u32[]{:S(2)}) collective-permute-start(bf16[128,2048]{1,0:T(8,128)(2,1)} %collective-permute-done.7.refs_1_), channel_id=1, source_target_pairs={{0,8},{8,0},{16,24},{24,16},{1,9},{9,1},{17,25},{25,17},{2,10},{10... | collective-permute-start | bytes 1572872 | tf_op jit(solution)/shard_map/ppermute | solution.py:305
  41.1 2.9 %copy-start = (bf16[128,6656]{1,0:T(8,128)(2,1)}, bf16[128,6656]{1,0:T(8,128)(2,1)S(1)}, u32[]{:S(2)}) copy-start(bf16[128,6656]{1,0:T(8,128)(2,1)S(1)} %collective-permute-done.1.refs_5_.refs_2_) | copy-start | bytes 5111812
  42.5 1.8 copy-start.2
  44.3 32.8 %collective-permute-start.2 = (bf16[128,6656]{1,0:T(8,128)(2,1)}, bf16[128,6656]{1,0:T(8,128)(2,1)}, u32[]{:S(2)}, u32[]{:S(2)}) collective-permute-start(bf16[128,6656]{1,0:T(8,128)(2,1)} %broadcast_select_fusion), channel_id=1, source_target_pairs={{0,4},{1,3},{2,6},{3,1},{4,0},{5,7},{6,2},{7,5},{8,12},{9,11},{10,... | collective-permute-start | bytes 5111816 | tf_op jit(solution)/shard_map/ppermute | solution.py:27
  45.2 40.8 %collective-permute-start.3 = (bf16[128,6656]{1,0:T(8,128)(2,1)}, bf16[128,6656]{1,0:T(8,128)(2,1)}, u32[]{:S(2)}, u32[]{:S(2)}) collective-permute-start(bf16[128,6656]{1,0:T(8,128)(2,1)} %refs_0_.5), channel_id=1, source_target_pairs={{0,1},{1,0},{2,3},{3,2},{4,5},{5,4},{6,7},{7,6},{8,9},{9,8},{10,11... | collective-permute-start | bytes 5111816 | tf_op jit(solution)/shard_map/ppermute | solution.py:27
  46.9 9.4 %copy-start.6 = (bf16[2,64,2048]{2,1,0:T(8,128)(2,1)}, bf16[2,64,2048]{2,1,0:T(8,128)(2,1)S(1)}, u32[]{:S(2)}) copy-start(bf16[2,64,2048]{2,1,0:T(8,128)(2,1)S(1)} %slice.7) | copy-start | bytes 1572868
  46.9 29.5 %collective-permute-start.11 = (bf16[128,2048]{1,0:T(8,128)(2,1)S(1)}, bf16[128,2048]{1,0:T(8,128)(2,1)}, u32[]{:S(2)}, u32[]{:S(2)}) collective-permute-start(bf16[128,2048]{1,0:T(8,128)(2,1)S(1)} %bitcast.5), channel_id=1, source_target_pairs={{0,16},{8,24},{16,0},{24,8},{1,17},{9,25},{17,1},{25,9},{2,18},{10... | collective-permute-start | bytes 1572872 | tf_op jit(solution)/shard_map/ppermute | solution.py:35
  49.6 26.8 %collective-permute-start.10 = (bf16[128,2048]{1,0:T(8,128)(2,1)S(1)}, bf16[128,2048]{1,0:T(8,128)(2,1)}, u32[]{:S(2)}, u32[]{:S(2)}) collective-permute-start(bf16[128,2048]{1,0:T(8,128)(2,1)S(1)} %bitcast.6), channel_id=1, source_target_pairs={{0,8},{8,0},{16,24},{24,16},{1,9},{9,1},{17,25},{25,17},{2,10},{10... | collective-permute-start | bytes 1572872 | tf_op jit(solution)/shard_map/ppermute | solution.py:301
  56.3 20.6 %copy-start.1 = (bf16[128,6656]{1,0:T(8,128)(2,1)S(1)}, bf16[128,6656]{1,0:T(8,128)(2,1)}, u32[]{:S(2)}) copy-start(bf16[128,6656]{1,0:T(8,128)(2,1)} %copy-done) | copy-start | bytes 5111812
  56.3 20.8 %copy-start.3 = (bf16[128,6656]{1,0:T(8,128)(2,1)S(1)}, bf16[128,6656]{1,0:T(8,128)(2,1)}, u32[]{:S(2)}) copy-start(bf16[128,6656]{1,0:T(8,128)(2,1)} %copy-done.2) | copy-start | bytes 5111812
  76.4 6.4 %collective-permute-start.13 = (bf16[4,64,6656]{2,1,0:T(8,128)(2,1)}, bf16[4,64,6656]{2,1,0:T(8,128)(2,1)}, u32[]{:S(2)}, u32[]{:S(2)}) collective-permute-start(bf16[4,64,6656]{2,1,0:T(8,128)(2,1)} %get-tuple-element.31.refs_0_), channel_id=1, source_target_pairs={{0,1},{1,0},{2,3},{3,2},{4,5},{5,4},{6,7},{7,6},{8,9},{9,8},{10,11... | collective-permute-start | bytes 10223624 | tf_op jit(solution)/shard_map/ppermute | solution.py:27
  76.4 14.6 %collective-permute-start.12 = (bf16[128,2048]{1,0:T(8,128)(2,1)}, bf16[128,2048]{1,0:T(8,128)(2,1)S(1)}, u32[]{:S(2)}, u32[]{:S(2)}) collective-permute-start(bf16[128,2048]{1,0:T(8,128)(2,1)} %collective-permute-done.11.refs_2_), channel_id=1, source_target_pairs={{0,8},{8,0},{16,24},{24,16},{1,9},{9,1},{17,25},{25,17},{2,10},{10... | collective-permute-start | bytes 1572872 | tf_op jit(solution)/shard_map/ppermute | solution.py:305
  76.9 44.6 %collective-permute-start.5 = (bf16[128,6656]{1,0:T(8,128)(2,1)S(1)}, bf16[128,6656]{1,0:T(8,128)(2,1)}, u32[]{:S(2)}, u32[]{:S(2)}) collective-permute-start(bf16[128,6656]{1,0:T(8,128)(2,1)S(1)} %copy-done.1), channel_id=1, source_target_pairs={{0,1},{1,0},{2,3},{3,2},{4,5},{5,4},{6,7},{7,6},{8,9},{9,8},{10,11... | collective-permute-start | bytes 5111816 | tf_op jit(solution)/shard_map/ppermute | solution.py:27
  77.1 45.0 %collective-permute-start.4 = (bf16[128,6656]{1,0:T(8,128)(2,1)S(1)}, bf16[128,6656]{1,0:T(8,128)(2,1)}, u32[]{:S(2)}, u32[]{:S(2)}) collective-permute-start(bf16[128,6656]{1,0:T(8,128)(2,1)S(1)} %copy-done.3), channel_id=1, source_target_pairs={{0,1},{1,0},{2,3},{3,2},{4,5},{5,4},{6,7},{7,6},{8,9},{9,8},{10,11... | collective-permute-start | bytes 5111816 | tf_op jit(solution)/shard_map/ppermute | solution.py:27
  82.8 39.3 %collective-permute-start.6 = (bf16[128,6656]{1,0:T(8,128)(2,1)}, bf16[128,6656]{1,0:T(8,128)(2,1)}, u32[]{:S(2)}, u32[]{:S(2)}) collective-permute-start(bf16[128,6656]{1,0:T(8,128)(2,1)} %collective-permute-done.2.refs_3_), channel_id=1, source_target_pairs={{0,1},{1,0},{2,3},{3,2},{4,5},{5,4},{6,7},{7,6},{8,9},{9,8},{10,11... | collective-permute-start | bytes 5111816 | tf_op jit(solution)/shard_map/ppermute | solution.py:27
  85.9 45.9 %collective-permute-start.16 = (bf16[2,64,6656]{2,1,0:T(8,128)(2,1)}, bf16[2,64,6656]{2,1,0:T(8,128)(2,1)}, u32[]{:S(2)}, u32[]{:S(2)}) collective-permute-start(bf16[2,64,6656]{2,1,0:T(8,128)(2,1)} %sums.4.refs_4_.refs_0_), channel_id=1, source_target_pairs={{0,2},{1,5},{2,0},{3,7},{4,6},{5,1},{6,4},{7,3},{8,10},{9,13},{10,... | collective-permute-start | bytes 5111816 | tf_op jit(solution)/shard_map/ppermute | solution.py:27
  90.9 0.9 copy-start.9
  121.5 10.3 %collective-permute-start.15 = (bf16[4,64,3328]{2,1,0:T(8,128)(2,1)}, bf16[4,64,3328]{2,1,0:T(8,128)(2,1)}, u32[]{:S(2)}, u32[]{:S(2)}) collective-permute-start(bf16[4,64,3328]{2,1,0:T(8,128)(2,1)} %get-tuple-element.37.refs_10_), channel_id=1, source_target_pairs={{0,1},{1,0},{2,3},{3,2},{4,5},{5,4},{6,7},{7,6},{8,9},{9,8},{10,11... | collective-permute-start | bytes 5111816 | tf_op jit(solution)/shard_map/ppermute | solution.py:27
  121.5 10.3 %collective-permute-start.14 = (bf16[4,64,3328]{2,1,0:T(8,128)(2,1)}, bf16[4,64,3328]{2,1,0:T(8,128)(2,1)S(1)}, u32[]{:S(2)}, u32[]{:S(2)}) collective-permute-start(bf16[4,64,3328]{2,1,0:T(8,128)(2,1)} %get-tuple-element.35.refs_0_), channel_id=1, source_target_pairs={{0,1},{1,0},{2,3},{3,2},{4,5},{5,4},{6,7},{7,6},{8,9},{9,8},{10,11... | collective-permute-start | bytes 5111816 | tf_op jit(solution)/shard_map/ppermute | solution.py:27
  131.8 1.3 copy-start.4
  137.1 30.1 %collective-permute-start.18 = (bf16[1,64,6656]{2,1,0:T(8,128)(2,1)}, bf16[1,64,6656]{2,1,0:T(8,128)(2,1)S(1)}, u32[]{:S(2)}, u32[]{:S(2)}) collective-permute-start(bf16[1,64,6656]{2,1,0:T(8,128)(2,1)} %get-tuple-element.39.refs_10_), channel_id=1, source_target_pairs={{0,4},{1,3},{2,6},{3,1},{4,0},{5,7},{6,2},{7,5},{8,12},{9,11},{10,... | collective-permute-start | bytes 2555912 | tf_op jit(solution)/shard_map/ppermute | solution.py:27
  138.3 29.1 %collective-permute-start.17 = (bf16[2,64,6656]{2,1,0:T(8,128)(2,1)}, bf16[2,64,6656]{2,1,0:T(8,128)(2,1)S(1)}, u32[]{:S(2)}, u32[]{:S(2)}) collective-permute-start(bf16[2,64,6656]{2,1,0:T(8,128)(2,1)} %get-tuple-element.38), channel_id=1, source_target_pairs={{0,2},{1,5},{2,0},{3,7},{4,6},{5,1},{6,4},{7,3},{8,10},{9,13},{10,... | collective-permute-start | bytes 5111816 | tf_op jit(solution)/shard_map/ppermute | solution.py:27
  167.1 0.9 copy-start.8
  168.1 1.2 copy-start.5
  173.2 12.9 %collective-permute-start.19 = (bf16[1,64,6656]{2,1,0:T(8,128)(2,1)}, bf16[1,64,6656]{2,1,0:T(8,128)(2,1)S(1)}, u32[]{:S(2)}, u32[]{:S(2)}) collective-permute-start(bf16[1,64,6656]{2,1,0:T(8,128)(2,1)} %get-tuple-element.40.refs_10_), channel_id=1, source_target_pairs={{0,4},{1,3},{2,6},{3,1},{4,0},{5,7},{6,2},{7,5},{8,12},{9,11},{10,... | collective-permute-start | bytes 2555912 | tf_op jit(solution)/shard_map/ppermute | solution.py:27
  186.1 0.9 copy-start.7

commit v8 on v7

--- a/solution.py
+++ b/solution.py
@@ -51,7 +51,7 @@
 def assemble(where, blocks, orders, c, after):
     rows_of, arrays = list(blocks), list(blocks.values())
     depth, rows = arrays[0].shape[1], len(orders[0]) * c
-    steps = 4
+    steps = 2
     part = pl.BlockSpec((arrays[0].shape[0], depth // steps), lambda i, s: (0, i))
     return pl.pallas_call(
         functools.partial(assemble_kernel, rows_of, orders, c),

time: 190 us -> 188 us (0.989)
  Pallas kernels: 116 us -> 114 us
where the time goes in v8:
time: 188 us
  Pallas kernels  114 us (61%)
  waiting for transfers between devices  41.7 us (22%)
  starting transfers between devices  21 us (11%)
  local copies, waits for them, and re-layouts  8.06 us (4%)
  other arithmetic  2.13 us (1%)
    pallas_call x3, Pallas kernels, weight_rows(): pl.pallas_call(functools.partial(weight_kernel, places, chunks, n), out_s...  46.7 us
    pallas_call x3, Pallas kernels, partial_sums(): pl.pallas_call(partial_kernel, out_shape=(out, out), grid=(count,), in_sp...  44.7 us
    ppermute x2, waiting for transfers between devices, doubled(): held[j ^ bit] = lax.ppermute(held[j], 'row', pairs)  21.5 us
    ppermute x14, waiting for transfers between devices, flip(): return lax.ppermute(x, 'col', [(i, i ^ bits[i & 1]) for i in range(n)])  16.7 us
    pallas_call x4, Pallas kernels, sums(): pl.pallas_call(functools.partial(sums_kernel, layout, len(ended)), out_sh...  13.9 us
    ppermute x14, starting transfers between devices, flip(): return lax.ppermute(x, 'col', [(i, i ^ bits[i & 1]) for i in range(n)])  11.6 us
    pallas_call x2, Pallas kernels, assemble(): pl.pallas_call(functools.partial(assemble_kernel, rows_of, orders, c), ou...  8.47 us
    ppermute x2, starting transfers between devices, doubled(): held[j ^ bit] = lax.ppermute(held[j], 'row', pairs)  5.23 us
  transfers between devices with their start and end apart: 20, of which 7 were waited for; matrix products, arithmetic and copies ran while one was open for 3% of the time, Pallas kernels for 55%

profile of v8, /device:TPU:0, one launch (start us, length us, event | category | flops | bytes accessed | tf_op | source)
XLA Modules:
  0.0 188.1 jit_solution(13400015051436611342)
XLA Ops:
  0.6 3.0 %collective-permute-start.1 = (bf16[128,6656]{1,0:T(8,128)(2,1)}, bf16[128,6656]{1,0:T(8,128)(2,1)S(1)}, u32[]{:S(2)}, u32[]{:S(2)}) collective-permute-start(bf16[128,6656]{1,0:T(8,128)(2,1)} %refs_0_.5), channel_id=1, source_target_pairs={{0,4},{1,5},{2,6},{3,7},{4,0},{5,1},{6,2},{7,3},{8,12},{9,13},{10,... | collective-permute-start | bytes 5111816 | tf_op jit(solution)/shard_map/ppermute | solution.py:27
  3.7 1.5 collective-permute-start
  5.2 1.9 slice.8
  7.0 2.6 %collective-permute-start.7 = (bf16[128,2048]{1,0:T(8,128)(2,1)}, bf16[128,2048]{1,0:T(8,128)(2,1)}, u32[]{:S(2)}, u32[]{:S(2)}) collective-permute-start(bf16[128,2048]{1,0:T(8,128)(2,1)} %bitcast.3.refs_0_), channel_id=1, source_target_pairs={{0,16},{8,24},{16,0},{24,8},{1,17},{9,25},{17,1},{25,9},{2,18},{10... | collective-permute-start | bytes 1572872 | tf_op jit(solution)/shard_map/ppermute | solution.py:35
  9.6 1.6 collective-permute-start.8
  11.2 21.5 %collective-permute-done.7.refs_1_ = bf16[128,2048]{1,0:T(8,128)(2,1)} collective-permute-done((bf16[128,2048]{1,0:T(8,128)(2,1)}, bf16[128,2048]{1,0:T(8,128)(2,1)}, u32[]{:S(2)}, u32[]{:S(2)}) %collective-permute-start.7) | collective-permute-done | bytes 524320 | tf_op jit(solution)/shard_map/ppermute | solution.py:35
  32.7 0.6 collective-permute-start.9
  33.3 7.8 %collective-permute-done.1.refs_5_.refs_2_ = bf16[128,6656]{1,0:T(8,128)(2,1)S(1)} collective-permute-done((bf16[128,6656]{1,0:T(8,128)(2,1)}, bf16[128,6656]{1,0:T(8,128)(2,1)S(1)}, u32[]{:S(2)}, u32[]{:S(2)}) %collective-permute-start.1) | collective-permute-done | bytes 1703968 | tf_op jit(solution)/shard_map/ppermute | solution.py:27
  41.1 1.5 collective-permute-done.refs_4_.refs_1_
  42.5 1.5 broadcast_select_fusion
  44.0 0.3 copy-done.2
  44.3 0.8 collective-permute-start.2
  45.2 0.0 collective-permute-start.3
  45.2 0.6 pad_add_fusion.where_ref
  45.8 1.1 slice.7
  46.9 2.6 %collective-permute-start.11 = (bf16[128,2048]{1,0:T(8,128)(2,1)S(1)}, bf16[128,2048]{1,0:T(8,128)(2,1)}, u32[]{:S(2)}, u32[]{:S(2)}) collective-permute-start(bf16[128,2048]{1,0:T(8,128)(2,1)S(1)} %bitcast.5), channel_id=1, source_target_pairs={{0,16},{8,24},{16,0},{24,8},{1,17},{9,25},{17,1},{25,9},{2,18},{10... | collective-permute-start | bytes 1572872 | tf_op jit(solution)/shard_map/ppermute | solution.py:35
  49.6 1.6 collective-permute-start.10
  51.1 4.3 %assemble.2 = (bf16[512,2048]{1,0:T(8,128)(2,1)}, bf16[2048,512]{1,0:T(8,128)(2,1)}) custom-call(s32[2]{0:T(128)} %pad_add_fusion.where_ref, bf16[128,2048]{1,0:T(8,128)(2,1)} %bitcast.3.refs_0_, bf16[128,2048]{1,0:T(8,128)(2,1)} %collective-permute-done.7.refs_1_, bf16[128,2048]{1,0:T(8,128)(2,1)} %collective-permute-done.8.refs_2_, ...), custom_call_target="tpu_custom_call" | custom-call | bytes 6291456 | tf_op jit(solution)/shard_map/assemble/pallas_call | solution.py:56
  55.4 20.0 %partial_sums.3 = (bf16[4,64,6656]{2,1,0:T(8,128)(2,1)}, bf16[4,64,6656]{2,1,0:T(8,128)(2,1)}) custom-call(bf16[6656,2048]{1,0:T(8,128)(2,1)} %w_ref.5, bf16[2048,512]{1,0:T(8,128)(2,1)} %get-tuple-element.25.g_ref), custom_call_target="tpu_custom_call" | custom-call | flops 13958643712 | bytes 36175872 | tf_op jit(solution)/shard_map/partial_sums/pallas_call | solution.py:90
  75.5 0.5 collective-permute-start.12
  76.0 0.2 collective-permute-start.5
  76.2 0.3 collective-permute-start.4
  76.5 0.6 hold.1.refs_2_
  77.1 4.7 %collective-permute-done.13.refs_1_.refs_6_ = bf16[4,64,6656]{2,1,0:T(8,128)(2,1)} collective-permute-done((bf16[4,64,6656]{2,1,0:T(8,128)(2,1)}, bf16[4,64,6656]{2,1,0:T(8,128)(2,1)}, u32[]{:S(2)}, u32[]{:S(2)}) %collective-permute-start.13) | collective-permute-done | bytes 3407904 | tf_op jit(solution)/shard_map/ppermute | solution.py:27
  81.9 0.1 collective-permute-start.6
  82.0 3.0 %sums.4.refs_4_.refs_0_ = bf16[2,64,6656]{2,1,0:T(8,128)(2,1)} custom-call(bf16[4,64,6656]{2,1,0:T(8,128)(2,1)} %get-tuple-element.30.refs_0_.refs_5_, bf16[4,64,6656]{2,1,0:T(8,128)(2,1)} %collective-permute-done.13.refs_1_.refs_6_, f32[8,128]{1,0:T(8,128)} %hold.1.refs_2_), custom_call_target="tpu_custom_call" | custom-call | flops 2555904 | bytes 5111808 | tf_op jit(solution)/shard_map/sums/pallas_call | solution.py:214
  85.0 1.5 collective-permute-start.16
  86.5 3.5 %collective-permute-done.12.refs_3_ = bf16[128,2048]{1,0:T(8,128)(2,1)S(1)} collective-permute-done((bf16[128,2048]{1,0:T(8,128)(2,1)}, bf16[128,2048]{1,0:T(8,128)(2,1)S(1)}, u32[]{:S(2)}, u32[]{:S(2)}) %collective-permute-start.12) | collective-permute-done | bytes 524320 | tf_op jit(solution)/shard_map/ppermute | solution.py:305
  90.1 0.9 copy-done.9
  90.9 4.2 %assemble.3 = (bf16[512,2048]{1,0:T(8,128)(2,1)}, bf16[2048,512]{1,0:T(8,128)(2,1)}) custom-call(s32[2]{0:T(128)} %pad_add_fusion.where_ref, bf16[128,2048]{1,0:T(8,128)(2,1)} %bitcast.7, bf16[128,2048]{1,0:T(8,128)(2,1)} %collective-permute-done.10.refs_1_, bf16[128,2048]{1,0:T(8,128)(2,1)} %collective-permute-done.11.refs_2_, bf16[128,2048]{1,0:T(8,128)(2,1)} %copy-done.9, ...), custom_call_target="tpu_custom_call" | custom-call | bytes 6291456 | tf_op jit(solution)/shard_map/assemble/pallas_call | solution.py:56
  95.1 12.3 %partial_sums.4 = (bf16[4,64,3328]{2,1,0:T(8,128)(2,1)}, bf16[4,64,3328]{2,1,0:T(8,128)(2,1)}) custom-call(bf16[6656,2048]{1,0:T(8,128)(2,1)} %w_ref.5, bf16[2048,512]{1,0:T(8,128)(2,1)} %get-tuple-element.33.g_ref, bf16[2,64,6656]{2,1,0:T(8,128)(2,1)} %sums.4.refs_4_.refs_0_), custom_call_target="tpu_custom_call" | custom-call | flops 6979321856 | bytes 19136512 | tf_op jit(solution)/shard_map/partial_sums/pallas_call | solution.py:90
  107.4 12.4 %partial_sums.5 = (bf16[4,64,3328]{2,1,0:T(8,128)(2,1)}, bf16[4,64,3328]{2,1,0:T(8,128)(2,1)}) custom-call(bf16[6656,2048]{1,0:T(8,128)(2,1)} %w_ref.5, bf16[2048,512]{1,0:T(8,128)(2,1)} %get-tuple-element.33.g_ref, bf16[4,64,3328]{2,1,0:T(8,128)(2,1)} %get-tuple-element.35.refs_0_), custom_call_target="tpu_custom_call" | custom-call | flops 6979321856 | bytes 19136512 | tf_op jit(solution)/shard_map/partial_sums/pallas_call | solution.py:90
  119.8 0.5 collective-permute-start.14
  120.3 9.7 %weight_rows.3.refs_7_.refs_11_ = bf16[6656,2048]{1,0:T(8,128)(2,1)} custom-call(s32[2]{0:T(128)} %pad_add_fusion.where_ref, bf16[128,6656]{1,0:T(8,128)(2,1)} %refs_0_.5, bf16[128,6656]{1,0:T(8,128)(2,1)} %copy-done.2, bf16[128,6656]{1,0:T(8,128)(2,1)} %copy-done, bf16[128,6656]{1,0:T(8,128)(2,1)} %collective-permute-done.2.refs_3_, ...), custom_call_target="tpu_custom_call" | custom-call | flops 4294967296 | bytes 10485760 | tf_op jit(solution)/shard_map/weight_rows/pallas_call | solution.py:142
  130.1 1.3 copy-done.4
  131.4 3.9 %sums.5 = (bf16[1,64,6656]{2,1,0:T(8,128)(2,1)}, bf16[2,64,6656]{2,1,0:T(8,128)(2,1)}) custom-call(bf16[4,64,6656]{2,1,0:T(8,128)(2,1)} %get-tuple-element.30.refs_0_.refs_5_, bf16[4,64,6656]{2,1,0:T(8,128)(2,1)} %collective-permute-done.13.refs_1_.refs_6_, bf16[2,64,6656]{2,1,0:T(8,128)(2,1)} %collective-permute-done.16.refs_2_.refs_7_, ...), custom_call_target="tpu_custom_call" | custom-call | flops 5963776 | bytes 11927552 | tf_op jit(solution)/shard_map/sums/pallas_call | solution.py:214
  135.3 1.2 collective-permute-start.18
  136.5 1.5 collective-permute-start.17
  138.0 27.2 %weight_rows.4.refs_9_.refs_11_ = bf16[6656,2048]{1,0:T(8,128)(2,1)} custom-call(s32[2]{0:T(128)} %pad_add_fusion.where_ref, bf16[128,6656]{1,0:T(8,128)(2,1)} %refs_0_.5, bf16[128,6656]{1,0:T(8,128)(2,1)} %copy-done.2, bf16[128,6656]{1,0:T(8,128)(2,1)} %copy-done, ...), custom_call_target="tpu_custom_call", output_to_operand_aliasing={{}: (12, {})} | custom-call | flops 19327352832 | bytes 32505856 | tf_op jit(solution)/shard_map/weight_rows/pallas_call | solution.py:142
  165.3 0.3 collective-permute-done.17.refs_4_
  165.6 0.6 copy-done.8
  166.2 1.2 copy-done.5
  167.3 4.0 %sums.6 = (bf16[1,64,6656]{2,1,0:T(8,128)(2,1)}, bf16[128,6656]{1,0:T(8,128)(2,1)}) custom-call(bf16[4,64,3328]{2,1,0:T(8,128)(2,1)} %get-tuple-element.34.refs_3_.refs_0_, bf16[4,64,3328]{2,1,0:T(8,128)(2,1)} %get-tuple-element.36.refs_4_.refs_1_, bf16[4,64,3328]{2,1,0:T(8,128)(2,1)} %copy-done.4, ...), custom_call_target="tpu_custom_call" | custom-call | flops 4685824 | bytes 9371648 | tf_op jit(solution)/shard_map/sums/pallas_call | solution.py:214
  171.3 0.8 collective-permute-start.19
  172.1 9.7 %weight_rows.5.refs_6_ = bf16[6656,2048]{1,0:T(8,128)(2,1)} custom-call(s32[2]{0:T(128)} %pad_add_fusion.where_ref, bf16[128,6656]{1,0:T(8,128)(2,1)} %refs_0_.5, bf16[128,6656]{1,0:T(8,128)(2,1)} %copy-done.2, bf16[128,6656]{1,0:T(8,128)(2,1)} %copy-done, bf16[128,6656]{1,0:T(8,128)(2,1)} %collective-permute-done.2.refs_3_, ...), custom_call_target="tpu_custom_call", output_to_operand_aliasing={{}: (12, {})} | custom-call | flops 4294967296 | bytes 10485760 | tf_op jit(solution)/shard_map/weight_rows/pallas_call | solution.py:142
  181.9 2.3 %collective-permute-done.19.refs_5_ = bf16[1,64,6656]{2,1,0:T(8,128)(2,1)S(1)} collective-permute-done((bf16[1,64,6656]{2,1,0:T(8,128)(2,1)}, bf16[1,64,6656]{2,1,0:T(8,128)(2,1)S(1)}, u32[]{:S(2)}, u32[]{:S(2)}) %collective-permute-start.19) | collective-permute-done | bytes 852000 | tf_op jit(solution)/shard_map/ppermute | solution.py:27
  184.2 0.9 copy-done.7
  185.1 3.0 %sums.7 = bf16[128,6656]{1,0:T(8,128)(2,1)} custom-call(bf16[4,64,3328]{2,1,0:T(8,128)(2,1)} %get-tuple-element.34.refs_3_.refs_0_, bf16[4,64,3328]{2,1,0:T(8,128)(2,1)} %get-tuple-element.36.refs_4_.refs_1_, bf16[4,64,3328]{2,1,0:T(8,128)(2,1)} %copy-done.4, ...), custom_call_target="tpu_custom_call", output_to_operand_aliasing={{}: (7, {})} | custom-call | flops 2981888 | bytes 5963776 | tf_op jit(solution)/shard_map/sums/pallas_call | solution.py:214
  (29 shorter events, 0.1 us)
Async XLA Ops:
  0.6 40.4 %collective-permute-start.1 = (bf16[128,6656]{1,0:T(8,128)(2,1)}, bf16[128,6656]{1,0:T(8,128)(2,1)S(1)}, u32[]{:S(2)}, u32[]{:S(2)}) collective-permute-start(bf16[128,6656]{1,0:T(8,128)(2,1)} %refs_0_.5), channel_id=1, source_target_pairs={{0,4},{1,5},{2,6},{3,7},{4,0},{5,1},{6,2},{7,3},{8,12},{9,13},{10,... | collective-permute-start | bytes 5111816 | tf_op jit(solution)/shard_map/ppermute | solution.py:27
  3.7 38.9 %collective-permute-start = (bf16[128,6656]{1,0:T(8,128)(2,1)}, bf16[128,6656]{1,0:T(8,128)(2,1)S(1)}, u32[]{:S(2)}, u32[]{:S(2)}) collective-permute-start(bf16[128,6656]{1,0:T(8,128)(2,1)} %refs_0_.5), channel_id=1, source_target_pairs={{0,2},{1,3},{2,0},{3,1},{4,6},{5,7},{6,4},{7,5},{8,10},{9,11},{10,... | collective-permute-start | bytes 5111816 | tf_op jit(solution)/shard_map/ppermute | solution.py:27
  7.0 25.7 %collective-permute-start.7 = (bf16[128,2048]{1,0:T(8,128)(2,1)}, bf16[128,2048]{1,0:T(8,128)(2,1)}, u32[]{:S(2)}, u32[]{:S(2)}) collective-permute-start(bf16[128,2048]{1,0:T(8,128)(2,1)} %bitcast.3.refs_0_), channel_id=1, source_target_pairs={{0,16},{8,24},{16,0},{24,8},{1,17},{9,25},{17,1},{25,9},{2,18},{10... | collective-permute-start | bytes 1572872 | tf_op jit(solution)/shard_map/ppermute | solution.py:35
  9.6 39.9 %collective-permute-start.8 = (bf16[128,2048]{1,0:T(8,128)(2,1)}, bf16[128,2048]{1,0:T(8,128)(2,1)}, u32[]{:S(2)}, u32[]{:S(2)}) collective-permute-start(bf16[128,2048]{1,0:T(8,128)(2,1)} %bitcast.3.refs_0_), channel_id=1, source_target_pairs={{0,8},{8,0},{16,24},{24,16},{1,9},{9,1},{17,25},{25,17},{2,10},{10... | collective-permute-start | bytes 1572872 | tf_op jit(solution)/shard_map/ppermute | solution.py:301
  32.7 18.5 %collective-permute-start.9 = (bf16[128,2048]{1,0:T(8,128)(2,1)}, bf16[128,2048]{1,0:T(8,128)(2,1)}, u32[]{:S(2)}, u32[]{:S(2)}) collective-permute-start(bf16[128,2048]{1,0:T(8,128)(2,1)} %collective-permute-done.7.refs_1_), channel_id=1, source_target_pairs={{0,8},{8,0},{16,24},{24,16},{1,9},{9,1},{17,25},{25,17},{2,10},{10... | collective-permute-start | bytes 1572872 | tf_op jit(solution)/shard_map/ppermute | solution.py:305
  41.1 2.9 %copy-start = (bf16[128,6656]{1,0:T(8,128)(2,1)}, bf16[128,6656]{1,0:T(8,128)(2,1)S(1)}, u32[]{:S(2)}) copy-start(bf16[128,6656]{1,0:T(8,128)(2,1)S(1)} %collective-permute-done.1.refs_5_.refs_2_) | copy-start | bytes 5111812
  42.5 1.8 copy-start.2
  44.3 31.9 %collective-permute-start.2 = (bf16[128,6656]{1,0:T(8,128)(2,1)}, bf16[128,6656]{1,0:T(8,128)(2,1)}, u32[]{:S(2)}, u32[]{:S(2)}) collective-permute-start(bf16[128,6656]{1,0:T(8,128)(2,1)} %broadcast_select_fusion), channel_id=1, source_target_pairs={{0,4},{1,3},{2,6},{3,1},{4,0},{5,7},{6,2},{7,5},{8,12},{9,11},{10,... | collective-permute-start | bytes 5111816 | tf_op jit(solution)/shard_map/ppermute | solution.py:27
  45.2 39.9 %collective-permute-start.3 = (bf16[128,6656]{1,0:T(8,128)(2,1)}, bf16[128,6656]{1,0:T(8,128)(2,1)}, u32[]{:S(2)}, u32[]{:S(2)}) collective-permute-start(bf16[128,6656]{1,0:T(8,128)(2,1)} %refs_0_.5), channel_id=1, source_target_pairs={{0,1},{1,0},{2,3},{3,2},{4,5},{5,4},{6,7},{7,6},{8,9},{9,8},{10,11... | collective-permute-start | bytes 5111816 | tf_op jit(solution)/shard_map/ppermute | solution.py:27
  46.9 8.5 %copy-start.6 = (bf16[2,64,2048]{2,1,0:T(8,128)(2,1)}, bf16[2,64,2048]{2,1,0:T(8,128)(2,1)S(1)}, u32[]{:S(2)}) copy-start(bf16[2,64,2048]{2,1,0:T(8,128)(2,1)S(1)} %slice.7) | copy-start | bytes 1572868
  46.9 28.6 %collective-permute-start.11 = (bf16[128,2048]{1,0:T(8,128)(2,1)S(1)}, bf16[128,2048]{1,0:T(8,128)(2,1)}, u32[]{:S(2)}, u32[]{:S(2)}) collective-permute-start(bf16[128,2048]{1,0:T(8,128)(2,1)S(1)} %bitcast.5), channel_id=1, source_target_pairs={{0,16},{8,24},{16,0},{24,8},{1,17},{9,25},{17,1},{25,9},{2,18},{10... | collective-permute-start | bytes 1572872 | tf_op jit(solution)/shard_map/ppermute | solution.py:35
  49.6 25.9 %collective-permute-start.10 = (bf16[128,2048]{1,0:T(8,128)(2,1)S(1)}, bf16[128,2048]{1,0:T(8,128)(2,1)}, u32[]{:S(2)}, u32[]{:S(2)}) collective-permute-start(bf16[128,2048]{1,0:T(8,128)(2,1)S(1)} %bitcast.6), channel_id=1, source_target_pairs={{0,8},{8,0},{16,24},{24,16},{1,9},{9,1},{17,25},{25,17},{2,10},{10... | collective-permute-start | bytes 1572872 | tf_op jit(solution)/shard_map/ppermute | solution.py:301
  55.4 20.6 %copy-start.1 = (bf16[128,6656]{1,0:T(8,128)(2,1)S(1)}, bf16[128,6656]{1,0:T(8,128)(2,1)}, u32[]{:S(2)}) copy-start(bf16[128,6656]{1,0:T(8,128)(2,1)} %copy-done) | copy-start | bytes 5111812
  55.4 20.8 %copy-start.3 = (bf16[128,6656]{1,0:T(8,128)(2,1)S(1)}, bf16[128,6656]{1,0:T(8,128)(2,1)}, u32[]{:S(2)}) copy-start(bf16[128,6656]{1,0:T(8,128)(2,1)} %copy-done.2) | copy-start | bytes 5111812
  75.5 6.4 %collective-permute-start.13 = (bf16[4,64,6656]{2,1,0:T(8,128)(2,1)}, bf16[4,64,6656]{2,1,0:T(8,128)(2,1)}, u32[]{:S(2)}, u32[]{:S(2)}) collective-permute-start(bf16[4,64,6656]{2,1,0:T(8,128)(2,1)} %get-tuple-element.31.refs_0_), channel_id=1, source_target_pairs={{0,1},{1,0},{2,3},{3,2},{4,5},{5,4},{6,7},{7,6},{8,9},{9,8},{10,11... | collective-permute-start | bytes 10223624 | tf_op jit(solution)/shard_map/ppermute | solution.py:27
  75.5 14.6 %collective-permute-start.12 = (bf16[128,2048]{1,0:T(8,128)(2,1)}, bf16[128,2048]{1,0:T(8,128)(2,1)S(1)}, u32[]{:S(2)}, u32[]{:S(2)}) collective-permute-start(bf16[128,2048]{1,0:T(8,128)(2,1)} %collective-permute-done.11.refs_2_), channel_id=1, source_target_pairs={{0,8},{8,0},{16,24},{24,16},{1,9},{9,1},{17,25},{25,17},{2,10},{10... | collective-permute-start | bytes 1572872 | tf_op jit(solution)/shard_map/ppermute | solution.py:305
  76.0 43.8 %collective-permute-start.5 = (bf16[128,6656]{1,0:T(8,128)(2,1)S(1)}, bf16[128,6656]{1,0:T(8,128)(2,1)}, u32[]{:S(2)}, u32[]{:S(2)}) collective-permute-start(bf16[128,6656]{1,0:T(8,128)(2,1)S(1)} %copy-done.1), channel_id=1, source_target_pairs={{0,1},{1,0},{2,3},{3,2},{4,5},{5,4},{6,7},{7,6},{8,9},{9,8},{10,11... | collective-permute-start | bytes 5111816 | tf_op jit(solution)/shard_map/ppermute | solution.py:27
  76.2 44.1 %collective-permute-start.4 = (bf16[128,6656]{1,0:T(8,128)(2,1)S(1)}, bf16[128,6656]{1,0:T(8,128)(2,1)}, u32[]{:S(2)}, u32[]{:S(2)}) collective-permute-start(bf16[128,6656]{1,0:T(8,128)(2,1)S(1)} %copy-done.3), channel_id=1, source_target_pairs={{0,1},{1,0},{2,3},{3,2},{4,5},{5,4},{6,7},{7,6},{8,9},{9,8},{10,11... | collective-permute-start | bytes 5111816 | tf_op jit(solution)/shard_map/ppermute | solution.py:27
  81.9 38.5 %collective-permute-start.6 = (bf16[128,6656]{1,0:T(8,128)(2,1)}, bf16[128,6656]{1,0:T(8,128)(2,1)}, u32[]{:S(2)}, u32[]{:S(2)}) collective-permute-start(bf16[128,6656]{1,0:T(8,128)(2,1)} %collective-permute-done.2.refs_3_), channel_id=1, source_target_pairs={{0,1},{1,0},{2,3},{3,2},{4,5},{5,4},{6,7},{7,6},{8,9},{9,8},{10,11... | collective-permute-start | bytes 5111816 | tf_op jit(solution)/shard_map/ppermute | solution.py:27
  85.0 45.0 %collective-permute-start.16 = (bf16[2,64,6656]{2,1,0:T(8,128)(2,1)}, bf16[2,64,6656]{2,1,0:T(8,128)(2,1)}, u32[]{:S(2)}, u32[]{:S(2)}) collective-permute-start(bf16[2,64,6656]{2,1,0:T(8,128)(2,1)} %sums.4.refs_4_.refs_0_), channel_id=1, source_target_pairs={{0,2},{1,5},{2,0},{3,7},{4,6},{5,1},{6,4},{7,3},{8,10},{9,13},{10,... | collective-permute-start | bytes 5111816 | tf_op jit(solution)/shard_map/ppermute | solution.py:27
  90.1 0.9 copy-start.9
  119.8 10.3 %collective-permute-start.15 = (bf16[4,64,3328]{2,1,0:T(8,128)(2,1)}, bf16[4,64,3328]{2,1,0:T(8,128)(2,1)}, u32[]{:S(2)}, u32[]{:S(2)}) collective-permute-start(bf16[4,64,3328]{2,1,0:T(8,128)(2,1)} %get-tuple-element.37.refs_10_), channel_id=1, source_target_pairs={{0,1},{1,0},{2,3},{3,2},{4,5},{5,4},{6,7},{7,6},{8,9},{9,8},{10,11... | collective-permute-start | bytes 5111816 | tf_op jit(solution)/shard_map/ppermute | solution.py:27
  119.8 10.3 %collective-permute-start.14 = (bf16[4,64,3328]{2,1,0:T(8,128)(2,1)}, bf16[4,64,3328]{2,1,0:T(8,128)(2,1)S(1)}, u32[]{:S(2)}, u32[]{:S(2)}) collective-permute-start(bf16[4,64,3328]{2,1,0:T(8,128)(2,1)} %get-tuple-element.35.refs_0_), channel_id=1, source_target_pairs={{0,1},{1,0},{2,3},{3,2},{4,5},{5,4},{6,7},{7,6},{8,9},{9,8},{10,11... | collective-permute-start | bytes 5111816 | tf_op jit(solution)/shard_map/ppermute | solution.py:27
  130.1 1.3 copy-start.4
  135.3 29.9 %collective-permute-start.18 = (bf16[1,64,6656]{2,1,0:T(8,128)(2,1)}, bf16[1,64,6656]{2,1,0:T(8,128)(2,1)S(1)}, u32[]{:S(2)}, u32[]{:S(2)}) collective-permute-start(bf16[1,64,6656]{2,1,0:T(8,128)(2,1)} %get-tuple-element.39.refs_10_), channel_id=1, source_target_pairs={{0,4},{1,3},{2,6},{3,1},{4,0},{5,7},{6,2},{7,5},{8,12},{9,11},{10,... | collective-permute-start | bytes 2555912 | tf_op jit(solution)/shard_map/ppermute | solution.py:27
  136.5 29.1 %collective-permute-start.17 = (bf16[2,64,6656]{2,1,0:T(8,128)(2,1)}, bf16[2,64,6656]{2,1,0:T(8,128)(2,1)S(1)}, u32[]{:S(2)}, u32[]{:S(2)}) collective-permute-start(bf16[2,64,6656]{2,1,0:T(8,128)(2,1)} %get-tuple-element.38), channel_id=1, source_target_pairs={{0,2},{1,5},{2,0},{3,7},{4,6},{5,1},{6,4},{7,3},{8,10},{9,13},{10,... | collective-permute-start | bytes 5111816 | tf_op jit(solution)/shard_map/ppermute | solution.py:27
  165.2 0.9 copy-start.8
  166.2 1.2 copy-start.5
  171.3 12.9 %collective-permute-start.19 = (bf16[1,64,6656]{2,1,0:T(8,128)(2,1)}, bf16[1,64,6656]{2,1,0:T(8,128)(2,1)S(1)}, u32[]{:S(2)}, u32[]{:S(2)}) collective-permute-start(bf16[1,64,6656]{2,1,0:T(8,128)(2,1)} %get-tuple-element.40.refs_10_), channel_id=1, source_target_pairs={{0,4},{1,3},{2,6},{3,1},{4,0},{5,7},{6,2},{7,5},{8,12},{9,11},{10,... | collective-permute-start | bytes 2555912 | tf_op jit(solution)/shard_map/ppermute | solution.py:27
  184.2 0.9 copy-start.7
